TPU v7x, 32 devices: a whole 2x2x4 slice. The times are simulated.
32 devices in a mesh: groups: 2 (over y), head: 4 (over z), req: 2 (over x), seq: 2 (over core).
Axes of the slice: x: 2, y: 2, z: 4, core: 2. Of those that a mesh axis runs over, the one named last changes fastest.
Arguments:
- queries: bfloat16 [4, 256, 6144], P(('groups', 'req'), 'seq', 'head'), parts along dimension 0, may hold values from -400 to 400
- hidden: bfloat16 [4, 256, 7168], P(('groups', 'req'), 'seq', 'head'), parts along dimension 0, may hold values from -6 to 6
- w_dkv: bfloat16 [7168, 576], P('head'), may hold values from -0.0625 to 0.0625
- kv_gain: float32 [512], replicated, may hold values from 0.1 to 1.9
- w_uk: bfloat16 [32, 128, 512], P('head'), may hold values from -0.5 to 0.5
- value_up_weight: bfloat16 [32, 512, 128], P('head'), may hold values from -0.25 to 0.25
- page_pool: bfloat16 [512, 36864], P(('groups', 'head', 'req')), parts along dimension 0, may hold values from -6 to 6
- page_owner: int32 [4, 64, 1], P('groups'), parts along dimension 0, may hold values from 0 to 7; in each aligned block of 64 rows (0 to 63, 64 to 127, ..., all dimensions but the last counted through in order) at most 16 rows name the same one
- page_slot: int32 [4, 64], P('groups'), parts along dimension 0, may hold values from 0 to 31
- prefix_len: int32 [4], P('groups'), parts along dimension 0, may hold values from 64 to 4096, as said below
- suffix_len: int32 [4], P('groups'), parts along dimension 0, may hold values from 128 to 256, as said below
Outputs:
- attn_out: bfloat16 [4, 256, 4096], P(('groups', 'req'), 'seq', 'head'), parts along dimension 0
- new_pages: bfloat16 [4, 4, 36864], P(('groups', 'req'), 'seq'), parts along dimension 0
There are 2 independent parts, one for each index of `groups`. A program takes and returns all parts, laid end to end along the dimension named above; an argument that names none is the same for every part. Nothing has to cross between parts.
Inputs may be any that keep to these rules, and one draw needn't show every extreme that they name: `page_owner`: in the rows of one request batch (1 request) no owner holds more than 16 pages, and some owner holds exactly 16. `prefix_len`: some request has the longest prefix. `suffix_len`: some request fills all suffix slots.
All inputs are finite; a program needn't handle non-finite values.
Results may differ from a plain program's by a relative error of at most 0.0055.
The roundings to bfloat16 on the way count: a program that leaves them out, or rounds other values in their place, can miss the bound.
Values may be sent and summed in bfloat16 or wider, within the bound.
No kernel may reach another device: no remote copies, remote signals or barrier semaphores. Data moves between devices by JAX's collectives and lax.ppermute only.
A program may use at most 128 MiB of HBM per device.

v0:
```python
import functools
import math

import jax
import jax.numpy as jnp
from jax import lax
from jax.experimental import pallas as pl
from jax.experimental.pallas import tpu as pltpu
from jax.sharding import PartitionSpec as P

LOWEST = -1e30
MASKED = -1e38
MIB = 1024 * 1024


def rotate(vector, cosine_table, sine_table):
    half_width = vector.shape[-1] // 2
    first_half = vector[..., :half_width]
    second_half = vector[..., half_width:]
    return jnp.concatenate(
        [
            first_half * cosine_table - second_half * sine_table,
            first_half * sine_table + second_half * cosine_table,
        ],
        axis=-1,
    )


def angles(positions, rope_width):
    half_width = rope_width // 2
    frequency = 10000.0 ** (-2.0 * jnp.arange(half_width, dtype=jnp.float32) / rope_width)
    phases = positions.astype(jnp.float32)[:, None] * frequency[None, :]
    return (jnp.cos(phases), jnp.sin(phases))


def finish_latent(summed, positions, live_rows, kv_gain, latent_width):
    latent_part = summed[:, :latent_width]
    mean_square = jnp.mean(latent_part * latent_part, axis=-1, keepdims=True)
    normed = latent_part * lax.rsqrt(mean_square + 1e-06) * kv_gain
    cosine_table, sine_table = angles(positions, summed.shape[1] - latent_width)
    rotated = rotate(summed[:, latent_width:], cosine_table, sine_table)
    joined = jnp.concatenate([normed, rotated], axis=-1).astype(jnp.bfloat16)
    return jnp.where(live_rows[:, None], joined, jnp.zeros_like(joined))


def any_spec():
    return pl.BlockSpec(memory_space=pl.ANY)


def smem_spec():
    return pl.BlockSpec(memory_space=pltpu.SMEM)


def vmem_spec():
    return pl.BlockSpec(memory_space=pltpu.VMEM)


def hbm_spec():
    return pl.BlockSpec(memory_space=pltpu.HBM)


def pick_kernel(
    cap, page_len, owner_hbm, slot_hbm, prefix_hbm, suffix_hbm, pool_hbm, hidden_hbm, down_hbm, count_ref,
    most_ref, length_ref, live_ref, first_ref, rest_ref, foreign_ref, partial_ref, owner_ref, slot_ref,
    prefix_ref, suffix_ref, pool_ref, hidden_ref, down_ref, pages, lists, table, sems,
):
    n_req = lax.axis_size("req")
    head_idx = lax.axis_index("head")
    req_idx = lax.axis_index("req")
    seq_idx = lax.axis_index("seq")
    n_pages = owner_ref.shape[1]
    pool_pages, pairs, pair_width = pages.shape
    chunk = first_ref.shape[0]
    loads = [
        pltpu.make_async_copy(owner_hbm, owner_ref, sems.at[0]),
        pltpu.make_async_copy(slot_hbm, slot_ref, sems.at[1]),
        pltpu.make_async_copy(pool_hbm, pool_ref, sems.at[2]),
        pltpu.make_async_copy(hidden_hbm, hidden_ref, sems.at[6]),
        pltpu.make_async_copy(down_hbm, down_ref, sems.at[7]),
        pltpu.make_async_copy(prefix_hbm, prefix_ref, sems.at[8]),
        pltpu.make_async_copy(suffix_hbm, suffix_ref, sems.at[9]),
    ]
    for load in loads:
        load.start()
    loads[0].wait()
    loads[1].wait()
    loads[5].wait()
    loads[6].wait()
    length_ref[0] = prefix_ref[req_idx]
    live_ref[0] = suffix_ref[req_idx]
    self_owner = head_idx * n_req + req_idx
    n_owners = table.shape[1]
    for shift in range(n_req):
        for owner in range(n_owners):
            table[shift, owner] = 0
    founds = []
    most = jnp.int32(0)
    for shift in range(n_req):
        request = lax.rem(req_idx + shift, n_req)

        def note(page, found, shift=shift, request=request):
            owner = owner_ref[request, page]
            needed = page * page_len < prefix_ref[request]
            table[shift, owner] += needed.astype(jnp.int32)
            lists[shift, found] = slot_ref[request, page]
            return found + (needed & (owner == self_owner)).astype(jnp.int32)

        founds.append(lax.fori_loop(0, n_pages, note, jnp.int32(0), unroll=8))
        for place in range(n_owners // n_req):
            held = functools.reduce(jnp.add, [table[shift, place * n_req + i] for i in range(n_req)])
            early = jnp.minimum(table[shift, place * n_req + request], chunk)
            most = jnp.maximum(most, held - early)
    for shift in range(n_req):
        count_ref[shift] = table[0, head_idx * n_req + lax.rem(req_idx + n_req - shift, n_req)]
    most_ref[0] = most
    loads[2].wait()
    step = 16
    row = lax.broadcasted_iota(jnp.int32, (step * step, step * step), 0)
    column = lax.broadcasted_iota(jnp.int32, (step * step, step * step), 1)
    swap = ((row // step == column % step) & (row % step == column // step)).astype(jnp.bfloat16)
    for page in range(0, pool_pages, step):
        for pair in range(0, pairs, step):
            rows = jnp.concatenate(
                [
                    pool_ref[page : page + step, (pair + i) * pair_width : (pair + i + 1) * pair_width]
                    for i in range(step)
                ],
                axis=0,
            )
            turned = jnp.dot(swap, rows, preferred_element_type=jnp.float32).astype(jnp.bfloat16)
            pages[page : page + step, pair : pair + step, :] = turned.reshape(step, step, pair_width)

    def send(shift, rank, target, sem):
        slot = jnp.where(rank < founds[shift], lists[shift, rank], 0)
        pltpu.make_async_copy(pages.at[slot], target, sem).start()

    for rank in range(cap):
        if rank < chunk:
            send(0, rank, first_ref.at[rank], sems.at[3])
        else:
            send(0, rank, rest_ref.at[rank - chunk], sems.at[4])
    half_cap = foreign_ref.shape[1]
    for shift in range(1, n_req):
        for j in range(half_cap):
            send(shift, seq_idx * half_cap + j, foreign_ref.at[shift - 1, j], sems.at[5])
    loads[3].wait()
    loads[4].wait()
    partial_ref[...] = lax.dot_general(
        hidden_ref[...], down_ref[...], (((1,), (1,)), ((), ())), preferred_element_type=jnp.float32
    )
    pltpu.make_async_copy(first_ref, first_ref, sems.at[3]).wait()
    if cap > chunk:
        pltpu.make_async_copy(rest_ref, rest_ref, sems.at[4]).wait()
    pltpu.make_async_copy(foreign_ref, foreign_ref, sems.at[5]).wait()


def pick_pages(
    page_owner, page_slot, prefix_len, suffix_len, page_pool, hidden, down,
    cap, chunk, n_head, n_req, n_seq, pairs,
):
    pool_pages, page_width = page_pool.shape
    page = (pairs, page_width // pairs)
    return pl.pallas_call(
        functools.partial(pick_kernel, cap, 2 * pairs),
        out_shape=(
            jax.ShapeDtypeStruct((n_req,), jnp.int32),
            jax.ShapeDtypeStruct((1,), jnp.int32),
            jax.ShapeDtypeStruct((1,), jnp.int32),
            jax.ShapeDtypeStruct((1,), jnp.int32),
            jax.ShapeDtypeStruct((chunk, *page), jnp.bfloat16),
            jax.ShapeDtypeStruct((max(1, cap - chunk), *page), jnp.bfloat16),
            jax.ShapeDtypeStruct((n_req - 1, cap // n_seq, *page), jnp.bfloat16),
            jax.ShapeDtypeStruct((hidden.shape[0], down.shape[0]), jnp.float32),
        ),
        in_specs=[any_spec()] * 4 + [hbm_spec()] * 3,
        out_specs=(smem_spec(), smem_spec(), smem_spec(), smem_spec(), hbm_spec(), hbm_spec(), hbm_spec(), vmem_spec()),
        scratch_shapes=[
            pltpu.SMEM(page_owner.shape, jnp.int32),
            pltpu.SMEM(page_slot.shape, jnp.int32),
            pltpu.SMEM(prefix_len.shape, jnp.int32),
            pltpu.SMEM(suffix_len.shape, jnp.int32),
            pltpu.VMEM((pool_pages, page_width), jnp.bfloat16),
            pltpu.VMEM(hidden.shape, jnp.bfloat16),
            pltpu.VMEM(down.shape, jnp.bfloat16),
            pltpu.VMEM((pool_pages, *page), jnp.bfloat16),
            pltpu.SMEM((n_req, cap + 1), jnp.int32),
            pltpu.SMEM((n_req, n_head * n_req), jnp.int32),
            pltpu.SemaphoreType.DMA((10,)),
        ],
        compiler_params=pltpu.CompilerParams(vmem_limit_bytes=60 * MIB),
        cost_estimate=pl.CostEstimate(flops=10**9, bytes_accessed=6 * 10**6, transcendentals=0),
        name="pick_pages",
    )(page_owner, page_slot, prefix_len, suffix_len, page_pool, hidden, down)


def join_kernel(chunk, cap, count_ref, rest_ref, mine_ref, other_ref, *refs):
    n_req = count_ref.shape[0]
    targets, sems = refs[:-1], refs[-1]
    seq_idx = lax.axis_index("seq")
    half_cap = mine_ref.shape[1]
    excess = jnp.maximum(count_ref[0] - chunk, 0)
    j = 0
    for part, target in enumerate(targets):
        for place in range(target.shape[0]):

            def fetch(condition, source, target=target, place=place, part=part):
                @pl.when(condition)
                def _():
                    pltpu.make_async_copy(source, target.at[place], sems.at[part]).start()

            rank = jnp.int32(j)
            taken = rank < excess
            if cap > chunk:
                fetch(taken, rest_ref.at[jnp.minimum(rank, cap - chunk - 1)])
            rank = rank - excess
            for shift in range(1, n_req):
                here = jnp.logical_not(taken) & (rank < count_ref[shift])
                half = rank // half_cap
                slot = jnp.clip(rank - half * half_cap, 0, half_cap - 1)
                fetch(here & (half == seq_idx), mine_ref.at[shift - 1, slot])
                fetch(here & (half != seq_idx), other_ref.at[shift - 1, slot])
                taken = taken | here
                rank = rank - count_ref[shift]
            fetch(jnp.logical_not(taken), mine_ref.at[0, 0])
            j += 1
    for part, target in enumerate(targets):
        pltpu.make_async_copy(target, target, sems.at[part]).wait()


def join_pages(counts, rest, mine, other, chunk, cap, sizes):
    return pl.pallas_call(
        functools.partial(join_kernel, chunk, cap),
        out_shape=tuple(jax.ShapeDtypeStruct((size, *rest.shape[1:]), jnp.bfloat16) for size in sizes),
        in_specs=[smem_spec()] + [hbm_spec()] * 3,
        out_specs=(vmem_spec(),) * len(sizes),
        scratch_shapes=[pltpu.SemaphoreType.DMA((len(sizes),))],
        compiler_params=pltpu.CompilerParams(vmem_limit_bytes=10 * MIB),
        cost_estimate=pl.CostEstimate(flops=0, bytes_accessed=3 * 10**6, transcendentals=0),
        name="join_pages",
    )(counts, rest, mine, other)


def plan_kernel(page_len, chunk, owner_ref, prefix_ref, limit_ref):
    n_head = lax.axis_size("head")
    n_req = lax.axis_size("req")
    head_idx = lax.axis_index("head")
    req_idx = lax.axis_index("req")
    upward = 2 * lax.axis_index("seq") - 1
    n = owner_ref.shape[1]
    prefix = prefix_ref[req_idx]
    diagonal = lax.broadcasted_iota(jnp.int32, (n, n), 0) == lax.broadcasted_iota(jnp.int32, (n, n), 1)

    def column(values):
        return jnp.sum(jnp.where(diagonal, values, 0), axis=1, keepdims=True)

    owner = owner_ref[pl.ds(req_idx, 1), :]
    place = jnp.zeros_like(owner)
    for head in range(1, n_head):
        place = place + (owner >= head * n_req).astype(jnp.int32)
    shift = req_idx - (owner - place * n_req)
    shift = jnp.where(shift < 0, shift + n_req, shift)
    order = lax.broadcasted_iota(jnp.int32, (1, n), 1)
    needed = (order * page_len < prefix).astype(jnp.int32)
    key = shift * n + order
    together = (column(place) == place) & (column(needed) > 0)
    rank = jnp.sum((together & (column(key) < key)).astype(jnp.int32), axis=0, keepdims=True)
    held = jnp.sum((together & (column(shift) == 0)).astype(jnp.int32), axis=0, keepdims=True)
    early = (shift == 0) & (rank < chunk)
    within = jnp.where(early, rank, chunk + rank - jnp.minimum(held, chunk))
    away = place - head_idx
    distance = jnp.abs(away)
    origin = jnp.where(away * upward > 0, 2 * distance - 1, 2 * distance)
    origins = 2 * n_head - 1
    slot = jnp.where(
        within < chunk,
        origin * chunk + within,
        jnp.where(
            within < 3 * chunk,
            (origins + 2 * origin) * chunk + within - chunk,
            (3 * origins + origin) * chunk + within - 3 * chunk,
        ),
    )
    slot = column(jnp.where(needed > 0, slot, -1))
    tokens = column(jnp.clip(prefix - order * page_len, 0, page_len))
    lane = lax.broadcasted_iota(jnp.int32, (n, limit_ref.shape[1]), 1)
    limit_ref[...] = jnp.sum(jnp.where(lane == slot, tokens, 0), axis=0, keepdims=True)


def plan_blocks(page_owner, prefix_len, n_head, chunk, page_len):
    return pl.pallas_call(
        functools.partial(plan_kernel, page_len, chunk),
        out_shape=jax.ShapeDtypeStruct((1, 4 * (2 * n_head - 1) * chunk), jnp.int32),
        in_specs=[vmem_spec(), smem_spec()],
        out_specs=vmem_spec(),
        cost_estimate=pl.CostEstimate(flops=10**4, bytes_accessed=10**4, transcendentals=0),
        name="plan_blocks",
    )(page_owner, prefix_len)


def over_groups(most):
    n_groups = lax.axis_size("groups")
    passed = most
    for _ in range(n_groups - 1):
        passed = lax.ppermute(passed, "groups", [(i, (i + 1) % n_groups) for i in range(n_groups)])
        most = jnp.maximum(most, passed)
    return most[0]


def query_kernel(query_hbm, up_hbm, cosine_ref, sine_ref, out_ref, query_ref, up_ref, sems):
    loads = [
        pltpu.make_async_copy(query_hbm, query_ref, sems.at[0]),
        pltpu.make_async_copy(up_hbm, up_ref, sems.at[1]),
    ]
    for load in loads:
        load.start()
    for load in loads:
        load.wait()
    heads, nope_width, latent_width = up_ref.shape
    half_len, width = query_ref.shape
    query_width = width // heads
    half_rope = cosine_ref.shape[0]
    key_width = latent_width + 2 * half_rope
    for head in range(heads):
        part = slice(head * half_len, (head + 1) * half_len)
        both = query_ref[:, head * query_width : (head + 1) * query_width]
        latent = lax.dot_general(
            up_ref[head], both[:, :nope_width], (((0,), (1,)), ((), ())), preferred_element_type=jnp.float32
        )
        out_ref[:latent_width, part] = latent.astype(jnp.bfloat16)
        turned = both[:, nope_width:].astype(jnp.float32).T
        low, high = turned[:half_rope], turned[half_rope:]
        out_ref[latent_width : latent_width + half_rope, part] = (
            low * cosine_ref[...] - high * sine_ref[...]
        ).astype(jnp.bfloat16)
        out_ref[latent_width + half_rope : key_width, part] = (
            low * sine_ref[...] + high * cosine_ref[...]
        ).astype(jnp.bfloat16)
    rest = out_ref.shape[0] - key_width
    row = lax.broadcasted_iota(jnp.int32, (rest, out_ref.shape[1]), 0)
    out_ref[key_width:, :] = (row == 0).astype(jnp.bfloat16)


def turn_queries(queries, w_uk, cosine_table, sine_table, key_rows):
    heads, nope_width, latent_width = w_uk.shape
    rows = heads * queries.shape[0]
    return pl.pallas_call(
        query_kernel,
        out_shape=jax.ShapeDtypeStruct((key_rows, rows), jnp.bfloat16),
        in_specs=[any_spec()] * 2 + [vmem_spec()] * 2,
        out_specs=vmem_spec(),
        scratch_shapes=[
            pltpu.VMEM(queries.shape, jnp.bfloat16),
            pltpu.VMEM(w_uk.shape, jnp.bfloat16),
            pltpu.SemaphoreType.DMA((2,)),
        ],
        compiler_params=pltpu.CompilerParams(vmem_limit_bytes=60 * MIB),
        cost_estimate=pl.CostEstimate(
            flops=2 * rows * nope_width * latent_width, bytes_accessed=3 * 10**6, transcendentals=0
        ),
        name="turn_queries",
    )(queries, w_uk, cosine_table, sine_table)


def score_block(keys, queries_ref, target, note, highest, weight_sum, tile, scale, bias=None):
    rows = queries_ref.shape[1]
    for start in range(0, rows, tile):
        part = slice(start, start + tile)
        scores = jnp.dot(keys[...], queries_ref[:, part], preferred_element_type=jnp.float32) * scale
        if bias is not None:
            scores = scores + bias
        old = highest[:, part]
        new = jnp.maximum(old, jnp.max(scores, axis=0, keepdims=True))
        weights = jnp.exp2(scores - new)
        highest[:, part] = new
        weight_sum[:, part] = weight_sum[:, part] * jnp.exp2(old - new) + jnp.sum(
            weights, axis=0, keepdims=True
        )
        target[:, part] = weights
        note(part, new)


def block_limits(limit_ref, block, chunk):
    return [limit_ref[0, block * chunk + j] for j in range(chunk)]


def any_token(limit_ref, block, chunk):
    return functools.reduce(jnp.maximum, block_limits(limit_ref, block, chunk)) > 0


def load_block(block_ref, keys, limits, key_width):
    chunk, pairs, pair_width = block_ref.shape
    pair_rows = chunk * pairs
    page_rows = block_ref[...].reshape(pair_rows, pair_width)
    keys[:pair_rows, :key_width] = page_rows[:, :key_width]
    keys[pair_rows:, :key_width] = page_rows[:, key_width:]
    shape = (2 * pair_rows, keys.shape[1] - key_width)
    row = lax.broadcasted_iota(jnp.int32, shape, 0)
    pair_row = lax.rem(row, pair_rows)
    token = 2 * lax.rem(pair_row, pairs) + row // pair_rows
    limit = jnp.zeros_like(row)
    for j, value in enumerate(limits):
        limit = jnp.where(pair_row // pairs == j, value, limit)
    masked = (lax.broadcasted_iota(jnp.int32, shape, 1) == 0) & (token >= limit)
    keys[:, key_width:] = jnp.where(masked, MASKED, 0.0).astype(jnp.bfloat16)


def turn_values(keys, latent_width):
    return keys[:, :latent_width].T


def near_bias(n_keys, half_len, tile, live):
    seq_idx = lax.axis_index("seq")
    place = lax.broadcasted_iota(jnp.int32, (n_keys, tile), 0)
    query = lax.rem(lax.broadcasted_iota(jnp.int32, (n_keys, tile), 1), half_len) + seq_idx * half_len
    allowed = (place <= query) & (place < live)
    return jnp.where(allowed, 0.0, -jnp.inf)


def score_kernel(shape, base, n_sources, first, near, limit_ref, queries_ref, *refs):
    tile, scale, chunk, key_width = shape
    refs = list(refs)
    if not first:
        marks_in, sum_in, high_in = [refs.pop(0) for _ in range(3)]
        refs.pop(0), refs.pop(0)
    if near:
        live_ref, suffix_ref = refs.pop(0), refs.pop(0)
    sources = [refs.pop(0) for _ in range(n_sources)]
    weights_hbm, values_hbm, marks, weight_sum, highest = [refs.pop(0) for _ in range(5)]
    if near:
        near_weights, near_values, near_mark = [refs.pop(0) for _ in range(3)]
    blocks, keys, weights, values, load_sems, weight_sems, value_sems = [refs.pop(0) for _ in range(7)]
    n_blocks = blocks.shape[0]
    latent_width = values.shape[1]
    index = 0
    for source in sources:
        for i in range(source.shape[0] // chunk):
            pltpu.make_async_copy(
                source.at[i * chunk : (i + 1) * chunk], blocks.at[index], load_sems.at[index]
            ).start()
            index += 1
    if first:
        marks[...] = jnp.zeros_like(marks)
        weight_sum[...] = jnp.zeros_like(weight_sum)
        highest[...] = jnp.full_like(highest, LOWEST)
    else:
        marks[...] = marks_in[...]
        weight_sum[...] = sum_in[...]
        highest[...] = high_in[...]

    def stores(block):
        return (
            pltpu.make_async_copy(weights.at[block], weights_hbm.at[base + block], weight_sems.at[block]),
            pltpu.make_async_copy(values.at[block], values_hbm.at[base + block], value_sems.at[block]),
        )

    def one_block(block, carry):
        pltpu.make_async_copy(blocks.at[block], blocks.at[block], load_sems.at[block]).wait()

        @pl.when(any_token(limit_ref, base + block, chunk))
        def _():
            load_block(blocks.at[block], keys, block_limits(limit_ref, base + block, chunk), key_width)

            def note(part, new):
                marks[pl.ds(base + block, 1), part] = new

            score_block(
                keys, queries_ref, weights.at[block], note, highest, weight_sum, tile, scale
            )
            values[block] = turn_values(keys, latent_width)
            for copy in stores(block):
                copy.start()

        return carry

    lax.fori_loop(0, n_blocks, one_block, 0)
    if near:
        near_keys = refs.pop(0)
        n_near = suffix_ref.shape[0]
        near_keys[:, key_width:] = jnp.zeros_like(near_keys[:, key_width:])
        near_keys[:, :key_width] = suffix_ref[...]

        def note_near(part, new):
            near_mark[:, part] = new

        score_block(
            near_keys, queries_ref, near_weights, note_near, highest, weight_sum, tile, scale,
            near_bias(n_near, n_near // lax.axis_size("seq"), tile, live_ref[0]),
        )
        near_values[...] = turn_values(near_keys, latent_width)

    def one_wait(block, carry):
        @pl.when(any_token(limit_ref, base + block, chunk))
        def _():
            for copy in stores(block):
                copy.wait()

        return carry

    lax.fori_loop(0, n_blocks, one_wait, 0)


def score_part(base, total, limits, queries, sources, state, shape, latent_width, near=None):
    tile, scale, chunk, key_width = shape
    width, rows = queries.shape
    _, pairs, pair_width = sources[0].shape
    block_keys = 2 * chunk * pairs
    n_blocks = sum(s.shape[0] for s in sources) // chunk
    row = jax.ShapeDtypeStruct((1, rows), jnp.float32)
    out_shape = [
        jax.ShapeDtypeStruct((total, block_keys, rows), jnp.float32),
        jax.ShapeDtypeStruct((total, latent_width, block_keys), jnp.bfloat16),
        jax.ShapeDtypeStruct((total, rows), jnp.float32),
        row,
        row,
    ]
    out_specs = [hbm_spec(), hbm_spec(), vmem_spec(), vmem_spec(), vmem_spec()]
    operands = [limits, queries]
    specs = [smem_spec(), vmem_spec()]
    aliases = {}
    if state is not None:
        operands += [state[2], state[3], state[4], state[0], state[1]]
        specs += [vmem_spec()] * 3 + [hbm_spec()] * 2
        aliases = {5: 0, 6: 1}
    scratch = [
        pltpu.VMEM((n_blocks, chunk, pairs, pair_width), jnp.bfloat16),
        pltpu.VMEM((block_keys, width), jnp.bfloat16),
        pltpu.VMEM((n_blocks, block_keys, rows), jnp.float32),
        pltpu.VMEM((n_blocks, latent_width, block_keys), jnp.bfloat16),
        pltpu.SemaphoreType.DMA((n_blocks,)),
        pltpu.SemaphoreType.DMA((n_blocks,)),
        pltpu.SemaphoreType.DMA((n_blocks,)),
    ]
    if near is not None:
        near_keys = near[-1].shape[0]
        operands += list(near)
        specs += [smem_spec(), vmem_spec()]
        out_shape += [
            jax.ShapeDtypeStruct((near_keys, rows), jnp.float32),
            jax.ShapeDtypeStruct((latent_width, near_keys), jnp.bfloat16),
            row,
        ]
        out_specs += [vmem_spec()] * 3
        scratch.append(pltpu.VMEM((near_keys, width), jnp.bfloat16))
    operands += list(sources)
    specs += [hbm_spec()] * len(sources)
    work = n_blocks * block_keys * rows // 2
    return pl.pallas_call(
        functools.partial(score_kernel, shape, base, len(sources), state is None, near is not None),
        out_shape=tuple(out_shape),
        in_specs=specs,
        out_specs=tuple(out_specs),
        scratch_shapes=scratch,
        input_output_aliases=aliases,
        compiler_params=pltpu.CompilerParams(vmem_limit_bytes=54 * MIB),
        cost_estimate=pl.CostEstimate(
            flops=work, bytes_accessed=10**5, transcendentals=0
        ),
        name="score_part",
    )(*operands)


def finish_kernel(
    shape, depth, n_blocks, n_sources, limit_ref, queries_ref, marks, sum_in, high_in,
    near_weights, near_values, near_mark, live_ref, up_ref, weights_hbm, values_hbm, *refs,
):
    tile, scale, chunk, key_width = shape
    sources, refs = refs[:n_sources], refs[n_sources:]
    (
        out_ref, weight_sum, highest, total, blocks, keys, last_weights, last_values, last_marks,
        weights, values, used, load_sems, weight_sems, value_sems,
    ) = refs
    rows = queries_ref.shape[1]
    latent_width = total.shape[0]
    n_last = blocks.shape[0]
    index = 0
    for source in sources:
        for i in range(source.shape[0] // chunk):
            pltpu.make_async_copy(
                source.at[i * chunk : (i + 1) * chunk], blocks.at[index], load_sems.at[index]
            ).start()
            index += 1

    def list_block(block, count):
        used[count] = block
        return count + any_token(limit_ref, block, chunk).astype(jnp.int32)

    n_used = lax.fori_loop(0, n_blocks, list_block, jnp.int32(0))

    def fetches(number):
        place = lax.rem(number, depth)
        return (
            pltpu.make_async_copy(weights_hbm.at[used[number]], weights.at[place], weight_sems.at[place]),
            pltpu.make_async_copy(values_hbm.at[used[number]], values.at[place], value_sems.at[place]),
        )

    def fetch(number):
        @pl.when(number < n_used)
        def _():
            for copy in fetches(number):
                copy.start()

    for number in range(depth):
        fetch(jnp.int32(number))
    weight_sum[...] = sum_in[...]
    highest[...] = high_in[...]
    last_marks[...] = jnp.zeros_like(last_marks)

    def one_score(block, carry):
        pltpu.make_async_copy(blocks.at[block], blocks.at[block], load_sems.at[block]).wait()

        @pl.when(any_token(limit_ref, n_blocks + block, chunk))
        def _():
            load_block(blocks.at[block], keys, block_limits(limit_ref, n_blocks + block, chunk), key_width)

            def note(part, new):
                last_marks[pl.ds(block, 1), part] = new

            score_block(
                keys, queries_ref, last_weights.at[block], note, highest, weight_sum, tile, scale
            )
            last_values[block] = turn_values(keys, latent_width)

        return carry

    lax.fori_loop(0, n_last, one_score, 0)

    def add_block(weight_block, value_block, mark, begin=False):
        for start in range(0, rows, tile):
            part = slice(start, start + tile)
            factor = jnp.exp2(mark[:, part] - highest[:, part]) / weight_sum[:, part]
            added = jnp.dot(
                value_block[...],
                (weight_block[:, part] * factor).astype(jnp.bfloat16),
                preferred_element_type=jnp.float32,
            )
            total[:, part] = added if begin else total[:, part] + added

    add_block(near_weights, near_values, near_mark, begin=True)

    def one_add(number, carry):
        for copy in fetches(number):
            copy.wait()
        place = lax.rem(number, depth)
        add_block(weights.at[place], values.at[place], marks.at[pl.ds(used[number], 1)])
        fetch(number + depth)
        return carry

    lax.fori_loop(0, n_used, one_add, 0)

    def one_last(block, carry):
        @pl.when(any_token(limit_ref, n_blocks + block, chunk))
        def _():
            add_block(last_weights.at[block], last_values.at[block], last_marks.at[pl.ds(block, 1)])

        return carry

    lax.fori_loop(0, n_last, one_last, 0)
    heads, _, value_width = up_ref.shape
    half_len = out_ref.shape[0]
    steps = lax.broadcasted_iota(jnp.int32, (half_len, value_width), 0)
    steps = steps + lax.axis_index("seq") * half_len
    for head in range(heads):
        latent = total[:, head * half_len : (head + 1) * half_len].astype(jnp.bfloat16)
        raised = lax.dot_general(
            latent, up_ref[head], (((0,), (0,)), ((), ())), preferred_element_type=jnp.float32
        )
        out_ref[:, head * value_width : (head + 1) * value_width] = jnp.where(
            steps < live_ref[0], raised, 0.0
        ).astype(jnp.bfloat16)


def finish(n_blocks, limits, queries, state, near_state, sources, live, up_weight, half_len, shape):
    tile, scale, chunk, key_width = shape
    weights, values, marks, weight_sum, highest = state
    width, rows = queries.shape
    _, latent_width, block_keys = values.shape
    _, pairs, pair_width = sources[0].shape
    heads, _, value_width = up_weight.shape
    depth = 4
    n_last = sum(s.shape[0] for s in sources) // chunk
    row = pltpu.VMEM((1, rows), jnp.float32)
    work = (n_blocks // 2 + n_last) * block_keys * rows
    return pl.pallas_call(
        functools.partial(finish_kernel, shape, depth, n_blocks, len(sources)),
        out_shape=jax.ShapeDtypeStruct((half_len, heads * value_width), jnp.bfloat16),
        in_specs=[smem_spec()]
        + [vmem_spec()] * 7
        + [smem_spec(), vmem_spec()]
        + [hbm_spec()] * (2 + len(sources)),
        out_specs=vmem_spec(),
        scratch_shapes=[
            row,
            row,
            pltpu.VMEM((latent_width, rows), jnp.float32),
            pltpu.VMEM((n_last, chunk, pairs, pair_width), jnp.bfloat16),
            pltpu.VMEM((block_keys, width), jnp.bfloat16),
            pltpu.VMEM((n_last, block_keys, rows), jnp.float32),
            pltpu.VMEM((n_last, latent_width, block_keys), jnp.bfloat16),
            pltpu.VMEM((n_last, rows), jnp.float32),
            pltpu.VMEM((depth, block_keys, rows), jnp.float32),
            pltpu.VMEM((depth, latent_width, block_keys), jnp.bfloat16),
            pltpu.SMEM((n_blocks + depth + 1,), jnp.int32),
            pltpu.SemaphoreType.DMA((n_last,)),
            pltpu.SemaphoreType.DMA((depth,)),
            pltpu.SemaphoreType.DMA((depth,)),
        ],
        compiler_params=pltpu.CompilerParams(vmem_limit_bytes=54 * MIB),
        cost_estimate=pl.CostEstimate(
            flops=2 * work * latent_width, bytes_accessed=3 * 10**7, transcendentals=work // 4
        ),
        name="finish",
    )(
        limits, queries, marks, weight_sum, highest, *near_state, live, up_weight,
        weights, values, *sources,
    )


def local(
    queries,
    hidden,
    w_dkv,
    kv_gain,
    w_uk,
    value_up_weight,
    page_pool,
    page_owner,
    page_slot,
    prefix_len,
    suffix_len,
):
    n_head = lax.axis_size("head")
    n_req = lax.axis_size("req")
    n_seq = lax.axis_size("seq")
    head_idx = lax.axis_index("head")
    req_idx = lax.axis_index("req")
    seq_idx = lax.axis_index("seq")
    _, half_len, d_local = hidden.shape
    heads_dev, nope_width, latent_width = w_uk.shape
    lat_width = w_dkv.shape[1]
    rope_width = lat_width - latent_width
    query_width = queries.shape[2] // heads_dev
    page_width = page_pool.shape[1]
    page_len = page_width // lat_width
    pairs = page_len // 2
    pages_req = page_slot.shape[1]
    cap = max(2, 2 * pages_req // (n_head * n_req))
    chunk = n_req * cap // 4
    score_scale = float(query_width) ** (-0.5)

    owner_rows = page_owner[:, :, 0]
    counts, most, my_prefix, live, first, rest, foreign, partial_value = pick_pages(
        owner_rows, page_slot, prefix_len, suffix_len, page_pool, hidden[0], w_dkv.T,
        cap, chunk, n_head, n_req, n_seq, pairs,
    )
    swap_route = [(i, n_seq - 1 - i) for i in range(n_seq)]
    stream_route = []
    for i in range(n_head - 1):
        stream_route.append((i * n_seq, (i + 1) * n_seq))
        stream_route.append(((i + 1) * n_seq + 1, i * n_seq + 1))

    def swap(block):
        return lax.ppermute(block, "seq", swap_route)

    def stream(block):
        return lax.ppermute(block, ("head", "seq"), stream_route)

    positions = my_prefix + seq_idx * half_len + jnp.arange(half_len, dtype=jnp.int32)
    rows = heads_dev * half_len
    half_rope = rope_width // 2
    frequency = 10000.0 ** (-2.0 * jnp.arange(half_rope, dtype=jnp.float32) / rope_width)
    phases = frequency[:, None] * positions.astype(jnp.float32)[None, :]
    q_turned = turn_queries(queries[0], w_uk, jnp.cos(phases), jnp.sin(phases), lat_width + 64)

    arrived = [
        lax.ppermute(foreign[s - 1], "req", [(i, (i + s) % n_req) for i in range(n_req)])
        for s in range(1, n_req)
    ]
    early_steps = [stream(first)]
    share = half_len // n_head
    partials = lax.all_to_all(partial_value, "head", split_axis=0, concat_axis=0, tiled=True)
    summed = jnp.sum(partials.reshape(n_head, share, lat_width), axis=0)
    share_t = seq_idx * half_len + head_idx * share + jnp.arange(share, dtype=jnp.int32)
    latent = finish_latent(summed, my_prefix + share_t, share_t < live, kv_gain, latent_width)
    copies = jnp.concatenate([latent] * n_head, axis=0)
    fresh = lax.all_to_all(copies, "head", split_axis=0, concat_axis=0, tiled=True)
    early_steps[0], fresh = lax.optimization_barrier((early_steps[0], fresh))
    for step in range(1, n_head - 1):
        early_steps.append(stream(early_steps[-1]))
    early_steps = [[block, None] for block in early_steps]
    for step in range(n_head - 2):
        early_steps[step][1] = swap(early_steps[step][0])
    mine = arrived[0][None] if n_req == 2 else jnp.stack(arrived)
    most = over_groups(most)
    mine, fresh, most = lax.optimization_barrier((mine, fresh, most))
    other = swap(mine)
    middle, late = join_pages(counts, rest, mine, other, chunk, cap, (2 * chunk, chunk))

    tile = 256 if rows % 256 == 0 and 256 % half_len == 0 else half_len
    shape = (tile, score_scale * math.log2(math.e), chunk, lat_width)
    last = n_head - 2
    near_state = ()
    extra = 4 + 1 + 2 * last
    total = 1 + 2 * (last + 1) + 2 + 4 * last + extra
    limits = plan_blocks(owner_rows, prefix_len, n_head, chunk, page_len)
    n_blocks = 0
    state = None

    def arrays_of(arrived_steps, steps):
        return [arrived_steps[step][side] for step in steps for side in range(2)]

    def score(arrays, near=None):
        nonlocal n_blocks, state, near_state
        result = score_part(
            n_blocks, total, limits, q_turned, arrays, state, shape, latent_width, near
        )
        state = result[:5]
        near_state = result[5:] or near_state
        n_blocks += sum(a.shape[0] for a in arrays) // chunk

    def tie(block):
        nonlocal state
        block, mark = lax.optimization_barrier((block, state[4]))
        state = (*state[:4], mark)
        return block

    middle, early_steps[last - 1][0] = lax.optimization_barrier((middle, early_steps[last - 1][0]))
    middle_steps = []
    block = stream(middle)
    for step in range(last + 1):
        received = block
        if step == 0:
            score([first] + arrays_of(early_steps, range(last)))
        elif step == 1:
            score(arrays_of(early_steps, [last]) + [middle] + arrays_of(middle_steps, [0]))
        else:
            score(
                arrays_of(middle_steps, [step - 1]), (live, suffix_latent) if step == last else None
            )
        received = tie(received)
        if step == 0:
            early_steps[last][0] = tie(early_steps[last][0])
            early_steps[last][1] = swap(early_steps[last][0])
            opposite = swap(fresh)
            suffix_latent = jnp.where(
                seq_idx == 0,
                jnp.concatenate([fresh, opposite], axis=0),
                jnp.concatenate([opposite, fresh], axis=0),
            )
        if step < last:
            block = stream(received)
        middle_steps.append([received, swap(received)])

    last_arrays = arrays_of(middle_steps, [last])

    def end(blocks, final_arrays, current):
        return finish(
            blocks, limits, q_turned, current, near_state, final_arrays, live, value_up_weight, half_len, shape
        )

    def with_late(_):
        block = stream(late)
        arrays = last_arrays + [late]
        current, blocks = state, n_blocks
        for step in range(last + 1):
            received = block
            current = score_part(
                blocks, total, limits, q_turned, arrays, current, shape, latent_width
            )[:5]
            blocks += sum(a.shape[0] for a in arrays) // chunk
            received, mark = lax.optimization_barrier((received, current[4]))
            current = (*current[:4], mark)
            if step < last:
                block = stream(received)
            arrays = [received, swap(received)]
        return end(blocks, arrays, current)

    def without_late(_):
        return end(n_blocks, last_arrays, state)

    attn_out = lax.cond(most > 2 * chunk, with_late, without_late, 0)
    new_pages = fresh.reshape(1, half_len // page_len, page_len * lat_width)
    return (attn_out[None], new_pages)


def solution(mesh):
    placed = (
        P(("groups", "req"), "seq", "head"),
        P(("groups", "req"), "seq", "head"),
        P("head", None),
        P(),
        P("head", None, None),
        P("head", None, None),
        P(("groups", "head", "req"), None),
        P("groups", None, None),
        P("groups", None),
        P("groups"),
        P("groups"),
    )
    return jax.shard_map(
        local,
        mesh=mesh,
        in_specs=placed,
        out_specs=(P(("groups", "req"), "seq", "head"), P(("groups", "req"), "seq", None)),
        check_vma=False,
    )
```

profile of v0, /device:TPU:0, one launch (start us, length us, event | category | flops | bytes accessed | tf_op | source)
XLA Modules:
  0.0 122.0 jit_solution(8973119154599744185)
XLA Ops:
  0.6 5.0 %pick_pages.1 = (s32[2]{0:T(128)}, s32[1]{0:T(128)}, s32[1]{0:T(128)}, s32[1]{0:T(128)}, bf16[8,32,1152]{2,1,0:T(8,128)(2,1)}, /*index=5*/bf16[8,32,1152]{2,1,0:...) custom-call(s32[2,64]{1,0:T(2,128)} %bitcast.24, s32[2,64]{1,0:T(2,128)} %slot_hbm.1, s32[2]{0:T(128)} %prefix_ref.1, ...), custom_call_target="tpu_custom_call" | custom-call | flops 1000000000 | bytes 6000000 | tf_op jit(solution)/shard_map/pick_pages/pallas_call | solution.py:163
  5.6 6.3 %all-to-all-start = ((f32[4,32,576]{2,1,0:T(8,128)}), f32[4,32,576]{2,1,0:T(8,128)S(1)}, u32[]{:S(2)}, u32[]{:S(2)}) async-start(f32[4,32,576]{2,1,0:T(8,128)} %bitcast.21), calls=%async_computation | async-start | bytes 655360 | tf_op jit(solution)/shard_map/all_to_all | solution.py:780
  12.0 4.0 %collective-permute-start.7 = (bf16[8,32,1152]{2,1,0:T(8,128)(2,1)}, bf16[8,32,1152]{2,1,0:T(8,128)(2,1)S(1)}, u32[]{:S(2)}, u32[]{:S(2)}) collective-permute-start(bf16[8,32,1152]{2,1,0:T(8,128)(2,1)} %get-tuple-element.158.refs_0_), channel_id=1, source_target_pairs={{0,4},{5,1},{4,8},{9,5},{8,12},{13,9},{2,6},{7,3},{6,10},{11,7},{1... | collective-permute-start | bytes 1769480 | tf_op jit(solution)/shard_map/ppermute | solution.py:765
  15.9 1.6 %collective-permute-start.6 = (bf16[8,32,1152]{2,1,0:T(8,128)(2,1)}, bf16[8,32,1152]{2,1,0:T(8,128)(2,1)S(1)}, u32[]{:S(2)}, u32[]{:S(2)}) collective-permute-start(bf16[8,32,1152]{2,1,0:T(8,128)(2,1)} %bitcast.26), channel_id=1, source_target_pairs={{0,2},{2,0},{1,3},{3,1},{4,6},{6,4},{5,7},{7,5},{8,10},{10,8},{9,1... | collective-permute-start | bytes 1769480 | tf_op jit(solution)/shard_map/ppermute | solution.py:775
  17.5 0.6 add_convert_fusion.1
  18.1 0.6 fusion.8
  18.8 4.6 %all-to-all-done = f32[4,32,576]{2,1,0:T(8,128)S(1)} async-done(((f32[4,32,576]{2,1,0:T(8,128)}), f32[4,32,576]{2,1,0:T(8,128)S(1)}, u32[]{:S(2)}, u32[]{:S(2)}) %all-to-all-start) | async-done | bytes 294944 | tf_op jit(solution)/shard_map/all_to_all | solution.py:780
  23.4 0.1 multiply_reduce_fusion
  23.5 0.8 multiply_convert_fusion
  24.3 0.1 fusion.5
  24.4 0.1 maximum_select_fusion.1
  24.5 0.7 pad_maximum_fusion
  25.2 4.0 %all-to-all-start.1 = ((bf16[4,32,576]{2,1,0:T(8,128)(2,1)}), bf16[4,32,576]{2,1,0:T(8,128)(2,1)}, u32[]{:S(2)}, u32[]{:S(2)}) async-start(bf16[4,32,576]{2,1,0:T(8,128)(2,1)} %bitcast.10), calls=%async_computation.1 | async-start | bytes 327680 | tf_op jit(solution)/shard_map/all_to_all | solution.py:785
  29.1 1.6 %collective-permute-start.8 = (s32[1]{0:T(128)}, s32[1]{0:T(128)}, u32[]{:S(2)}, u32[]{:S(2)}) collective-permute-start(s32[1]{0:T(128)} %get-tuple-element.163), channel_id=1, source_target_pairs={{0,16},{16,0},{1,17},{17,1},{2,18},{18,2},{3,19},{19,3},{4,20},{20... | collective-permute-start | bytes 20 | tf_op jit(solution)/shard_map/ppermute | solution.py:304
  30.7 2.2 %collective-permute-done.8 = s32[1]{0:T(128)} collective-permute-done((s32[1]{0:T(128)}, s32[1]{0:T(128)}, u32[]{:S(2)}, u32[]{:S(2)}) %collective-permute-start.8) | collective-permute-done | bytes 36 | tf_op jit(solution)/shard_map/ppermute | solution.py:304
  34.2 0.0 collective-permute-done.7.refs_1_
  34.2 0.0 copy-start.13
  34.2 1.0 all-to-all-done.1
  35.2 0.0 collective-permute-done.6
  35.2 0.0 collective-permute-start.10
  35.2 4.2 %collective-permute-start.11 = (bf16[8,32,1152]{2,1,0:T(8,128)(2,1)S(1)}, bf16[8,32,1152]{2,1,0:T(8,128)(2,1)}, u32[]{:S(2)}, u32[]{:S(2)}) collective-permute-start(bf16[8,32,1152]{2,1,0:T(8,128)(2,1)S(1)} %collective-permute-done.7.refs_1_), channel_id=1, source_target_pairs={{0,4},{5,1},{4,8},{9,5},{8,12},{13,9},{2,6},{7,3},{6,10},{11,7},{1... | collective-permute-start | bytes 1769480 | tf_op jit(solution)/shard_map/ppermute | solution.py:765
  39.4 0.0 collective-permute-done.10.other_ref
  39.4 1.1 copy-done.1
  40.5 0.7 copy-done.2
  41.1 4.3 %join_pages.1 = (bf16[16,32,1152]{2,1,0:T(8,128)(2,1)S(1)}, bf16[8,32,1152]{2,1,0:T(8,128)(2,1)}) custom-call(s32[2]{0:T(128)S(1)} %copy-done.2, bf16[8,32,1152]{2,1,0:T(8,128)(2,1)S(1)} %copy-done.1, bf16[1,8,32,1152]{3,2,1,0:T(8,128)(2,1)S(1)} %bitcast.17, bf16[1,8,32,1152]{3,2,1,0:T(8,128)(2,1)S(1)} %collective-permute-done.10.other_ref), custom_call_target="tpu_custom_call" | custom-call | bytes 3000000 | tf_op jit(solution)/shard_map/join_pages/pallas_call | solution.py:231
  45.5 0.0 copy-start
  45.5 0.5 collective-permute-done.11.refs_3_
  45.9 5.5 %collective-permute-start.14 = (bf16[16,32,1152]{2,1,0:T(8,128)(2,1)S(1)}, bf16[16,32,1152]{2,1,0:T(8,128)(2,1)}, u32[]{:S(2)}, u32[]{:S(2)}) collective-permute-start(bf16[16,32,1152]{2,1,0:T(8,128)(2,1)S(1)} %get-tuple-element.173.refs_7_), channel_id=1, source_target_pairs={{0,4},{5,1},{4,8},{9,5},{8,12},{13,9},{2,6},{7,3},{6,10},{11,7},{1... | collective-permute-start | bytes 3538952 | tf_op jit(solution)/shard_map/ppermute | solution.py:765
  51.5 0.0 collective-permute-start.9
  51.5 0.5 collective-permute-start.12
  52.0 1.1 plan_blocks.1.limit_ref
  53.7 0.8 multiply_sine_fusion
  54.4 2.9 %turn_queries.1.queries_ref = bf16[640,1024]{1,0:T(8,128)(2,1)S(1)} custom-call(bf16[128,1536]{1,0:T(8,128)(2,1)} %bitcast.20, bf16[8,128,512]{2,1,0:T(8,128)(2,1)} %up_hbm.1, f32[32,128]{1,0:T(8,128)} %get-tuple-element.203.cosine_ref, f32[32,128]{1,0:T(8,128)} %get-tuple-element.202.sine_ref), custom_call_target="tpu_custom_call" | custom-call | flops 134217728 | bytes 3000000 | tf_op jit(solution)/shard_map/turn_queries/pallas_call | solution.py:346
  57.4 2.0 %collective-permute-start.13 = (bf16[8,32,1152]{2,1,0:T(8,128)(2,1)}, bf16[8,32,1152]{2,1,0:T(8,128)(2,1)S(1)}, u32[]{:S(2)}, u32[]{:S(2)}) collective-permute-start(bf16[8,32,1152]{2,1,0:T(8,128)(2,1)} %collective-permute-done.11.refs_3_), channel_id=1, source_target_pairs={{0,4},{5,1},{4,8},{9,5},{8,12},{13,9},{2,6},{7,3},{6,10},{11,7},{1... | collective-permute-start | bytes 1769480 | tf_op jit(solution)/shard_map/ppermute | solution.py:765
  59.4 0.0 collective-permute-done.9.refs_2_
  59.4 0.0 collective-permute-done.12.refs_4_
  59.4 0.0 copy-done.13
  59.4 7.9 %score_part.9 = (f32[26,512,1024]{2,1,0:T(8,128)}, bf16[26,512,512]{2,1,0:T(8,128)(2,1)}, f32[26,1024]{1,0:T(8,128)}, f32[1,1024]{1,0:T(1,128)}, f32[1,1024]{1,0:T(1,128)}) custom-call(s32[1,224]{1,0:T(1,128)S(1)} %plan_blocks.1.limit_ref, bf16[640,1024]{1,0:T(8,128)(2,1)S(1)} %turn_queries.1.queries_ref, bf16[8,32,1152]{2,1,0:T(8,128)(2,1)} %get-tuple-element.158.refs_0_, ...), custom_call_target="tpu_custom_call" | custom-call | flops 1310720 | bytes 100000 | tf_op jit(solution)/shard_map/score_part/pallas_call | solution.py:547
  67.3 0.0 collective-permute-done.14.refs_8_
  67.3 0.1 collective-permute-start.16
  67.4 5.9 %collective-permute-start.17 = (bf16[16,32,1152]{2,1,0:T(8,128)(2,1)}, bf16[16,32,1152]{2,1,0:T(8,128)(2,1)}, u32[]{:S(2)}, u32[]{:S(2)}) collective-permute-start(bf16[16,32,1152]{2,1,0:T(8,128)(2,1)} %collective-permute-done.14.refs_8_), channel_id=1, source_target_pairs={{0,4},{5,1},{4,8},{9,5},{8,12},{13,9},{2,6},{7,3},{6,10},{11,7},{1... | collective-permute-start | bytes 3538952 | tf_op jit(solution)/shard_map/ppermute | solution.py:765
  73.3 0.0 collective-permute-done.13.refs_5_
  73.3 0.0 collective-permute-start.15
  73.3 2.0 %collective-permute-done.15.refs_6_ = bf16[8,32,1152]{2,1,0:T(8,128)(2,1)S(1)} collective-permute-done((bf16[8,32,1152]{2,1,0:T(8,128)(2,1)S(1)}, bf16[8,32,1152]{2,1,0:T(8,128)(2,1)S(1)}, u32[]{:S(2)}, u32[]{:S(2)}) %collective-permute-start.15) | collective-permute-done | bytes 589856 | tf_op jit(solution)/shard_map/ppermute | solution.py:762
  75.3 0.0 collective-permute-done.16.refs_9_
  75.3 0.0 copy-done
  75.4 0.0 copy-done.14
  75.4 0.8 copy-done.15
  76.2 0.4 copy-done.5
  76.6 9.9 %score_part.10 = (f32[26,512,1024]{2,1,0:T(8,128)}, bf16[26,512,512]{2,1,0:T(8,128)(2,1)}, f32[26,1024]{1,0:T(8,128)}, f32[1,1024]{1,0:T(1,128)}, f32[1,1024]{1,0:T(1,128)}) custom-call(s32[1,224]{1,0:T(1,128)S(1)} %plan_blocks.1.limit_ref, bf16[640,1024]{1,0:T(8,128)(2,1)S(1)} %turn_queries.1.queries_ref, ...), custom_call_target="tpu_custom_call", output_to_operand_aliasing={{0}: (5, {}), {1}: (6, {})} | custom-call | flops 2097152 | bytes 100000 | tf_op jit(solution)/shard_map/score_part/pallas_call | solution.py:547
  86.5 0.0 collective-permute-done.17.refs_7_
  86.6 0.1 collective-permute-start.19
  86.6 4.1 %collective-permute-start.20 = (bf16[16,32,1152]{2,1,0:T(8,128)(2,1)}, bf16[16,32,1152]{2,1,0:T(8,128)(2,1)S(1)}, u32[]{:S(2)}, u32[]{:S(2)}) collective-permute-start(bf16[16,32,1152]{2,1,0:T(8,128)(2,1)} %collective-permute-done.17.refs_7_), channel_id=1, source_target_pairs={{0,4},{5,1},{4,8},{9,5},{8,12},{13,9},{2,6},{7,3},{6,10},{11,7},{1... | collective-permute-start | bytes 3538952 | tf_op jit(solution)/shard_map/ppermute | solution.py:765
  90.8 0.1 collective-permute-start.18
  90.8 1.6 %collective-permute-done.18 = bf16[128,576]{1,0:T(8,128)(2,1)S(1)} collective-permute-done((bf16[128,576]{1,0:T(8,128)(2,1)}, bf16[128,576]{1,0:T(8,128)(2,1)S(1)}, u32[]{:S(2)}, u32[]{:S(2)}) %collective-permute-start.18) | collective-permute-done | bytes 147488 | tf_op jit(solution)/shard_map/ppermute | solution.py:762
  92.4 1.8 %maximum_select_fusion.refs_6_ = bf16[256,576]{1,0:T(8,128)(2,1)} fusion(bf16[128,576]{1,0:T(8,128)(2,1)S(1)} %collective-permute-done.18, bf16[128,576]{1,0:T(8,128)(2,1)} %bitcast.11, pred[]{:T(512)S(6)} %eq.3), kind=kLoop, calls=%fused_computation | loop fusion | flops 1327104 | bytes 589825 | tf_op jit(solution)/shard_map/jit(_where)/select_n | solution.py:844
  94.2 0.0 collective-permute-done.19.refs_8_
  94.2 8.5 %score_part.11 = (f32[26,512,1024]{2,1,0:T(8,128)}, bf16[26,512,512]{2,1,0:T(8,128)(2,1)}, f32[26,1024]{1,0:T(8,128)}, f32[1,1024]{1,0:T(1,128)S(1)}, f32[1,1024...) custom-call(s32[1,224]{1,0:T(1,128)S(1)} %plan_blocks.1.limit_ref, ...), custom_call_target="tpu_custom_call", output_to_operand_aliasing={{0}: (5, {}), {1}: (6, {})} | custom-call | flops 1048576 | bytes 100000 | tf_op jit(solution)/shard_map/score_part/pallas_call | solution.py:547
  102.8 1.9 %collective-permute-done.20 = bf16[16,32,1152]{2,1,0:T(8,128)(2,1)S(1)} collective-permute-done((bf16[16,32,1152]{2,1,0:T(8,128)(2,1)}, bf16[16,32,1152]{2,1,0:T(8,128)(2,1)S(1)}, u32[]{:S(2)}, u32[]{:S(2)}) %collective-permute-start.20) | collective-permute-done | bytes 1179680 | tf_op jit(solution)/shard_map/ppermute | solution.py:765
  104.7 0.0 collective-permute-start.21
  104.7 1.8 %reshape.46 = bf16[1,2,36864]{2,1,0:T(2,128)(2,1)} reshape(bf16[128,576]{1,0:T(8,128)(2,1)} %bitcast.11) | data formatting | bytes 294912 | tf_op jit(solution)/shard_map/reshape | solution.py:881
  106.5 1.2 collective-permute-done.21
  107.7 14.1 %conditional.1 = (bf16[1,128,1024]{2,1,0:T(8,128)(2,1)}) conditional(s32[]{:T(128)} %convert_element_type.19, (s32[1,224]{1,0:T(1,128)S(1)}, bf16[640,1024]{1,0:T(8,128)(2,1)S(1)}, f32[26,1024]{1,0:T(8,128)}, f32[1,1024]{1,0:T(1,128)S(1)}, f32[1,1024]{1,0:T(1,128)S(1)}, /*index=5*/f32[256,1024]{1,0:T(8,128)}, bf16[512,256]{1,0:T(8,128)(2,1)}, ...), branch_computations={%region_2.3_spmd, %region_3.4_spmd} | conditional | flops 8055422976 | bytes 63854904 | solution.py:880
  107.7 13.9 %finish.2 = bf16[128,1024]{1,0:T(8,128)(2,1)} custom-call(s32[1,224]{1,0:T(1,128)S(1)} %get-tuple-element.62.limit_ref, bf16[640,1024]{1,0:T(8,128)(2,1)S(1)} %get-tuple-element.63.queries_ref, f32[26,1024]{1,0:T(8,128)} %get-tuple-element.64.marks, f32[1,1024]{1,0:T(1,128)S(1)} %get-tuple-element.65.sum_in, f32[1,1024]{1,0:T(1,128)S(1)} %get-tuple-element.66.high_in, ...), custom_call_target="tpu_custom_call" | custom-call | flops 6442450944 | bytes 30000000 | tf_op jit(solution)/shard_map/cond/branch_0_fun/finish/pallas_call | solution.py:683
  (11 shorter events, 0.1 us)
Async XLA Ops:
  5.6 17.7 %all-to-all-start = ((f32[4,32,576]{2,1,0:T(8,128)}), f32[4,32,576]{2,1,0:T(8,128)S(1)}, u32[]{:S(2)}, u32[]{:S(2)}) async-start(f32[4,32,576]{2,1,0:T(8,128)} %bitcast.21), calls=%async_computation | async-start | bytes 655360 | tf_op jit(solution)/shard_map/all_to_all | solution.py:780
  12.0 22.2 %collective-permute-start.7 = (bf16[8,32,1152]{2,1,0:T(8,128)(2,1)}, bf16[8,32,1152]{2,1,0:T(8,128)(2,1)S(1)}, u32[]{:S(2)}, u32[]{:S(2)}) collective-permute-start(bf16[8,32,1152]{2,1,0:T(8,128)(2,1)} %get-tuple-element.158.refs_0_), channel_id=1, source_target_pairs={{0,4},{5,1},{4,8},{9,5},{8,12},{13,9},{2,6},{7,3},{6,10},{11,7},{1... | collective-permute-start | bytes 1769480 | tf_op jit(solution)/shard_map/ppermute | solution.py:765
  15.9 19.3 %collective-permute-start.6 = (bf16[8,32,1152]{2,1,0:T(8,128)(2,1)}, bf16[8,32,1152]{2,1,0:T(8,128)(2,1)S(1)}, u32[]{:S(2)}, u32[]{:S(2)}) collective-permute-start(bf16[8,32,1152]{2,1,0:T(8,128)(2,1)} %bitcast.26), channel_id=1, source_target_pairs={{0,2},{2,0},{1,3},{3,1},{4,6},{6,4},{5,7},{7,5},{8,10},{10,8},{9,1... | collective-permute-start | bytes 1769480 | tf_op jit(solution)/shard_map/ppermute | solution.py:775
  25.2 10.0 %all-to-all-start.1 = ((bf16[4,32,576]{2,1,0:T(8,128)(2,1)}), bf16[4,32,576]{2,1,0:T(8,128)(2,1)}, u32[]{:S(2)}, u32[]{:S(2)}) async-start(bf16[4,32,576]{2,1,0:T(8,128)(2,1)} %bitcast.10), calls=%async_computation.1 | async-start | bytes 327680 | tf_op jit(solution)/shard_map/all_to_all | solution.py:785
  29.1 3.8 %collective-permute-start.8 = (s32[1]{0:T(128)}, s32[1]{0:T(128)}, u32[]{:S(2)}, u32[]{:S(2)}) collective-permute-start(s32[1]{0:T(128)} %get-tuple-element.163), channel_id=1, source_target_pairs={{0,16},{16,0},{1,17},{17,1},{2,18},{18,2},{3,19},{19,3},{4,20},{20... | collective-permute-start | bytes 20 | tf_op jit(solution)/shard_map/ppermute | solution.py:304
  34.2 25.2 %copy-start.13 = (bf16[8,32,1152]{2,1,0:T(8,128)(2,1)}, bf16[8,32,1152]{2,1,0:T(8,128)(2,1)S(1)}, u32[]{:S(2)}) copy-start(bf16[8,32,1152]{2,1,0:T(8,128)(2,1)S(1)} %collective-permute-done.7.refs_1_) | copy-start | bytes 1769476
  35.2 4.2 %collective-permute-start.10 = (bf16[1,8,32,1152]{3,2,1,0:T(8,128)(2,1)S(1)}, bf16[1,8,32,1152]{3,2,1,0:T(8,128)(2,1)S(1)}, u32[]{:S(2)}, u32[]{:S(2)}) collective-permute-start(bf16[1,8,32,1152]{3,2,1,0:T(8,128)(2,1)S(1)} %bitcast.16), channel_id=1, source_target_pairs={{0,1},{1,0},{2,3},{3,2},{4,5},{5,4},{6,7},{7,6},{8,9},{9,8},{10,11... | collective-permute-start | bytes 1769480 | tf_op jit(solution)/shard_map/ppermute | solution.py:762
  35.2 10.7 %collective-permute-start.11 = (bf16[8,32,1152]{2,1,0:T(8,128)(2,1)S(1)}, bf16[8,32,1152]{2,1,0:T(8,128)(2,1)}, u32[]{:S(2)}, u32[]{:S(2)}) collective-permute-start(bf16[8,32,1152]{2,1,0:T(8,128)(2,1)S(1)} %collective-permute-done.7.refs_1_), channel_id=1, source_target_pairs={{0,4},{5,1},{4,8},{9,5},{8,12},{13,9},{2,6},{7,3},{6,10},{11,7},{1... | collective-permute-start | bytes 1769480 | tf_op jit(solution)/shard_map/ppermute | solution.py:765
  39.4 1.1 copy-start.1
  40.5 0.7 copy-start.2
  45.5 29.9 %copy-start = (bf16[16,32,1152]{2,1,0:T(8,128)(2,1)}, bf16[16,32,1152]{2,1,0:T(8,128)(2,1)S(1)}, u32[]{:S(2)}) copy-start(bf16[16,32,1152]{2,1,0:T(8,128)(2,1)S(1)} %get-tuple-element.173.refs_7_) | copy-start | bytes 3538948
  45.9 21.4 %collective-permute-start.14 = (bf16[16,32,1152]{2,1,0:T(8,128)(2,1)S(1)}, bf16[16,32,1152]{2,1,0:T(8,128)(2,1)}, u32[]{:S(2)}, u32[]{:S(2)}) collective-permute-start(bf16[16,32,1152]{2,1,0:T(8,128)(2,1)S(1)} %get-tuple-element.173.refs_7_), channel_id=1, source_target_pairs={{0,4},{5,1},{4,8},{9,5},{8,12},{13,9},{2,6},{7,3},{6,10},{11,7},{1... | collective-permute-start | bytes 3538952 | tf_op jit(solution)/shard_map/ppermute | solution.py:765
  51.5 7.9 %collective-permute-start.9 = (bf16[8,32,1152]{2,1,0:T(8,128)(2,1)S(1)}, bf16[8,32,1152]{2,1,0:T(8,128)(2,1)}, u32[]{:S(2)}, u32[]{:S(2)}) collective-permute-start(bf16[8,32,1152]{2,1,0:T(8,128)(2,1)S(1)} %collective-permute-done.7.refs_1_), channel_id=1, source_target_pairs={{0,1},{1,0},{2,3},{3,2},{4,5},{5,4},{6,7},{7,6},{8,9},{9,8},{10,11... | collective-permute-start | bytes 1769480 | tf_op jit(solution)/shard_map/ppermute | solution.py:762
  51.5 7.9 %collective-permute-start.12 = (bf16[8,32,1152]{2,1,0:T(8,128)(2,1)}, bf16[8,32,1152]{2,1,0:T(8,128)(2,1)}, u32[]{:S(2)}, u32[]{:S(2)}) collective-permute-start(bf16[8,32,1152]{2,1,0:T(8,128)(2,1)} %collective-permute-done.11.refs_3_), channel_id=1, source_target_pairs={{0,1},{1,0},{2,3},{3,2},{4,5},{5,4},{6,7},{7,6},{8,9},{9,8},{10,11... | collective-permute-start | bytes 1769480 | tf_op jit(solution)/shard_map/ppermute | solution.py:762
  57.4 16.0 %collective-permute-start.13 = (bf16[8,32,1152]{2,1,0:T(8,128)(2,1)}, bf16[8,32,1152]{2,1,0:T(8,128)(2,1)S(1)}, u32[]{:S(2)}, u32[]{:S(2)}) collective-permute-start(bf16[8,32,1152]{2,1,0:T(8,128)(2,1)} %collective-permute-done.11.refs_3_), channel_id=1, source_target_pairs={{0,4},{5,1},{4,8},{9,5},{8,12},{13,9},{2,6},{7,3},{6,10},{11,7},{1... | collective-permute-start | bytes 1769480 | tf_op jit(solution)/shard_map/ppermute | solution.py:765
  67.3 8.0 %collective-permute-start.16 = (bf16[16,32,1152]{2,1,0:T(8,128)(2,1)}, bf16[16,32,1152]{2,1,0:T(8,128)(2,1)S(1)}, u32[]{:S(2)}, u32[]{:S(2)}) collective-permute-start(bf16[16,32,1152]{2,1,0:T(8,128)(2,1)} %collective-permute-done.14.refs_8_), channel_id=1, source_target_pairs={{0,1},{1,0},{2,3},{3,2},{4,5},{5,4},{6,7},{7,6},{8,9},{9,8},{10,11... | collective-permute-start | bytes 3538952 | tf_op jit(solution)/shard_map/ppermute | solution.py:762
  67.4 19.1 %collective-permute-start.17 = (bf16[16,32,1152]{2,1,0:T(8,128)(2,1)}, bf16[16,32,1152]{2,1,0:T(8,128)(2,1)}, u32[]{:S(2)}, u32[]{:S(2)}) collective-permute-start(bf16[16,32,1152]{2,1,0:T(8,128)(2,1)} %collective-permute-done.14.refs_8_), channel_id=1, source_target_pairs={{0,4},{5,1},{4,8},{9,5},{8,12},{13,9},{2,6},{7,3},{6,10},{11,7},{1... | collective-permute-start | bytes 3538952 | tf_op jit(solution)/shard_map/ppermute | solution.py:765
  73.3 2.0 %copy-start.14 = (bf16[8,32,1152]{2,1,0:T(8,128)(2,1)}, bf16[8,32,1152]{2,1,0:T(8,128)(2,1)S(1)}, u32[]{:S(2)}) copy-start(bf16[8,32,1152]{2,1,0:T(8,128)(2,1)S(1)} %collective-permute-done.13.refs_5_) | copy-start | bytes 1769476
  73.3 2.0 %collective-permute-start.15 = (bf16[8,32,1152]{2,1,0:T(8,128)(2,1)S(1)}, bf16[8,32,1152]{2,1,0:T(8,128)(2,1)S(1)}, u32[]{:S(2)}, u32[]{:S(2)}) collective-permute-start(bf16[8,32,1152]{2,1,0:T(8,128)(2,1)S(1)} %collective-permute-done.13.refs_5_), channel_id=1, source_target_pairs={{0,1},{1,0},{2,3},{3,2},{4,5},{5,4},{6,7},{7,6},{8,9},{9,8},{10,11... | collective-permute-start | bytes 1769480 | tf_op jit(solution)/shard_map/ppermute | solution.py:762
  75.3 0.8 copy-start.15
  75.3 1.3 %copy-start.5 = (bf16[16,32,1152]{2,1,0:T(8,128)(2,1)}, bf16[16,32,1152]{2,1,0:T(8,128)(2,1)S(1)}, u32[]{:S(2)}) copy-start(bf16[16,32,1152]{2,1,0:T(8,128)(2,1)S(1)} %collective-permute-done.16.refs_9_) | copy-start | bytes 3538948
  86.6 7.7 %collective-permute-start.19 = (bf16[16,32,1152]{2,1,0:T(8,128)(2,1)}, bf16[16,32,1152]{2,1,0:T(8,128)(2,1)}, u32[]{:S(2)}, u32[]{:S(2)}) collective-permute-start(bf16[16,32,1152]{2,1,0:T(8,128)(2,1)} %collective-permute-done.17.refs_7_), channel_id=1, source_target_pairs={{0,1},{1,0},{2,3},{3,2},{4,5},{5,4},{6,7},{7,6},{8,9},{9,8},{10,11... | collective-permute-start | bytes 3538952 | tf_op jit(solution)/shard_map/ppermute | solution.py:762
  86.6 18.1 %collective-permute-start.20 = (bf16[16,32,1152]{2,1,0:T(8,128)(2,1)}, bf16[16,32,1152]{2,1,0:T(8,128)(2,1)S(1)}, u32[]{:S(2)}, u32[]{:S(2)}) collective-permute-start(bf16[16,32,1152]{2,1,0:T(8,128)(2,1)} %collective-permute-done.17.refs_7_), channel_id=1, source_target_pairs={{0,4},{5,1},{4,8},{9,5},{8,12},{13,9},{2,6},{7,3},{6,10},{11,7},{1... | collective-permute-start | bytes 3538952 | tf_op jit(solution)/shard_map/ppermute | solution.py:765
  90.8 1.7 %collective-permute-start.18 = (bf16[128,576]{1,0:T(8,128)(2,1)}, bf16[128,576]{1,0:T(8,128)(2,1)S(1)}, u32[]{:S(2)}, u32[]{:S(2)}) collective-permute-start(bf16[128,576]{1,0:T(8,128)(2,1)} %bitcast.11), channel_id=1, source_target_pairs={{0,1},{1,0},{2,3},{3,2},{4,5},{5,4},{6,7},{7,6},{8,9},{9,8},{10,11... | collective-permute-start | bytes 442376 | tf_op jit(solution)/shard_map/ppermute | solution.py:762
  94.2 13.5 %copy-start.3 = (bf16[8,512,128]{2,1,0:T(8,128)(2,1)S(1)}, bf16[8,512,128]{2,1,0:T(8,128)(2,1)}, u32[]{:S(2)}) copy-start(bf16[8,512,128]{2,1,0:T(8,128)(2,1)} %param.18) | copy-start | bytes 3145732
  104.7 3.0 %collective-permute-start.21 = (bf16[16,32,1152]{2,1,0:T(8,128)(2,1)S(1)}, bf16[16,32,1152]{2,1,0:T(8,128)(2,1)}, u32[]{:S(2)}, u32[]{:S(2)}) collective-permute-start(bf16[16,32,1152]{2,1,0:T(8,128)(2,1)S(1)} %collective-permute-done.20), channel_id=1, source_target_pairs={{0,1},{1,0},{2,3},{3,2},{4,5},{5,4},{6,7},{7,6},{8,9},{9,8},{10,11... | collective-permute-start | bytes 3538952 | tf_op jit(solution)/shard_map/ppermute | solution.py:762
where the time goes:
time: 124 us; the launch traced here: 122 us
  Pallas kernels  53.6 us (43%)
  starting transfers between devices  39.9 us (32%)
  waiting for transfers between devices  15 us (12%)
  other arithmetic  5.63 us (5%)
  local copies, waits for them, and re-layouts  4.76 us (4%)
  between operations  2.94 us (2%)
    pallas_call x3, Pallas kernels, score_part(): pl.pallas_call(functools.partial(score_kernel, shape, base, len(sources),...  26.4 us
    ppermute x6, starting transfers between devices, stream(): return lax.ppermute(block, ('head', 'seq'), stream_route)  25.7 us
    pallas_call x1, Pallas kernels, finish(): pl.pallas_call(functools.partial(finish_kernel, shape, depth, n_blocks, l...  13.9 us
    all_to_all x1, starting transfers between devices, local(): lax.all_to_all(partial_value, 'head', split_axis=0, concat_axis=0, tiled=...  6.33 us
    pallas_call x1, Pallas kernels, pick_pages(): pl.pallas_call(functools.partial(pick_kernel, cap, 2 * pairs), out_shape=...  5 us
    ppermute x8, waiting for transfers between devices, swap(): return lax.ppermute(block, 'seq', swap_route)  4.79 us
    all_to_all x1, waiting for transfers between devices, local(): lax.all_to_all(partial_value, 'head', split_axis=0, concat_axis=0, tiled=...  4.57 us
    pallas_call x1, Pallas kernels, join_pages(): pl.pallas_call(functools.partial(join_kernel, chunk, cap), out_shape=tupl...  4.32 us
  transfers between devices with their start and end apart: 18, of which 8 were waited for; matrix products, arithmetic and copies ran while one was open for 6% of the time, Pallas kernels for 28%

commit v1 on v0

--- a/solution.py
+++ b/solution.py
@@ -775,25 +775,24 @@
         lax.ppermute(foreign[s - 1], "req", [(i, (i + s) % n_req) for i in range(n_req)])
         for s in range(1, n_req)
     ]
+    limits = plan_blocks(owner_rows, prefix_len, n_head, chunk, page_len)
+    partial_value, limits = lax.optimization_barrier((partial_value, limits))
     early_steps = [stream(first)]
-    share = half_len // n_head
-    partials = lax.all_to_all(partial_value, "head", split_axis=0, concat_axis=0, tiled=True)
-    summed = jnp.sum(partials.reshape(n_head, share, lat_width), axis=0)
-    share_t = seq_idx * half_len + head_idx * share + jnp.arange(share, dtype=jnp.int32)
-    latent = finish_latent(summed, my_prefix + share_t, share_t < live, kv_gain, latent_width)
-    copies = jnp.concatenate([latent] * n_head, axis=0)
-    fresh = lax.all_to_all(copies, "head", split_axis=0, concat_axis=0, tiled=True)
-    early_steps[0], fresh = lax.optimization_barrier((early_steps[0], fresh))
     for step in range(1, n_head - 1):
         early_steps.append(stream(early_steps[-1]))
     early_steps = [[block, None] for block in early_steps]
     for step in range(n_head - 2):
         early_steps[step][1] = swap(early_steps[step][0])
     mine = arrived[0][None] if n_req == 2 else jnp.stack(arrived)
-    most = over_groups(most)
-    mine, fresh, most = lax.optimization_barrier((mine, fresh, most))
+    mine, q_turned, limits = lax.optimization_barrier((mine, q_turned, limits))
     other = swap(mine)
     middle, late = join_pages(counts, rest, mine, other, chunk, cap, (2 * chunk, chunk))
+    share = half_len // n_head
+    partials = lax.all_to_all(partial_value, "head", split_axis=0, concat_axis=0, tiled=True)
+    partials, middle, most = lax.optimization_barrier((partials, middle, most))
+    summed = jnp.sum(partials.reshape(n_head, share, lat_width), axis=0)
+    share_t = seq_idx * half_len + head_idx * share + jnp.arange(share, dtype=jnp.int32)
+    latent = finish_latent(summed, my_prefix + share_t, share_t < live, kv_gain, latent_width)
 
     tile = 256 if rows % 256 == 0 and 256 % half_len == 0 else half_len
     shape = (tile, score_scale * math.log2(math.e), chunk, lat_width)
@@ -801,7 +800,6 @@
     near_state = ()
     extra = 4 + 1 + 2 * last
     total = 1 + 2 * (last + 1) + 2 + 4 * last + extra
-    limits = plan_blocks(owner_rows, prefix_len, n_head, chunk, page_len)
     n_blocks = 0
     state = None
 
@@ -838,6 +836,11 @@
             )
         received = tie(received)
         if step == 0:
+            most = over_groups(most)
+            received, latent = lax.optimization_barrier((received, latent))
+            copies = jnp.concatenate([latent] * n_head, axis=0)
+            fresh = lax.all_to_all(copies, "head", split_axis=0, concat_axis=0, tiled=True)
+            received, fresh, most = lax.optimization_barrier((received, fresh, most))
             early_steps[last][0] = tie(early_steps[last][0])
             early_steps[last][1] = swap(early_steps[last][0])
             opposite = swap(fresh)

time: 124 us -> 130 us (1.048)
  the two profiles are of different devices: /device:TPU:0 before, /device:TPU:27 now
where the time goes in v1:
time: 130 us; the launch traced here: 128 us
  Pallas kernels  56 us (43%)
  starting transfers between devices  43.3 us (33%)
  waiting for transfers between devices  14.5 us (11%)
  local copies, waits for them, and re-layouts  5.74 us (4%)
  other arithmetic  5.7 us (4%)
  between operations  3.03 us (2%)
    pallas_call x3, Pallas kernels, score_part(): pl.pallas_call(functools.partial(score_kernel, shape, base, len(sources),...  26.3 us
    ppermute x6, starting transfers between devices, stream(): return lax.ppermute(block, ('head', 'seq'), stream_route)  19.4 us
    pallas_call x1, Pallas kernels, finish(): pl.pallas_call(functools.partial(finish_kernel, shape, depth, n_blocks, l...  15.2 us
    ppermute x8, starting transfers between devices, swap(): return lax.ppermute(block, 'seq', swap_route)  10.8 us
    all_to_all x1, starting transfers between devices, local(): lax.all_to_all(copies, 'head', split_axis=0, concat_axis=0, tiled=True)  7.02 us
    ppermute x8, waiting for transfers between devices, swap(): return lax.ppermute(block, 'seq', swap_route)  5.29 us
    pallas_call x1, Pallas kernels, pick_pages(): pl.pallas_call(functools.partial(pick_kernel, cap, 2 * pairs), out_shape=...  4.98 us
    ppermute x1, waiting for transfers between devices, local(): lax.ppermute(foreign[s - 1], 'req', [(i, (i + s) % n_req) for i in range(...  4.68 us
  transfers between devices with their start and end apart: 18, of which 9 were waited for; matrix products, arithmetic and copies ran while one was open for 5% of the time, Pallas kernels for 28%

profile of v1, /device:TPU:27, one launch (start us, length us, event | category | flops | bytes accessed | tf_op | source)
XLA Modules:
  0.0 128.5 jit_solution(13363710747176571509)
XLA Ops:
  0.6 5.0 %pick_pages.1 = (s32[2]{0:T(128)}, s32[1]{0:T(128)}, s32[1]{0:T(128)}, s32[1]{0:T(128)}, bf16[8,32,1152]{2,1,0:T(8,128)(2,1)}, /*index=5*/bf16[8,32,1152]{2,1,0:...) custom-call(s32[2,64]{1,0:T(2,128)} %bitcast.26, s32[2,64]{1,0:T(2,128)} %slot_hbm.1, s32[2]{0:T(128)} %prefix_ref.1, ...), custom_call_target="tpu_custom_call" | custom-call | flops 1000000000 | bytes 6000000 | tf_op jit(solution)/shard_map/pick_pages/pallas_call | solution.py:163
  5.6 0.3 collective-permute-start.6
  5.9 2.9 %collective-permute-start.8 = (bf16[8,32,1152]{2,1,0:T(8,128)(2,1)}, bf16[8,32,1152]{2,1,0:T(8,128)(2,1)}, u32[]{:S(2)}, u32[]{:S(2)}) collective-permute-start(bf16[8,32,1152]{2,1,0:T(8,128)(2,1)} %get-tuple-element.176.refs_0_), channel_id=1, source_target_pairs={{0,4},{5,1},{4,8},{9,5},{8,12},{13,9},{2,6},{7,3},{6,10},{11,7},{1... | collective-permute-start | bytes 1769480 | tf_op jit(solution)/shard_map/ppermute | solution.py:765
  8.8 1.1 plan_blocks.1.limit_ref
  10.6 0.8 multiply_sine_fusion.1
  11.4 4.0 %turn_queries.1.queries_ref = bf16[640,1024]{1,0:T(8,128)(2,1)} custom-call(bf16[128,1536]{1,0:T(8,128)(2,1)} %bitcast.22, bf16[8,128,512]{2,1,0:T(8,128)(2,1)} %up_hbm.1, f32[32,128]{1,0:T(8,128)} %get-tuple-element.219.cosine_ref, f32[32,128]{1,0:T(8,128)} %get-tuple-element.218.sine_ref), custom_call_target="tpu_custom_call" | custom-call | flops 134217728 | bytes 3000000 | tf_op jit(solution)/shard_map/turn_queries/pallas_call | solution.py:346
  15.4 4.7 %collective-permute-done.6 = bf16[8,32,1152]{2,1,0:T(8,128)(2,1)S(1)} collective-permute-done((bf16[8,32,1152]{2,1,0:T(8,128)(2,1)}, bf16[8,32,1152]{2,1,0:T(8,128)(2,1)S(1)}, u32[]{:S(2)}, u32[]{:S(2)}) %collective-permute-start.6) | collective-permute-done | bytes 589856 | tf_op jit(solution)/shard_map/ppermute | solution.py:775
  20.1 1.6 %collective-permute-start.7 = (bf16[1,8,32,1152]{3,2,1,0:T(8,128)(2,1)S(1)}, bf16[1,8,32,1152]{3,2,1,0:T(8,128)(2,1)S(1)}, u32[]{:S(2)}, u32[]{:S(2)}) collective-permute-start(bf16[1,8,32,1152]{3,2,1,0:T(8,128)(2,1)S(1)} %bitcast.18), channel_id=1, source_target_pairs={{0,1},{1,0},{2,3},{3,2},{4,5},{5,4},{6,7},{7,6},{8,9},{9,8},{10,11... | collective-permute-start | bytes 1769480 | tf_op jit(solution)/shard_map/ppermute | solution.py:762
  21.6 0.0 collective-permute-done.8.refs_1_
  21.6 2.1 %collective-permute-start.9 = (bf16[8,32,1152]{2,1,0:T(8,128)(2,1)}, bf16[8,32,1152]{2,1,0:T(8,128)(2,1)S(1)}, u32[]{:S(2)}, u32[]{:S(2)}) collective-permute-start(bf16[8,32,1152]{2,1,0:T(8,128)(2,1)} %collective-permute-done.8.refs_1_), channel_id=1, source_target_pairs={{0,4},{5,1},{4,8},{9,5},{8,12},{13,9},{2,6},{7,3},{6,10},{11,7},{1... | collective-permute-start | bytes 1769480 | tf_op jit(solution)/shard_map/ppermute | solution.py:765
  23.7 4.5 %all-to-all-start = ((f32[4,32,576]{2,1,0:T(8,128)}), f32[4,32,576]{2,1,0:T(8,128)S(1)}, u32[]{:S(2)}, u32[]{:S(2)}) async-start(f32[4,32,576]{2,1,0:T(8,128)} %bitcast.23), calls=%async_computation | async-start | bytes 655360 | tf_op jit(solution)/shard_map/all_to_all | solution.py:791
  28.3 0.0 collective-permute-done.7.other_ref
  28.3 1.1 copy-done.1
  29.4 0.7 copy-done.2
  30.0 4.4 %join_pages.1 = (bf16[16,32,1152]{2,1,0:T(8,128)(2,1)S(1)}, bf16[8,32,1152]{2,1,0:T(8,128)(2,1)}) custom-call(s32[2]{0:T(128)S(1)} %copy-done.2, bf16[8,32,1152]{2,1,0:T(8,128)(2,1)S(1)} %copy-done.1, bf16[1,8,32,1152]{3,2,1,0:T(8,128)(2,1)S(1)} %bitcast.19, bf16[1,8,32,1152]{3,2,1,0:T(8,128)(2,1)S(1)} %collective-permute-done.7.other_ref), custom_call_target="tpu_custom_call" | custom-call | bytes 3000000 | tf_op jit(solution)/shard_map/join_pages/pallas_call | solution.py:231
  34.4 0.0 copy-start
  34.4 1.7 %all-to-all-done = f32[4,32,576]{2,1,0:T(8,128)S(1)} async-done(((f32[4,32,576]{2,1,0:T(8,128)}), f32[4,32,576]{2,1,0:T(8,128)S(1)}, u32[]{:S(2)}, u32[]{:S(2)}) %all-to-all-start) | async-done | bytes 294944 | tf_op jit(solution)/shard_map/all_to_all | solution.py:791
  36.1 0.0 collective-permute-done.9.refs_3_
  36.2 4.8 %collective-permute-start.10 = (bf16[16,32,1152]{2,1,0:T(8,128)(2,1)S(1)}, bf16[16,32,1152]{2,1,0:T(8,128)(2,1)}, u32[]{:S(2)}, u32[]{:S(2)}) collective-permute-start(bf16[16,32,1152]{2,1,0:T(8,128)(2,1)S(1)} %get-tuple-element.177.refs_7_), channel_id=1, source_target_pairs={{0,4},{5,1},{4,8},{9,5},{8,12},{13,9},{2,6},{7,3},{6,10},{11,7},{1... | collective-permute-start | bytes 3538952 | tf_op jit(solution)/shard_map/ppermute | solution.py:765
  41.0 0.7 add_convert_fusion
  41.7 0.6 fusion.8
  42.3 0.9 collective-permute-start.11
  43.2 0.1 collective-permute-start.12
  43.3 0.1 multiply_reduce_fusion
  43.4 0.1 fusion.5
  43.6 0.8 multiply_convert_fusion
  44.4 0.1 maximum_select_fusion.1
  44.5 0.6 collective-permute-done.11.refs_2_
  45.1 0.6 collective-permute-done.12.refs_4_
  45.7 0.0 copy-done.14
  45.7 0.2 copy-done.15
  45.9 0.8 copy-done.16
  46.7 8.7 %score_part.9 = (f32[26,512,1024]{2,1,0:T(8,128)}, bf16[26,512,512]{2,1,0:T(8,128)(2,1)}, f32[26,1024]{1,0:T(8,128)}, f32[1,1024]{1,0:T(1,128)}, f32[1,1024]{1,0:T(1,128)}) custom-call(s32[1,224]{1,0:T(1,128)S(1)} %plan_blocks.1.limit_ref, bf16[640,1024]{1,0:T(8,128)(2,1)} %turn_queries.1.queries_ref, bf16[8,32,1152]{2,1,0:T(8,128)(2,1)} %get-tuple-element.176.refs_0_, ...), custom_call_target="tpu_custom_call" | custom-call | flops 1310720 | bytes 100000 | tf_op jit(solution)/shard_map/score_part/pallas_call | solution.py:547
  55.4 0.0 collective-permute-done.10.refs_8_
  55.4 0.7 pad_maximum_fusion
  56.1 7.0 %all-to-all-start.1 = ((bf16[4,32,576]{2,1,0:T(8,128)(2,1)}), bf16[4,32,576]{2,1,0:T(8,128)(2,1)}, u32[]{:S(2)}, u32[]{:S(2)}) async-start(bf16[4,32,576]{2,1,0:T(8,128)(2,1)} %bitcast.15), calls=%async_computation.1 | async-start | bytes 327680 | tf_op jit(solution)/shard_map/all_to_all | solution.py:842
  63.1 1.2 collective-permute-start.13
  64.3 2.6 %collective-permute-start.14 = (bf16[8,32,1152]{2,1,0:T(8,128)(2,1)}, bf16[8,32,1152]{2,1,0:T(8,128)(2,1)S(1)}, u32[]{:S(2)}, u32[]{:S(2)}) collective-permute-start(bf16[8,32,1152]{2,1,0:T(8,128)(2,1)} %copy-done.14), channel_id=1, source_target_pairs={{0,4},{5,1},{4,8},{9,5},{8,12},{13,9},{2,6},{7,3},{6,10},{11,7},{1... | collective-permute-start | bytes 1769480 | tf_op jit(solution)/shard_map/ppermute | solution.py:765
  67.0 0.0 collective-permute-done.13
  68.3 0.0 all-to-all-done.1
  68.3 1.3 %collective-permute-start.16 = (bf16[16,32,1152]{2,1,0:T(8,128)(2,1)}, bf16[16,32,1152]{2,1,0:T(8,128)(2,1)S(1)}, u32[]{:S(2)}, u32[]{:S(2)}) collective-permute-start(bf16[16,32,1152]{2,1,0:T(8,128)(2,1)} %collective-permute-done.10.refs_8_), channel_id=1, source_target_pairs={{0,1},{1,0},{2,3},{3,2},{4,5},{5,4},{6,7},{7,6},{8,9},{9,8},{10,11... | collective-permute-start | bytes 3538952 | tf_op jit(solution)/shard_map/ppermute | solution.py:762
  69.6 4.4 %collective-permute-start.17 = (bf16[16,32,1152]{2,1,0:T(8,128)(2,1)}, bf16[16,32,1152]{2,1,0:T(8,128)(2,1)}, u32[]{:S(2)}, u32[]{:S(2)}) collective-permute-start(bf16[16,32,1152]{2,1,0:T(8,128)(2,1)} %collective-permute-done.10.refs_8_), channel_id=1, source_target_pairs={{0,4},{5,1},{4,8},{9,5},{8,12},{13,9},{2,6},{7,3},{6,10},{11,7},{1... | collective-permute-start | bytes 3538952 | tf_op jit(solution)/shard_map/ppermute | solution.py:765
  74.0 0.1 collective-permute-done.14.refs_5_
  74.0 4.0 %collective-permute-start.15 = (bf16[8,32,1152]{2,1,0:T(8,128)(2,1)S(1)}, bf16[8,32,1152]{2,1,0:T(8,128)(2,1)S(1)}, u32[]{:S(2)}, u32[]{:S(2)}) collective-permute-start(bf16[8,32,1152]{2,1,0:T(8,128)(2,1)S(1)} %collective-permute-done.14.refs_5_), channel_id=1, source_target_pairs={{0,1},{1,0},{2,3},{3,2},{4,5},{5,4},{6,7},{7,6},{8,9},{9,8},{10,11... | collective-permute-start | bytes 1769480 | tf_op jit(solution)/shard_map/ppermute | solution.py:762
  78.0 1.6 %collective-permute-done.15.refs_6_ = bf16[8,32,1152]{2,1,0:T(8,128)(2,1)S(1)} collective-permute-done((bf16[8,32,1152]{2,1,0:T(8,128)(2,1)S(1)}, bf16[8,32,1152]{2,1,0:T(8,128)(2,1)S(1)}, u32[]{:S(2)}, u32[]{:S(2)}) %collective-permute-start.15) | collective-permute-done | bytes 589856 | tf_op jit(solution)/shard_map/ppermute | solution.py:762
  79.6 0.0 collective-permute-done.16.refs_9_
  79.6 0.0 copy-done
  79.7 0.8 copy-done.18
  80.5 0.4 copy-done.6
  80.9 10.5 %score_part.10 = (f32[26,512,1024]{2,1,0:T(8,128)}, bf16[26,512,512]{2,1,0:T(8,128)(2,1)}, f32[26,1024]{1,0:T(8,128)}, f32[1,1024]{1,0:T(1,128)}, f32[1,1024]{1,0:T(1,128)}) custom-call(s32[1,224]{1,0:T(1,128)S(1)} %plan_blocks.1.limit_ref, bf16[640,1024]{1,0:T(8,128)(2,1)} %turn_queries.1.queries_ref, ...), custom_call_target="tpu_custom_call", output_to_operand_aliasing={{0}: (5, {}), {1}: (6, {})} | custom-call | flops 2097152 | bytes 100000 | tf_op jit(solution)/shard_map/score_part/pallas_call | solution.py:547
  91.3 0.0 collective-permute-done.17.refs_7_
  91.4 0.2 collective-permute-start.19
  91.6 2.6 %collective-permute-start.20 = (bf16[16,32,1152]{2,1,0:T(8,128)(2,1)}, bf16[16,32,1152]{2,1,0:T(8,128)(2,1)S(1)}, u32[]{:S(2)}, u32[]{:S(2)}) collective-permute-start(bf16[16,32,1152]{2,1,0:T(8,128)(2,1)} %collective-permute-done.17.refs_7_), channel_id=1, source_target_pairs={{0,4},{5,1},{4,8},{9,5},{8,12},{13,9},{2,6},{7,3},{6,10},{11,7},{1... | collective-permute-start | bytes 3538952 | tf_op jit(solution)/shard_map/ppermute | solution.py:765
  94.2 0.1 collective-permute-start.18
  94.3 1.6 %collective-permute-done.18 = bf16[128,576]{1,0:T(8,128)(2,1)S(1)} collective-permute-done((bf16[128,576]{1,0:T(8,128)(2,1)}, bf16[128,576]{1,0:T(8,128)(2,1)S(1)}, u32[]{:S(2)}, u32[]{:S(2)}) %collective-permute-start.18) | collective-permute-done | bytes 147488 | tf_op jit(solution)/shard_map/ppermute | solution.py:762
  95.8 1.8 %maximum_select_fusion.refs_6_ = bf16[256,576]{1,0:T(8,128)(2,1)} fusion(bf16[128,576]{1,0:T(8,128)(2,1)S(1)} %collective-permute-done.18, bf16[128,576]{1,0:T(8,128)(2,1)} %bitcast.16, pred[]{:T(512)S(6)} %eq.3), kind=kLoop, calls=%fused_computation | loop fusion | flops 1327104 | bytes 589825 | tf_op jit(solution)/shard_map/jit(_where)/select_n | solution.py:847
  97.7 0.0 collective-permute-done.19.refs_8_
  97.7 7.2 %score_part.11 = (f32[26,512,1024]{2,1,0:T(8,128)}, bf16[26,512,512]{2,1,0:T(8,128)(2,1)}, f32[26,1024]{1,0:T(8,128)}, f32[1,1024]{1,0:T(1,128)S(1)}, f32[1,1024...) custom-call(s32[1,224]{1,0:T(1,128)S(1)} %plan_blocks.1.limit_ref, ...), custom_call_target="tpu_custom_call", output_to_operand_aliasing={{0}: (5, {}), {1}: (6, {})} | custom-call | flops 1048576 | bytes 100000 | tf_op jit(solution)/shard_map/score_part/pallas_call | solution.py:547
  104.9 2.7 %collective-permute-done.20 = bf16[16,32,1152]{2,1,0:T(8,128)(2,1)S(1)} collective-permute-done((bf16[16,32,1152]{2,1,0:T(8,128)(2,1)}, bf16[16,32,1152]{2,1,0:T(8,128)(2,1)S(1)}, u32[]{:S(2)}, u32[]{:S(2)}) %collective-permute-start.20) | collective-permute-done | bytes 1179680 | tf_op jit(solution)/shard_map/ppermute | solution.py:765
  107.5 2.7 %collective-permute-start.21 = (bf16[16,32,1152]{2,1,0:T(8,128)(2,1)S(1)}, bf16[16,32,1152]{2,1,0:T(8,128)(2,1)}, u32[]{:S(2)}, u32[]{:S(2)}) collective-permute-start(bf16[16,32,1152]{2,1,0:T(8,128)(2,1)S(1)} %collective-permute-done.20), channel_id=1, source_target_pairs={{0,1},{1,0},{2,3},{3,2},{4,5},{5,4},{6,7},{7,6},{8,9},{9,8},{10,11... | collective-permute-start | bytes 3538952 | tf_op jit(solution)/shard_map/ppermute | solution.py:762
  110.2 1.8 %reshape.48 = bf16[1,2,36864]{2,1,0:T(2,128)(2,1)} reshape(bf16[128,576]{1,0:T(8,128)(2,1)} %bitcast.16) | data formatting | bytes 294912 | tf_op jit(solution)/shard_map/reshape | solution.py:884
  112.0 0.8 collective-permute-done.21
  112.8 15.4 %conditional.1 = (bf16[1,128,1024]{2,1,0:T(8,128)(2,1)}) conditional(s32[]{:T(128)} %convert_element_type.20, (s32[1,224]{1,0:T(1,128)S(1)}, bf16[640,1024]{1,0:T(8,128)(2,1)S(1)}, f32[26,1024]{1,0:T(8,128)}, f32[1,1024]{1,0:T(1,128)S(1)}, f32[1,1024]{1,0:T(1,128)S(1)}, /*index=5*/f32[256,1024]{1,0:T(8,128)}, bf16[512,256]{1,0:T(8,128)(2,1)}, ...), branch_computations={%region_2.3_spmd, %region_3.4_spmd} | conditional | flops 8055422976 | bytes 63854904 | solution.py:883
  112.8 15.2 %finish.2 = bf16[128,1024]{1,0:T(8,128)(2,1)} custom-call(s32[1,224]{1,0:T(1,128)S(1)} %get-tuple-element.62.limit_ref, bf16[640,1024]{1,0:T(8,128)(2,1)S(1)} %get-tuple-element.63.queries_ref, f32[26,1024]{1,0:T(8,128)} %get-tuple-element.64.marks, f32[1,1024]{1,0:T(1,128)S(1)} %get-tuple-element.65.sum_in, f32[1,1024]{1,0:T(1,128)S(1)} %get-tuple-element.66.high_in, ...), custom_call_target="tpu_custom_call" | custom-call | flops 6442450944 | bytes 30000000 | tf_op jit(solution)/shard_map/cond/branch_0_fun/finish/pallas_call | solution.py:683
  (17 shorter events, 0.1 us)
Async XLA Ops:
  5.6 14.5 %collective-permute-start.6 = (bf16[8,32,1152]{2,1,0:T(8,128)(2,1)}, bf16[8,32,1152]{2,1,0:T(8,128)(2,1)S(1)}, u32[]{:S(2)}, u32[]{:S(2)}) collective-permute-start(bf16[8,32,1152]{2,1,0:T(8,128)(2,1)} %bitcast.28), channel_id=1, source_target_pairs={{0,2},{2,0},{1,3},{3,1},{4,6},{6,4},{5,7},{7,5},{8,10},{10,8},{9,1... | collective-permute-start | bytes 1769480 | tf_op jit(solution)/shard_map/ppermute | solution.py:775
  5.9 15.7 %collective-permute-start.8 = (bf16[8,32,1152]{2,1,0:T(8,128)(2,1)}, bf16[8,32,1152]{2,1,0:T(8,128)(2,1)}, u32[]{:S(2)}, u32[]{:S(2)}) collective-permute-start(bf16[8,32,1152]{2,1,0:T(8,128)(2,1)} %get-tuple-element.176.refs_0_), channel_id=1, source_target_pairs={{0,4},{5,1},{4,8},{9,5},{8,12},{13,9},{2,6},{7,3},{6,10},{11,7},{1... | collective-permute-start | bytes 1769480 | tf_op jit(solution)/shard_map/ppermute | solution.py:765
  20.1 8.2 %collective-permute-start.7 = (bf16[1,8,32,1152]{3,2,1,0:T(8,128)(2,1)S(1)}, bf16[1,8,32,1152]{3,2,1,0:T(8,128)(2,1)S(1)}, u32[]{:S(2)}, u32[]{:S(2)}) collective-permute-start(bf16[1,8,32,1152]{3,2,1,0:T(8,128)(2,1)S(1)} %bitcast.18), channel_id=1, source_target_pairs={{0,1},{1,0},{2,3},{3,2},{4,5},{5,4},{6,7},{7,6},{8,9},{9,8},{10,11... | collective-permute-start | bytes 1769480 | tf_op jit(solution)/shard_map/ppermute | solution.py:762
  21.6 14.5 %collective-permute-start.9 = (bf16[8,32,1152]{2,1,0:T(8,128)(2,1)}, bf16[8,32,1152]{2,1,0:T(8,128)(2,1)S(1)}, u32[]{:S(2)}, u32[]{:S(2)}) collective-permute-start(bf16[8,32,1152]{2,1,0:T(8,128)(2,1)} %collective-permute-done.8.refs_1_), channel_id=1, source_target_pairs={{0,4},{5,1},{4,8},{9,5},{8,12},{13,9},{2,6},{7,3},{6,10},{11,7},{1... | collective-permute-start | bytes 1769480 | tf_op jit(solution)/shard_map/ppermute | solution.py:765
  23.7 12.4 %all-to-all-start = ((f32[4,32,576]{2,1,0:T(8,128)}), f32[4,32,576]{2,1,0:T(8,128)S(1)}, u32[]{:S(2)}, u32[]{:S(2)}) async-start(f32[4,32,576]{2,1,0:T(8,128)} %bitcast.23), calls=%async_computation | async-start | bytes 655360 | tf_op jit(solution)/shard_map/all_to_all | solution.py:791
  28.3 1.1 copy-start.1
  29.4 0.7 copy-start.2
  34.4 45.2 %copy-start = (bf16[16,32,1152]{2,1,0:T(8,128)(2,1)}, bf16[16,32,1152]{2,1,0:T(8,128)(2,1)S(1)}, u32[]{:S(2)}) copy-start(bf16[16,32,1152]{2,1,0:T(8,128)(2,1)S(1)} %get-tuple-element.177.refs_7_) | copy-start | bytes 3538948
  36.2 9.5 %copy-start.14 = (bf16[8,32,1152]{2,1,0:T(8,128)(2,1)}, bf16[8,32,1152]{2,1,0:T(8,128)(2,1)S(1)}, u32[]{:S(2)}) copy-start(bf16[8,32,1152]{2,1,0:T(8,128)(2,1)S(1)} %collective-permute-done.9.refs_3_) | copy-start | bytes 1769476
  36.2 19.2 %collective-permute-start.10 = (bf16[16,32,1152]{2,1,0:T(8,128)(2,1)S(1)}, bf16[16,32,1152]{2,1,0:T(8,128)(2,1)}, u32[]{:S(2)}, u32[]{:S(2)}) collective-permute-start(bf16[16,32,1152]{2,1,0:T(8,128)(2,1)S(1)} %get-tuple-element.177.refs_7_), channel_id=1, source_target_pairs={{0,4},{5,1},{4,8},{9,5},{8,12},{13,9},{2,6},{7,3},{6,10},{11,7},{1... | collective-permute-start | bytes 3538952 | tf_op jit(solution)/shard_map/ppermute | solution.py:765
  42.3 2.8 %collective-permute-start.11 = (bf16[8,32,1152]{2,1,0:T(8,128)(2,1)}, bf16[8,32,1152]{2,1,0:T(8,128)(2,1)S(1)}, u32[]{:S(2)}, u32[]{:S(2)}) collective-permute-start(bf16[8,32,1152]{2,1,0:T(8,128)(2,1)} %collective-permute-done.8.refs_1_), channel_id=1, source_target_pairs={{0,1},{1,0},{2,3},{3,2},{4,5},{5,4},{6,7},{7,6},{8,9},{9,8},{10,11... | collective-permute-start | bytes 1769480 | tf_op jit(solution)/shard_map/ppermute | solution.py:762
  43.2 2.5 %collective-permute-start.12 = (bf16[8,32,1152]{2,1,0:T(8,128)(2,1)S(1)}, bf16[8,32,1152]{2,1,0:T(8,128)(2,1)S(1)}, u32[]{:S(2)}, u32[]{:S(2)}) collective-permute-start(bf16[8,32,1152]{2,1,0:T(8,128)(2,1)S(1)} %collective-permute-done.9.refs_3_), channel_id=1, source_target_pairs={{0,1},{1,0},{2,3},{3,2},{4,5},{5,4},{6,7},{7,6},{8,9},{9,8},{10,11... | collective-permute-start | bytes 1769480 | tf_op jit(solution)/shard_map/ppermute | solution.py:762
  45.1 0.8 copy-start.15
  45.9 0.8 copy-start.16
  56.1 12.2 %all-to-all-start.1 = ((bf16[4,32,576]{2,1,0:T(8,128)(2,1)}), bf16[4,32,576]{2,1,0:T(8,128)(2,1)}, u32[]{:S(2)}, u32[]{:S(2)}) async-start(bf16[4,32,576]{2,1,0:T(8,128)(2,1)} %bitcast.15), calls=%async_computation.1 | async-start | bytes 327680 | tf_op jit(solution)/shard_map/all_to_all | solution.py:842
  63.1 3.9 %collective-permute-start.13 = (s32[1]{0:T(128)}, s32[1]{0:T(128)}, u32[]{:S(2)}, u32[]{:S(2)}) collective-permute-start(s32[1]{0:T(128)} %get-tuple-element.187), channel_id=1, source_target_pairs={{0,16},{16,0},{1,17},{17,1},{2,18},{18,2},{3,19},{19,3},{4,20},{20... | collective-permute-start | bytes 20 | tf_op jit(solution)/shard_map/ppermute | solution.py:304
  64.3 9.7 %collective-permute-start.14 = (bf16[8,32,1152]{2,1,0:T(8,128)(2,1)}, bf16[8,32,1152]{2,1,0:T(8,128)(2,1)S(1)}, u32[]{:S(2)}, u32[]{:S(2)}) collective-permute-start(bf16[8,32,1152]{2,1,0:T(8,128)(2,1)} %copy-done.14), channel_id=1, source_target_pairs={{0,4},{5,1},{4,8},{9,5},{8,12},{13,9},{2,6},{7,3},{6,10},{11,7},{1... | collective-permute-start | bytes 1769480 | tf_op jit(solution)/shard_map/ppermute | solution.py:765
  68.3 11.4 %collective-permute-start.16 = (bf16[16,32,1152]{2,1,0:T(8,128)(2,1)}, bf16[16,32,1152]{2,1,0:T(8,128)(2,1)S(1)}, u32[]{:S(2)}, u32[]{:S(2)}) collective-permute-start(bf16[16,32,1152]{2,1,0:T(8,128)(2,1)} %collective-permute-done.10.refs_8_), channel_id=1, source_target_pairs={{0,1},{1,0},{2,3},{3,2},{4,5},{5,4},{6,7},{7,6},{8,9},{9,8},{10,11... | collective-permute-start | bytes 3538952 | tf_op jit(solution)/shard_map/ppermute | solution.py:762
  69.6 21.8 %collective-permute-start.17 = (bf16[16,32,1152]{2,1,0:T(8,128)(2,1)}, bf16[16,32,1152]{2,1,0:T(8,128)(2,1)}, u32[]{:S(2)}, u32[]{:S(2)}) collective-permute-start(bf16[16,32,1152]{2,1,0:T(8,128)(2,1)} %collective-permute-done.10.refs_8_), channel_id=1, source_target_pairs={{0,4},{5,1},{4,8},{9,5},{8,12},{13,9},{2,6},{7,3},{6,10},{11,7},{1... | collective-permute-start | bytes 3538952 | tf_op jit(solution)/shard_map/ppermute | solution.py:765
  74.0 5.6 %copy-start.17 = (bf16[8,32,1152]{2,1,0:T(8,128)(2,1)}, bf16[8,32,1152]{2,1,0:T(8,128)(2,1)S(1)}, u32[]{:S(2)}) copy-start(bf16[8,32,1152]{2,1,0:T(8,128)(2,1)S(1)} %collective-permute-done.14.refs_5_) | copy-start | bytes 1769476
  74.0 5.6 %collective-permute-start.15 = (bf16[8,32,1152]{2,1,0:T(8,128)(2,1)S(1)}, bf16[8,32,1152]{2,1,0:T(8,128)(2,1)S(1)}, u32[]{:S(2)}, u32[]{:S(2)}) collective-permute-start(bf16[8,32,1152]{2,1,0:T(8,128)(2,1)S(1)} %collective-permute-done.14.refs_5_), channel_id=1, source_target_pairs={{0,1},{1,0},{2,3},{3,2},{4,5},{5,4},{6,7},{7,6},{8,9},{9,8},{10,11... | collective-permute-start | bytes 1769480 | tf_op jit(solution)/shard_map/ppermute | solution.py:762
  79.6 0.8 copy-start.18
  79.6 1.2 copy-start.6
  80.8 16.8 %copy-start.3 = (bf16[640,1024]{1,0:T(8,128)(2,1)S(1)}, bf16[640,1024]{1,0:T(8,128)(2,1)}, u32[]{:S(2)}) copy-start(bf16[640,1024]{1,0:T(8,128)(2,1)} %turn_queries.1.queries_ref) | copy-start | bytes 3932164
  91.4 6.3 %collective-permute-start.19 = (bf16[16,32,1152]{2,1,0:T(8,128)(2,1)}, bf16[16,32,1152]{2,1,0:T(8,128)(2,1)}, u32[]{:S(2)}, u32[]{:S(2)}) collective-permute-start(bf16[16,32,1152]{2,1,0:T(8,128)(2,1)} %collective-permute-done.17.refs_7_), channel_id=1, source_target_pairs={{0,1},{1,0},{2,3},{3,2},{4,5},{5,4},{6,7},{7,6},{8,9},{9,8},{10,11... | collective-permute-start | bytes 3538952 | tf_op jit(solution)/shard_map/ppermute | solution.py:762
  91.6 16.0 %collective-permute-start.20 = (bf16[16,32,1152]{2,1,0:T(8,128)(2,1)}, bf16[16,32,1152]{2,1,0:T(8,128)(2,1)S(1)}, u32[]{:S(2)}, u32[]{:S(2)}) collective-permute-start(bf16[16,32,1152]{2,1,0:T(8,128)(2,1)} %collective-permute-done.17.refs_7_), channel_id=1, source_target_pairs={{0,4},{5,1},{4,8},{9,5},{8,12},{13,9},{2,6},{7,3},{6,10},{11,7},{1... | collective-permute-start | bytes 3538952 | tf_op jit(solution)/shard_map/ppermute | solution.py:765
  94.2 1.7 %collective-permute-start.18 = (bf16[128,576]{1,0:T(8,128)(2,1)}, bf16[128,576]{1,0:T(8,128)(2,1)S(1)}, u32[]{:S(2)}, u32[]{:S(2)}) collective-permute-start(bf16[128,576]{1,0:T(8,128)(2,1)} %bitcast.16), channel_id=1, source_target_pairs={{0,1},{1,0},{2,3},{3,2},{4,5},{5,4},{6,7},{7,6},{8,9},{9,8},{10,11... | collective-permute-start | bytes 442376 | tf_op jit(solution)/shard_map/ppermute | solution.py:762
  97.7 15.2 %copy-start.4 = (bf16[8,512,128]{2,1,0:T(8,128)(2,1)S(1)}, bf16[8,512,128]{2,1,0:T(8,128)(2,1)}, u32[]{:S(2)}) copy-start(bf16[8,512,128]{2,1,0:T(8,128)(2,1)} %param.18) | copy-start | bytes 3145732
  107.5 5.3 %collective-permute-start.21 = (bf16[16,32,1152]{2,1,0:T(8,128)(2,1)S(1)}, bf16[16,32,1152]{2,1,0:T(8,128)(2,1)}, u32[]{:S(2)}, u32[]{:S(2)}) collective-permute-start(bf16[16,32,1152]{2,1,0:T(8,128)(2,1)S(1)} %collective-permute-done.20), channel_id=1, source_target_pairs={{0,1},{1,0},{2,3},{3,2},{4,5},{5,4},{6,7},{7,6},{8,9},{9,8},{10,11... | collective-permute-start | bytes 3538952 | tf_op jit(solution)/shard_map/ppermute | solution.py:762

commit v2 on v0

--- a/solution.py
+++ b/solution.py
@@ -362,10 +362,16 @@
 
 
 def score_block(keys, queries_ref, target, note, highest, weight_sum, tile, scale, bias=None):
-    rows = queries_ref.shape[1]
-    for start in range(0, rows, tile):
-        part = slice(start, start + tile)
-        scores = jnp.dot(keys[...], queries_ref[:, part], preferred_element_type=jnp.float32) * scale
+    parts = [slice(start, start + tile) for start in range(0, queries_ref.shape[1], tile)]
+
+    def product(part):
+        return jnp.dot(keys[...], queries_ref[:, part], preferred_element_type=jnp.float32)
+
+    following = product(parts[0])
+    for number, part in enumerate(parts):
+        scores = following * scale
+        if number + 1 < len(parts):
+            following = product(parts[number + 1])
         if bias is not None:
             scores = scores + bias
         old = highest[:, part]
@@ -625,14 +631,17 @@
     lax.fori_loop(0, n_last, one_score, 0)
 
     def add_block(weight_block, value_block, mark, begin=False):
-        for start in range(0, rows, tile):
-            part = slice(start, start + tile)
+        parts = [slice(start, start + tile) for start in range(0, rows, tile)]
+
+        def scaled(part):
             factor = jnp.exp2(mark[:, part] - highest[:, part]) / weight_sum[:, part]
-            added = jnp.dot(
-                value_block[...],
-                (weight_block[:, part] * factor).astype(jnp.bfloat16),
-                preferred_element_type=jnp.float32,
-            )
+            return (weight_block[:, part] * factor).astype(jnp.bfloat16)
+
+        following = scaled(parts[0])
+        for number, part in enumerate(parts):
+            added = jnp.dot(value_block[...], following, preferred_element_type=jnp.float32)
+            if number + 1 < len(parts):
+                following = scaled(parts[number + 1])
             total[:, part] = added if begin else total[:, part] + added
 
     add_block(near_weights, near_values, near_mark, begin=True)

time: 124 us -> 124 us (level); the launches traced: 122 us -> 123 us
    pallas_call x3, Pallas kernels: 26.4 us -> 25 us  [score_part(): pl.pallas_call(functools.partial(score_kernel, shape, base, len(sources),...]
    pallas_call x1, Pallas kernels: 13.9 us -> 15.2 us  [finish(): pl.pallas_call(functools.partial(finish_kernel, shape, depth, n_blocks, l...]
  transfers between devices with their start and end apart: 18 -> 18, of which waited for: 8 -> 9; matrix products, arithmetic and copies ran while one was open for 6% -> 6% of each run, Pallas kernels for 28% -> 27%
where the time goes in v2:
time: 124 us; the launch traced here: 123 us
  Pallas kernels  53.5 us (43%)
  starting transfers between devices  40.1 us (32%)
  waiting for transfers between devices  16.1 us (13%)
  other arithmetic  5.63 us (5%)
  local copies, waits for them, and re-layouts  4.76 us (4%)
  between operations  2.92 us (2%)
    ppermute x6, starting transfers between devices, stream(): return lax.ppermute(block, ('head', 'seq'), stream_route)  26 us
    pallas_call x3, Pallas kernels, score_part(): pl.pallas_call(functools.partial(score_kernel, shape, base, len(sources),...  25 us
    pallas_call x1, Pallas kernels, finish(): pl.pallas_call(functools.partial(finish_kernel, shape, depth, n_blocks, l...  15.2 us
    all_to_all x1, starting transfers between devices, local(): lax.all_to_all(partial_value, 'head', split_axis=0, concat_axis=0, tiled=...  6.33 us
    pallas_call x1, Pallas kernels, pick_pages(): pl.pallas_call(functools.partial(pick_kernel, cap, 2 * pairs), out_shape=...  5 us
    ppermute x8, waiting for transfers between devices, swap(): return lax.ppermute(block, 'seq', swap_route)  4.79 us
    all_to_all x1, waiting for transfers between devices, local(): lax.all_to_all(partial_value, 'head', split_axis=0, concat_axis=0, tiled=...  4.57 us
    pallas_call x1, Pallas kernels, join_pages(): pl.pallas_call(functools.partial(join_kernel, chunk, cap), out_shape=tupl...  4.32 us
  transfers between devices with their start and end apart: 18, of which 9 were waited for; matrix products, arithmetic and copies ran while one was open for 6% of the time, Pallas kernels for 27%

profile of v2, /device:TPU:0, one launch (start us, length us, event | category | flops | bytes accessed | tf_op | source)
XLA Modules:
  0.0 123.3 jit_solution(869214640935979923)
XLA Ops:
  0.6 5.0 %pick_pages.1 = (s32[2]{0:T(128)}, s32[1]{0:T(128)}, s32[1]{0:T(128)}, s32[1]{0:T(128)}, bf16[8,32,1152]{2,1,0:T(8,128)(2,1)}, /*index=5*/bf16[8,32,1152]{2,1,0:...) custom-call(s32[2,64]{1,0:T(2,128)} %bitcast.24, s32[2,64]{1,0:T(2,128)} %slot_hbm.1, s32[2]{0:T(128)} %prefix_ref.1, ...), custom_call_target="tpu_custom_call" | custom-call | flops 1000000000 | bytes 6000000 | tf_op jit(solution)/shard_map/pick_pages/pallas_call | solution.py:163
  5.6 6.3 %all-to-all-start = ((f32[4,32,576]{2,1,0:T(8,128)}), f32[4,32,576]{2,1,0:T(8,128)S(1)}, u32[]{:S(2)}, u32[]{:S(2)}) async-start(f32[4,32,576]{2,1,0:T(8,128)} %bitcast.21), calls=%async_computation | async-start | bytes 655360 | tf_op jit(solution)/shard_map/all_to_all | solution.py:789
  12.0 4.0 %collective-permute-start.7 = (bf16[8,32,1152]{2,1,0:T(8,128)(2,1)}, bf16[8,32,1152]{2,1,0:T(8,128)(2,1)S(1)}, u32[]{:S(2)}, u32[]{:S(2)}) collective-permute-start(bf16[8,32,1152]{2,1,0:T(8,128)(2,1)} %get-tuple-element.158.refs_0_), channel_id=1, source_target_pairs={{0,4},{5,1},{4,8},{9,5},{8,12},{13,9},{2,6},{7,3},{6,10},{11,7},{1... | collective-permute-start | bytes 1769480 | tf_op jit(solution)/shard_map/ppermute | solution.py:774
  15.9 1.6 %collective-permute-start.6 = (bf16[8,32,1152]{2,1,0:T(8,128)(2,1)}, bf16[8,32,1152]{2,1,0:T(8,128)(2,1)S(1)}, u32[]{:S(2)}, u32[]{:S(2)}) collective-permute-start(bf16[8,32,1152]{2,1,0:T(8,128)(2,1)} %bitcast.26), channel_id=1, source_target_pairs={{0,2},{2,0},{1,3},{3,1},{4,6},{6,4},{5,7},{7,5},{8,10},{10,8},{9,1... | collective-permute-start | bytes 1769480 | tf_op jit(solution)/shard_map/ppermute | solution.py:784
  17.5 0.6 add_convert_fusion.1
  18.1 0.6 fusion.8
  18.8 4.6 %all-to-all-done = f32[4,32,576]{2,1,0:T(8,128)S(1)} async-done(((f32[4,32,576]{2,1,0:T(8,128)}), f32[4,32,576]{2,1,0:T(8,128)S(1)}, u32[]{:S(2)}, u32[]{:S(2)}) %all-to-all-start) | async-done | bytes 294944 | tf_op jit(solution)/shard_map/all_to_all | solution.py:789
  23.4 0.1 multiply_reduce_fusion
  23.5 0.8 multiply_convert_fusion
  24.3 0.1 fusion.5
  24.4 0.1 maximum_select_fusion.1
  24.5 0.7 pad_maximum_fusion
  25.2 4.0 %all-to-all-start.1 = ((bf16[4,32,576]{2,1,0:T(8,128)(2,1)}), bf16[4,32,576]{2,1,0:T(8,128)(2,1)}, u32[]{:S(2)}, u32[]{:S(2)}) async-start(bf16[4,32,576]{2,1,0:T(8,128)(2,1)} %bitcast.10), calls=%async_computation.1 | async-start | bytes 327680 | tf_op jit(solution)/shard_map/all_to_all | solution.py:794
  29.1 1.6 %collective-permute-start.8 = (s32[1]{0:T(128)}, s32[1]{0:T(128)}, u32[]{:S(2)}, u32[]{:S(2)}) collective-permute-start(s32[1]{0:T(128)} %get-tuple-element.163), channel_id=1, source_target_pairs={{0,16},{16,0},{1,17},{17,1},{2,18},{18,2},{3,19},{19,3},{4,20},{20... | collective-permute-start | bytes 20 | tf_op jit(solution)/shard_map/ppermute | solution.py:304
  30.7 2.2 %collective-permute-done.8 = s32[1]{0:T(128)} collective-permute-done((s32[1]{0:T(128)}, s32[1]{0:T(128)}, u32[]{:S(2)}, u32[]{:S(2)}) %collective-permute-start.8) | collective-permute-done | bytes 36 | tf_op jit(solution)/shard_map/ppermute | solution.py:304
  34.2 0.0 collective-permute-done.7.refs_1_
  34.2 0.0 copy-start.13
  34.2 1.0 all-to-all-done.1
  35.2 0.0 collective-permute-done.6
  35.2 0.0 collective-permute-start.10
  35.2 4.2 %collective-permute-start.11 = (bf16[8,32,1152]{2,1,0:T(8,128)(2,1)S(1)}, bf16[8,32,1152]{2,1,0:T(8,128)(2,1)}, u32[]{:S(2)}, u32[]{:S(2)}) collective-permute-start(bf16[8,32,1152]{2,1,0:T(8,128)(2,1)S(1)} %collective-permute-done.7.refs_1_), channel_id=1, source_target_pairs={{0,4},{5,1},{4,8},{9,5},{8,12},{13,9},{2,6},{7,3},{6,10},{11,7},{1... | collective-permute-start | bytes 1769480 | tf_op jit(solution)/shard_map/ppermute | solution.py:774
  39.4 0.0 collective-permute-done.10.other_ref
  39.4 1.1 copy-done.1
  40.5 0.7 copy-done.2
  41.1 4.3 %join_pages.1 = (bf16[16,32,1152]{2,1,0:T(8,128)(2,1)S(1)}, bf16[8,32,1152]{2,1,0:T(8,128)(2,1)}) custom-call(s32[2]{0:T(128)S(1)} %copy-done.2, bf16[8,32,1152]{2,1,0:T(8,128)(2,1)S(1)} %copy-done.1, bf16[1,8,32,1152]{3,2,1,0:T(8,128)(2,1)S(1)} %bitcast.17, bf16[1,8,32,1152]{3,2,1,0:T(8,128)(2,1)S(1)} %collective-permute-done.10.other_ref), custom_call_target="tpu_custom_call" | custom-call | bytes 3000000 | tf_op jit(solution)/shard_map/join_pages/pallas_call | solution.py:231
  45.5 0.0 copy-start
  45.5 0.5 collective-permute-done.11.refs_3_
  45.9 5.5 %collective-permute-start.14 = (bf16[16,32,1152]{2,1,0:T(8,128)(2,1)S(1)}, bf16[16,32,1152]{2,1,0:T(8,128)(2,1)}, u32[]{:S(2)}, u32[]{:S(2)}) collective-permute-start(bf16[16,32,1152]{2,1,0:T(8,128)(2,1)S(1)} %get-tuple-element.173.refs_7_), channel_id=1, source_target_pairs={{0,4},{5,1},{4,8},{9,5},{8,12},{13,9},{2,6},{7,3},{6,10},{11,7},{1... | collective-permute-start | bytes 3538952 | tf_op jit(solution)/shard_map/ppermute | solution.py:774
  51.5 0.0 collective-permute-start.9
  51.5 0.5 collective-permute-start.12
  52.0 1.1 plan_blocks.1.limit_ref
  53.7 0.8 multiply_sine_fusion
  54.4 2.9 %turn_queries.1.queries_ref = bf16[640,1024]{1,0:T(8,128)(2,1)S(1)} custom-call(bf16[128,1536]{1,0:T(8,128)(2,1)} %bitcast.20, bf16[8,128,512]{2,1,0:T(8,128)(2,1)} %up_hbm.1, f32[32,128]{1,0:T(8,128)} %get-tuple-element.203.cosine_ref, f32[32,128]{1,0:T(8,128)} %get-tuple-element.202.sine_ref), custom_call_target="tpu_custom_call" | custom-call | flops 134217728 | bytes 3000000 | tf_op jit(solution)/shard_map/turn_queries/pallas_call | solution.py:346
  57.4 2.0 %collective-permute-start.13 = (bf16[8,32,1152]{2,1,0:T(8,128)(2,1)}, bf16[8,32,1152]{2,1,0:T(8,128)(2,1)S(1)}, u32[]{:S(2)}, u32[]{:S(2)}) collective-permute-start(bf16[8,32,1152]{2,1,0:T(8,128)(2,1)} %collective-permute-done.11.refs_3_), channel_id=1, source_target_pairs={{0,4},{5,1},{4,8},{9,5},{8,12},{13,9},{2,6},{7,3},{6,10},{11,7},{1... | collective-permute-start | bytes 1769480 | tf_op jit(solution)/shard_map/ppermute | solution.py:774
  59.4 0.0 collective-permute-done.9.refs_2_
  59.4 0.0 collective-permute-done.12.refs_4_
  59.4 0.0 copy-done.13
  59.4 7.9 %score_part.9 = (f32[26,512,1024]{2,1,0:T(8,128)}, bf16[26,512,512]{2,1,0:T(8,128)(2,1)}, f32[26,1024]{1,0:T(8,128)}, f32[1,1024]{1,0:T(1,128)}, f32[1,1024]{1,0:T(1,128)}) custom-call(s32[1,224]{1,0:T(1,128)S(1)} %plan_blocks.1.limit_ref, bf16[640,1024]{1,0:T(8,128)(2,1)S(1)} %turn_queries.1.queries_ref, bf16[8,32,1152]{2,1,0:T(8,128)(2,1)} %get-tuple-element.158.refs_0_, ...), custom_call_target="tpu_custom_call" | custom-call | flops 1310720 | bytes 100000 | tf_op jit(solution)/shard_map/score_part/pallas_call | solution.py:553
  67.3 0.0 collective-permute-done.14.refs_8_
  67.3 0.1 collective-permute-start.16
  67.4 5.9 %collective-permute-start.17 = (bf16[16,32,1152]{2,1,0:T(8,128)(2,1)}, bf16[16,32,1152]{2,1,0:T(8,128)(2,1)}, u32[]{:S(2)}, u32[]{:S(2)}) collective-permute-start(bf16[16,32,1152]{2,1,0:T(8,128)(2,1)} %collective-permute-done.14.refs_8_), channel_id=1, source_target_pairs={{0,4},{5,1},{4,8},{9,5},{8,12},{13,9},{2,6},{7,3},{6,10},{11,7},{1... | collective-permute-start | bytes 3538952 | tf_op jit(solution)/shard_map/ppermute | solution.py:774
  73.3 0.0 collective-permute-done.13.refs_5_
  73.3 0.0 collective-permute-start.15
  73.3 2.0 %collective-permute-done.15.refs_6_ = bf16[8,32,1152]{2,1,0:T(8,128)(2,1)S(1)} collective-permute-done((bf16[8,32,1152]{2,1,0:T(8,128)(2,1)S(1)}, bf16[8,32,1152]{2,1,0:T(8,128)(2,1)S(1)}, u32[]{:S(2)}, u32[]{:S(2)}) %collective-permute-start.15) | collective-permute-done | bytes 589856 | tf_op jit(solution)/shard_map/ppermute | solution.py:771
  75.3 0.0 collective-permute-done.16.refs_9_
  75.3 0.0 copy-done
  75.3 0.0 copy-done.14
  75.3 0.8 copy-done.15
  76.1 0.4 copy-done.5
  76.6 8.6 %score_part.10 = (f32[26,512,1024]{2,1,0:T(8,128)}, bf16[26,512,512]{2,1,0:T(8,128)(2,1)}, f32[26,1024]{1,0:T(8,128)}, f32[1,1024]{1,0:T(1,128)}, f32[1,1024]{1,0:T(1,128)}) custom-call(s32[1,224]{1,0:T(1,128)S(1)} %plan_blocks.1.limit_ref, bf16[640,1024]{1,0:T(8,128)(2,1)S(1)} %turn_queries.1.queries_ref, ...), custom_call_target="tpu_custom_call", output_to_operand_aliasing={{0}: (5, {}), {1}: (6, {})} | custom-call | flops 2097152 | bytes 100000 | tf_op jit(solution)/shard_map/score_part/pallas_call | solution.py:553
  85.2 1.1 collective-permute-done.17.refs_7_
  86.3 0.0 collective-permute-start.19
  86.3 4.4 %collective-permute-start.20 = (bf16[16,32,1152]{2,1,0:T(8,128)(2,1)}, bf16[16,32,1152]{2,1,0:T(8,128)(2,1)S(1)}, u32[]{:S(2)}, u32[]{:S(2)}) collective-permute-start(bf16[16,32,1152]{2,1,0:T(8,128)(2,1)} %collective-permute-done.17.refs_7_), channel_id=1, source_target_pairs={{0,4},{5,1},{4,8},{9,5},{8,12},{13,9},{2,6},{7,3},{6,10},{11,7},{1... | collective-permute-start | bytes 3538952 | tf_op jit(solution)/shard_map/ppermute | solution.py:774
  90.7 0.1 collective-permute-start.18
  90.8 1.6 %collective-permute-done.18 = bf16[128,576]{1,0:T(8,128)(2,1)S(1)} collective-permute-done((bf16[128,576]{1,0:T(8,128)(2,1)}, bf16[128,576]{1,0:T(8,128)(2,1)S(1)}, u32[]{:S(2)}, u32[]{:S(2)}) %collective-permute-start.18) | collective-permute-done | bytes 147488 | tf_op jit(solution)/shard_map/ppermute | solution.py:771
  92.4 1.8 %maximum_select_fusion.refs_6_ = bf16[256,576]{1,0:T(8,128)(2,1)} fusion(bf16[128,576]{1,0:T(8,128)(2,1)S(1)} %collective-permute-done.18, bf16[128,576]{1,0:T(8,128)(2,1)} %bitcast.11, pred[]{:T(512)S(6)} %eq.3), kind=kLoop, calls=%fused_computation | loop fusion | flops 1327104 | bytes 589825 | tf_op jit(solution)/shard_map/jit(_where)/select_n | solution.py:853
  94.2 0.0 collective-permute-done.19.refs_8_
  94.2 8.5 %score_part.11 = (f32[26,512,1024]{2,1,0:T(8,128)}, bf16[26,512,512]{2,1,0:T(8,128)(2,1)}, f32[26,1024]{1,0:T(8,128)}, f32[1,1024]{1,0:T(1,128)S(1)}, f32[1,1024...) custom-call(s32[1,224]{1,0:T(1,128)S(1)} %plan_blocks.1.limit_ref, ...), custom_call_target="tpu_custom_call", output_to_operand_aliasing={{0}: (5, {}), {1}: (6, {})} | custom-call | flops 1048576 | bytes 100000 | tf_op jit(solution)/shard_map/score_part/pallas_call | solution.py:553
  102.7 1.9 %collective-permute-done.20 = bf16[16,32,1152]{2,1,0:T(8,128)(2,1)S(1)} collective-permute-done((bf16[16,32,1152]{2,1,0:T(8,128)(2,1)}, bf16[16,32,1152]{2,1,0:T(8,128)(2,1)S(1)}, u32[]{:S(2)}, u32[]{:S(2)}) %collective-permute-start.20) | collective-permute-done | bytes 1179680 | tf_op jit(solution)/shard_map/ppermute | solution.py:774
  104.7 0.0 collective-permute-start.21
  104.7 1.8 %reshape.46 = bf16[1,2,36864]{2,1,0:T(2,128)(2,1)} reshape(bf16[128,576]{1,0:T(8,128)(2,1)} %bitcast.11) | data formatting | bytes 294912 | tf_op jit(solution)/shard_map/reshape | solution.py:890
  106.5 1.2 collective-permute-done.21
  107.7 15.4 %conditional.1 = (bf16[1,128,1024]{2,1,0:T(8,128)(2,1)}) conditional(s32[]{:T(128)} %convert_element_type.19, (s32[1,224]{1,0:T(1,128)S(1)}, bf16[640,1024]{1,0:T(8,128)(2,1)S(1)}, f32[26,1024]{1,0:T(8,128)}, f32[1,1024]{1,0:T(1,128)S(1)}, f32[1,1024]{1,0:T(1,128)S(1)}, /*index=5*/f32[256,1024]{1,0:T(8,128)}, bf16[512,256]{1,0:T(8,128)(2,1)}, ...), branch_computations={%region_2.3_spmd, %region_3.4_spmd} | conditional | flops 8055422976 | bytes 63854904 | solution.py:889
  107.7 15.2 %finish.2 = bf16[128,1024]{1,0:T(8,128)(2,1)} custom-call(s32[1,224]{1,0:T(1,128)S(1)} %get-tuple-element.62.limit_ref, bf16[640,1024]{1,0:T(8,128)(2,1)S(1)} %get-tuple-element.63.queries_ref, f32[26,1024]{1,0:T(8,128)} %get-tuple-element.64.marks, f32[1,1024]{1,0:T(1,128)S(1)} %get-tuple-element.65.sum_in, f32[1,1024]{1,0:T(1,128)S(1)} %get-tuple-element.66.high_in, ...), custom_call_target="tpu_custom_call" | custom-call | flops 6442450944 | bytes 30000000 | tf_op jit(solution)/shard_map/cond/branch_0_fun/finish/pallas_call | solution.py:692
  (11 shorter events, 0.1 us)
Async XLA Ops:
  5.6 17.7 %all-to-all-start = ((f32[4,32,576]{2,1,0:T(8,128)}), f32[4,32,576]{2,1,0:T(8,128)S(1)}, u32[]{:S(2)}, u32[]{:S(2)}) async-start(f32[4,32,576]{2,1,0:T(8,128)} %bitcast.21), calls=%async_computation | async-start | bytes 655360 | tf_op jit(solution)/shard_map/all_to_all | solution.py:789
  12.0 22.2 %collective-permute-start.7 = (bf16[8,32,1152]{2,1,0:T(8,128)(2,1)}, bf16[8,32,1152]{2,1,0:T(8,128)(2,1)S(1)}, u32[]{:S(2)}, u32[]{:S(2)}) collective-permute-start(bf16[8,32,1152]{2,1,0:T(8,128)(2,1)} %get-tuple-element.158.refs_0_), channel_id=1, source_target_pairs={{0,4},{5,1},{4,8},{9,5},{8,12},{13,9},{2,6},{7,3},{6,10},{11,7},{1... | collective-permute-start | bytes 1769480 | tf_op jit(solution)/shard_map/ppermute | solution.py:774
  15.9 19.3 %collective-permute-start.6 = (bf16[8,32,1152]{2,1,0:T(8,128)(2,1)}, bf16[8,32,1152]{2,1,0:T(8,128)(2,1)S(1)}, u32[]{:S(2)}, u32[]{:S(2)}) collective-permute-start(bf16[8,32,1152]{2,1,0:T(8,128)(2,1)} %bitcast.26), channel_id=1, source_target_pairs={{0,2},{2,0},{1,3},{3,1},{4,6},{6,4},{5,7},{7,5},{8,10},{10,8},{9,1... | collective-permute-start | bytes 1769480 | tf_op jit(solution)/shard_map/ppermute | solution.py:784
  25.2 10.0 %all-to-all-start.1 = ((bf16[4,32,576]{2,1,0:T(8,128)(2,1)}), bf16[4,32,576]{2,1,0:T(8,128)(2,1)}, u32[]{:S(2)}, u32[]{:S(2)}) async-start(bf16[4,32,576]{2,1,0:T(8,128)(2,1)} %bitcast.10), calls=%async_computation.1 | async-start | bytes 327680 | tf_op jit(solution)/shard_map/all_to_all | solution.py:794
  29.1 3.8 %collective-permute-start.8 = (s32[1]{0:T(128)}, s32[1]{0:T(128)}, u32[]{:S(2)}, u32[]{:S(2)}) collective-permute-start(s32[1]{0:T(128)} %get-tuple-element.163), channel_id=1, source_target_pairs={{0,16},{16,0},{1,17},{17,1},{2,18},{18,2},{3,19},{19,3},{4,20},{20... | collective-permute-start | bytes 20 | tf_op jit(solution)/shard_map/ppermute | solution.py:304
  34.2 25.2 %copy-start.13 = (bf16[8,32,1152]{2,1,0:T(8,128)(2,1)}, bf16[8,32,1152]{2,1,0:T(8,128)(2,1)S(1)}, u32[]{:S(2)}) copy-start(bf16[8,32,1152]{2,1,0:T(8,128)(2,1)S(1)} %collective-permute-done.7.refs_1_) | copy-start | bytes 1769476
  35.2 4.2 %collective-permute-start.10 = (bf16[1,8,32,1152]{3,2,1,0:T(8,128)(2,1)S(1)}, bf16[1,8,32,1152]{3,2,1,0:T(8,128)(2,1)S(1)}, u32[]{:S(2)}, u32[]{:S(2)}) collective-permute-start(bf16[1,8,32,1152]{3,2,1,0:T(8,128)(2,1)S(1)} %bitcast.16), channel_id=1, source_target_pairs={{0,1},{1,0},{2,3},{3,2},{4,5},{5,4},{6,7},{7,6},{8,9},{9,8},{10,11... | collective-permute-start | bytes 1769480 | tf_op jit(solution)/shard_map/ppermute | solution.py:771
  35.2 10.7 %collective-permute-start.11 = (bf16[8,32,1152]{2,1,0:T(8,128)(2,1)S(1)}, bf16[8,32,1152]{2,1,0:T(8,128)(2,1)}, u32[]{:S(2)}, u32[]{:S(2)}) collective-permute-start(bf16[8,32,1152]{2,1,0:T(8,128)(2,1)S(1)} %collective-permute-done.7.refs_1_), channel_id=1, source_target_pairs={{0,4},{5,1},{4,8},{9,5},{8,12},{13,9},{2,6},{7,3},{6,10},{11,7},{1... | collective-permute-start | bytes 1769480 | tf_op jit(solution)/shard_map/ppermute | solution.py:774
  39.4 1.1 copy-start.1
  40.5 0.7 copy-start.2
  45.5 29.8 %copy-start = (bf16[16,32,1152]{2,1,0:T(8,128)(2,1)}, bf16[16,32,1152]{2,1,0:T(8,128)(2,1)S(1)}, u32[]{:S(2)}) copy-start(bf16[16,32,1152]{2,1,0:T(8,128)(2,1)S(1)} %get-tuple-element.173.refs_7_) | copy-start | bytes 3538948
  45.9 21.4 %collective-permute-start.14 = (bf16[16,32,1152]{2,1,0:T(8,128)(2,1)S(1)}, bf16[16,32,1152]{2,1,0:T(8,128)(2,1)}, u32[]{:S(2)}, u32[]{:S(2)}) collective-permute-start(bf16[16,32,1152]{2,1,0:T(8,128)(2,1)S(1)} %get-tuple-element.173.refs_7_), channel_id=1, source_target_pairs={{0,4},{5,1},{4,8},{9,5},{8,12},{13,9},{2,6},{7,3},{6,10},{11,7},{1... | collective-permute-start | bytes 3538952 | tf_op jit(solution)/shard_map/ppermute | solution.py:774
  51.5 7.9 %collective-permute-start.9 = (bf16[8,32,1152]{2,1,0:T(8,128)(2,1)S(1)}, bf16[8,32,1152]{2,1,0:T(8,128)(2,1)}, u32[]{:S(2)}, u32[]{:S(2)}) collective-permute-start(bf16[8,32,1152]{2,1,0:T(8,128)(2,1)S(1)} %collective-permute-done.7.refs_1_), channel_id=1, source_target_pairs={{0,1},{1,0},{2,3},{3,2},{4,5},{5,4},{6,7},{7,6},{8,9},{9,8},{10,11... | collective-permute-start | bytes 1769480 | tf_op jit(solution)/shard_map/ppermute | solution.py:771
  51.5 7.9 %collective-permute-start.12 = (bf16[8,32,1152]{2,1,0:T(8,128)(2,1)}, bf16[8,32,1152]{2,1,0:T(8,128)(2,1)}, u32[]{:S(2)}, u32[]{:S(2)}) collective-permute-start(bf16[8,32,1152]{2,1,0:T(8,128)(2,1)} %collective-permute-done.11.refs_3_), channel_id=1, source_target_pairs={{0,1},{1,0},{2,3},{3,2},{4,5},{5,4},{6,7},{7,6},{8,9},{9,8},{10,11... | collective-permute-start | bytes 1769480 | tf_op jit(solution)/shard_map/ppermute | solution.py:771
  57.4 15.9 %collective-permute-start.13 = (bf16[8,32,1152]{2,1,0:T(8,128)(2,1)}, bf16[8,32,1152]{2,1,0:T(8,128)(2,1)S(1)}, u32[]{:S(2)}, u32[]{:S(2)}) collective-permute-start(bf16[8,32,1152]{2,1,0:T(8,128)(2,1)} %collective-permute-done.11.refs_3_), channel_id=1, source_target_pairs={{0,4},{5,1},{4,8},{9,5},{8,12},{13,9},{2,6},{7,3},{6,10},{11,7},{1... | collective-permute-start | bytes 1769480 | tf_op jit(solution)/shard_map/ppermute | solution.py:774
  67.3 8.0 %collective-permute-start.16 = (bf16[16,32,1152]{2,1,0:T(8,128)(2,1)}, bf16[16,32,1152]{2,1,0:T(8,128)(2,1)S(1)}, u32[]{:S(2)}, u32[]{:S(2)}) collective-permute-start(bf16[16,32,1152]{2,1,0:T(8,128)(2,1)} %collective-permute-done.14.refs_8_), channel_id=1, source_target_pairs={{0,1},{1,0},{2,3},{3,2},{4,5},{5,4},{6,7},{7,6},{8,9},{9,8},{10,11... | collective-permute-start | bytes 3538952 | tf_op jit(solution)/shard_map/ppermute | solution.py:771
  67.4 18.9 %collective-permute-start.17 = (bf16[16,32,1152]{2,1,0:T(8,128)(2,1)}, bf16[16,32,1152]{2,1,0:T(8,128)(2,1)}, u32[]{:S(2)}, u32[]{:S(2)}) collective-permute-start(bf16[16,32,1152]{2,1,0:T(8,128)(2,1)} %collective-permute-done.14.refs_8_), channel_id=1, source_target_pairs={{0,4},{5,1},{4,8},{9,5},{8,12},{13,9},{2,6},{7,3},{6,10},{11,7},{1... | collective-permute-start | bytes 3538952 | tf_op jit(solution)/shard_map/ppermute | solution.py:774
  73.3 2.0 %copy-start.14 = (bf16[8,32,1152]{2,1,0:T(8,128)(2,1)}, bf16[8,32,1152]{2,1,0:T(8,128)(2,1)S(1)}, u32[]{:S(2)}) copy-start(bf16[8,32,1152]{2,1,0:T(8,128)(2,1)S(1)} %collective-permute-done.13.refs_5_) | copy-start | bytes 1769476
  73.3 2.0 %collective-permute-start.15 = (bf16[8,32,1152]{2,1,0:T(8,128)(2,1)S(1)}, bf16[8,32,1152]{2,1,0:T(8,128)(2,1)S(1)}, u32[]{:S(2)}, u32[]{:S(2)}) collective-permute-start(bf16[8,32,1152]{2,1,0:T(8,128)(2,1)S(1)} %collective-permute-done.13.refs_5_), channel_id=1, source_target_pairs={{0,1},{1,0},{2,3},{3,2},{4,5},{5,4},{6,7},{7,6},{8,9},{9,8},{10,11... | collective-permute-start | bytes 1769480 | tf_op jit(solution)/shard_map/ppermute | solution.py:771
  75.3 0.8 copy-start.15
  75.3 1.3 %copy-start.5 = (bf16[16,32,1152]{2,1,0:T(8,128)(2,1)}, bf16[16,32,1152]{2,1,0:T(8,128)(2,1)S(1)}, u32[]{:S(2)}) copy-start(bf16[16,32,1152]{2,1,0:T(8,128)(2,1)S(1)} %collective-permute-done.16.refs_9_) | copy-start | bytes 3538948
  86.3 7.9 %collective-permute-start.19 = (bf16[16,32,1152]{2,1,0:T(8,128)(2,1)}, bf16[16,32,1152]{2,1,0:T(8,128)(2,1)}, u32[]{:S(2)}, u32[]{:S(2)}) collective-permute-start(bf16[16,32,1152]{2,1,0:T(8,128)(2,1)} %collective-permute-done.17.refs_7_), channel_id=1, source_target_pairs={{0,1},{1,0},{2,3},{3,2},{4,5},{5,4},{6,7},{7,6},{8,9},{9,8},{10,11... | collective-permute-start | bytes 3538952 | tf_op jit(solution)/shard_map/ppermute | solution.py:771
  86.3 18.4 %collective-permute-start.20 = (bf16[16,32,1152]{2,1,0:T(8,128)(2,1)}, bf16[16,32,1152]{2,1,0:T(8,128)(2,1)S(1)}, u32[]{:S(2)}, u32[]{:S(2)}) collective-permute-start(bf16[16,32,1152]{2,1,0:T(8,128)(2,1)} %collective-permute-done.17.refs_7_), channel_id=1, source_target_pairs={{0,4},{5,1},{4,8},{9,5},{8,12},{13,9},{2,6},{7,3},{6,10},{11,7},{1... | collective-permute-start | bytes 3538952 | tf_op jit(solution)/shard_map/ppermute | solution.py:774
  90.7 1.7 %collective-permute-start.18 = (bf16[128,576]{1,0:T(8,128)(2,1)}, bf16[128,576]{1,0:T(8,128)(2,1)S(1)}, u32[]{:S(2)}, u32[]{:S(2)}) collective-permute-start(bf16[128,576]{1,0:T(8,128)(2,1)} %bitcast.11), channel_id=1, source_target_pairs={{0,1},{1,0},{2,3},{3,2},{4,5},{5,4},{6,7},{7,6},{8,9},{9,8},{10,11... | collective-permute-start | bytes 442376 | tf_op jit(solution)/shard_map/ppermute | solution.py:771
  94.2 13.5 %copy-start.3 = (bf16[8,512,128]{2,1,0:T(8,128)(2,1)S(1)}, bf16[8,512,128]{2,1,0:T(8,128)(2,1)}, u32[]{:S(2)}) copy-start(bf16[8,512,128]{2,1,0:T(8,128)(2,1)} %param.18) | copy-start | bytes 3145732
  104.7 3.0 %collective-permute-start.21 = (bf16[16,32,1152]{2,1,0:T(8,128)(2,1)S(1)}, bf16[16,32,1152]{2,1,0:T(8,128)(2,1)}, u32[]{:S(2)}, u32[]{:S(2)}) collective-permute-start(bf16[16,32,1152]{2,1,0:T(8,128)(2,1)S(1)} %collective-permute-done.20), channel_id=1, source_target_pairs={{0,1},{1,0},{2,3},{3,2},{4,5},{5,4},{6,7},{7,6},{8,9},{9,8},{10,11... | collective-permute-start | bytes 3538952 | tf_op jit(solution)/shard_map/ppermute | solution.py:771

commit v3 on v2

--- a/solution.py
+++ b/solution.py
@@ -787,22 +787,25 @@
     early_steps = [stream(first)]
     share = half_len // n_head
     partials = lax.all_to_all(partial_value, "head", split_axis=0, concat_axis=0, tiled=True)
+    limits = plan_blocks(owner_rows, prefix_len, n_head, chunk, page_len)
+    partials, q_turned, limits, early_steps[0] = lax.optimization_barrier(
+        (partials, q_turned, limits, early_steps[0])
+    )
     summed = jnp.sum(partials.reshape(n_head, share, lat_width), axis=0)
     share_t = seq_idx * half_len + head_idx * share + jnp.arange(share, dtype=jnp.int32)
     latent = finish_latent(summed, my_prefix + share_t, share_t < live, kv_gain, latent_width)
     copies = jnp.concatenate([latent] * n_head, axis=0)
     fresh = lax.all_to_all(copies, "head", split_axis=0, concat_axis=0, tiled=True)
-    early_steps[0], fresh = lax.optimization_barrier((early_steps[0], fresh))
     for step in range(1, n_head - 1):
         early_steps.append(stream(early_steps[-1]))
     early_steps = [[block, None] for block in early_steps]
     for step in range(n_head - 2):
         early_steps[step][1] = swap(early_steps[step][0])
     mine = arrived[0][None] if n_req == 2 else jnp.stack(arrived)
-    most = over_groups(most)
-    mine, fresh, most = lax.optimization_barrier((mine, fresh, most))
+    mine, partials = lax.optimization_barrier((mine, partials))
     other = swap(mine)
     middle, late = join_pages(counts, rest, mine, other, chunk, cap, (2 * chunk, chunk))
+    middle, fresh = lax.optimization_barrier((middle, fresh))
 
     tile = 256 if rows % 256 == 0 and 256 % half_len == 0 else half_len
     shape = (tile, score_scale * math.log2(math.e), chunk, lat_width)
@@ -810,7 +813,6 @@
     near_state = ()
     extra = 4 + 1 + 2 * last
     total = 1 + 2 * (last + 1) + 2 + 4 * last + extra
-    limits = plan_blocks(owner_rows, prefix_len, n_head, chunk, page_len)
     n_blocks = 0
     state = None
 
@@ -848,6 +850,8 @@
         received = tie(received)
         if step == 0:
             early_steps[last][0] = tie(early_steps[last][0])
+            received, most = lax.optimization_barrier((received, most))
+            most = over_groups(most)
             early_steps[last][1] = swap(early_steps[last][0])
             opposite = swap(fresh)
             suffix_latent = jnp.where(
@@ -855,6 +859,8 @@
                 jnp.concatenate([fresh, opposite], axis=0),
                 jnp.concatenate([opposite, fresh], axis=0),
             )
+        if step == last - 1:
+            received, most = lax.optimization_barrier((received, most))
         if step < last:
             block = stream(received)
         middle_steps.append([received, swap(received)])

time: 124 us -> 126 us (1.016)
  Pallas kernels: 53.5 us -> 58 us
  starting transfers between devices: 40.1 us -> 37.1 us
  local copies, waits for them, and re-layouts: 4.76 us -> 6.36 us
    ppermute x1, waiting for transfers between devices: 0.01 us -> 2.96 us  [local(): lax.ppermute(foreign[s - 1], 'req', [(i, (i + s) % n_req) for i in range(...]
    pallas_call x3, Pallas kernels: 25 us -> 27.6 us  [score_part(): pl.pallas_call(functools.partial(score_kernel, shape, base, len(sources),...]
    all_to_all x1, starting transfers between devices: 6.33 us -> 3.84 us  [local(): lax.all_to_all(partial_value, 'head', split_axis=0, concat_axis=0, tiled=...]
    ppermute x8, waiting for transfers between devices: 4.79 us -> 2.58 us  [swap(): return lax.ppermute(block, 'seq', swap_route)]
    all_to_all x1, waiting for transfers between devices: 4.57 us -> 2.42 us  [local(): lax.all_to_all(partial_value, 'head', split_axis=0, concat_axis=0, tiled=...]
    unnamed x16 -> x26, local copies, waits for them, and re-layouts: 2.98 us -> 4.58 us
  transfers between devices with their start and end apart: 18 -> 18, of which waited for: 9 -> 7; matrix products, arithmetic and copies ran while one was open for 6% -> 5% of each run, Pallas kernels for 27% -> 30%
where the time goes in v3:
time: 126 us; the launch traced here: 125 us
  Pallas kernels  58 us (46%)
  starting transfers between devices  37.1 us (29%)
  waiting for transfers between devices  15.5 us (12%)
  local copies, waits for them, and re-layouts  6.36 us (5%)
  other arithmetic  4.54 us (4%)
  between operations  3.01 us (2%)
    pallas_call x3, Pallas kernels, score_part(): pl.pallas_call(functools.partial(score_kernel, shape, base, len(sources),...  27.6 us
    ppermute x6, starting transfers between devices, stream(): return lax.ppermute(block, ('head', 'seq'), stream_route)  26 us
    pallas_call x1, Pallas kernels, finish(): pl.pallas_call(functools.partial(finish_kernel, shape, depth, n_blocks, l...  15.9 us
    pallas_call x1, Pallas kernels, pick_pages(): pl.pallas_call(functools.partial(pick_kernel, cap, 2 * pairs), out_shape=...  5 us
    unnamed x26, local copies, waits for them, and re-layouts  4.58 us
    ppermute x6, waiting for transfers between devices, stream(): return lax.ppermute(block, ('head', 'seq'), stream_route)  4.53 us
    pallas_call x1, Pallas kernels, join_pages(): pl.pallas_call(functools.partial(join_kernel, chunk, cap), out_shape=tupl...  4.38 us
    pallas_call x1, Pallas kernels, turn_queries(): pl.pallas_call(query_kernel, out_shape=jax.ShapeDtypeStruct((key_rows, ro...  3.99 us
  transfers between devices with their start and end apart: 18, of which 7 were waited for; matrix products, arithmetic and copies ran while one was open for 5% of the time, Pallas kernels for 30%

profile of v3, /device:TPU:0, one launch (start us, length us, event | category | flops | bytes accessed | tf_op | source)
XLA Modules:
  0.0 124.7 jit_solution(5878240101721146246)
XLA Ops:
  0.6 5.0 %pick_pages.1 = (s32[2]{0:T(128)}, s32[1]{0:T(128)}, s32[1]{0:T(128)}, s32[1]{0:T(128)}, bf16[8,32,1152]{2,1,0:T(8,128)(2,1)}, /*index=5*/bf16[8,32,1152]{2,1,0:...) custom-call(s32[2,64]{1,0:T(2,128)} %bitcast.29, s32[2,64]{1,0:T(2,128)} %slot_hbm.1, s32[2]{0:T(128)} %prefix_ref.1, ...), custom_call_target="tpu_custom_call" | custom-call | flops 1000000000 | bytes 6000000 | tf_op jit(solution)/shard_map/pick_pages/pallas_call | solution.py:163
  5.6 5.0 %collective-permute-start.7 = (bf16[8,32,1152]{2,1,0:T(8,128)(2,1)}, bf16[8,32,1152]{2,1,0:T(8,128)(2,1)S(1)}, u32[]{:S(2)}, u32[]{:S(2)}) collective-permute-start(bf16[8,32,1152]{2,1,0:T(8,128)(2,1)} %get-tuple-element.168.refs_0_), channel_id=1, source_target_pairs={{0,4},{5,1},{4,8},{9,5},{8,12},{13,9},{2,6},{7,3},{6,10},{11,7},{1... | collective-permute-start | bytes 1769480 | tf_op jit(solution)/shard_map/ppermute | solution.py:774
  10.6 3.8 %all-to-all-start = ((f32[4,32,576]{2,1,0:T(8,128)}), f32[4,32,576]{2,1,0:T(8,128)S(1)}, u32[]{:S(2)}, u32[]{:S(2)}) async-start(f32[4,32,576]{2,1,0:T(8,128)} %bitcast.26), calls=%async_computation | async-start | bytes 655360 | tf_op jit(solution)/shard_map/all_to_all | solution.py:789
  14.4 1.5 %collective-permute-start.6 = (bf16[8,32,1152]{2,1,0:T(8,128)(2,1)}, bf16[8,32,1152]{2,1,0:T(8,128)(2,1)S(1)}, u32[]{:S(2)}, u32[]{:S(2)}) collective-permute-start(bf16[8,32,1152]{2,1,0:T(8,128)(2,1)} %bitcast.31), channel_id=1, source_target_pairs={{0,2},{2,0},{1,3},{3,1},{4,6},{6,4},{5,7},{7,5},{8,10},{10,8},{9,1... | collective-permute-start | bytes 1769480 | tf_op jit(solution)/shard_map/ppermute | solution.py:784
  16.5 0.8 multiply_sine_fusion.1
  17.3 1.1 plan_blocks.1.limit_ref
  18.4 4.0 %turn_queries.1.queries_ref = bf16[640,1024]{1,0:T(8,128)(2,1)} custom-call(bf16[128,1536]{1,0:T(8,128)(2,1)} %bitcast.25, bf16[8,128,512]{2,1,0:T(8,128)(2,1)} %up_hbm.1, f32[32,128]{1,0:T(8,128)} %get-tuple-element.215.cosine_ref, f32[32,128]{1,0:T(8,128)} %get-tuple-element.214.sine_ref), custom_call_target="tpu_custom_call" | custom-call | flops 134217728 | bytes 3000000 | tf_op jit(solution)/shard_map/turn_queries/pallas_call | solution.py:346
  22.4 0.5 add_convert_fusion
  22.9 0.6 fusion.8
  23.5 2.4 %all-to-all-done = f32[4,32,576]{2,1,0:T(8,128)S(1)} async-done(((f32[4,32,576]{2,1,0:T(8,128)}), f32[4,32,576]{2,1,0:T(8,128)S(1)}, u32[]{:S(2)}, u32[]{:S(2)}) %all-to-all-start) | async-done | bytes 294944 | tf_op jit(solution)/shard_map/all_to_all | solution.py:789
  26.0 0.0 collective-permute-done.7.refs_1_
  26.0 0.1 multiply_reduce_fusion
  26.1 3.0 %collective-permute-done.6 = bf16[8,32,1152]{2,1,0:T(8,128)(2,1)S(1)} collective-permute-done((bf16[8,32,1152]{2,1,0:T(8,128)(2,1)}, bf16[8,32,1152]{2,1,0:T(8,128)(2,1)S(1)}, u32[]{:S(2)}, u32[]{:S(2)}) %collective-permute-start.6) | collective-permute-done | bytes 589856 | tf_op jit(solution)/shard_map/ppermute | solution.py:784
  29.1 0.0 collective-permute-start.8
  29.1 4.5 %collective-permute-start.9 = (bf16[8,32,1152]{2,1,0:T(8,128)(2,1)S(1)}, bf16[8,32,1152]{2,1,0:T(8,128)(2,1)}, u32[]{:S(2)}, u32[]{:S(2)}) collective-permute-start(bf16[8,32,1152]{2,1,0:T(8,128)(2,1)S(1)} %collective-permute-done.7.refs_1_), channel_id=1, source_target_pairs={{0,4},{5,1},{4,8},{9,5},{8,12},{13,9},{2,6},{7,3},{6,10},{11,7},{1... | collective-permute-start | bytes 1769480 | tf_op jit(solution)/shard_map/ppermute | solution.py:774
  33.5 0.8 multiply_convert_fusion
  34.3 0.1 fusion.5
  34.4 0.1 maximum_select_fusion.1
  34.5 0.7 pad_maximum_fusion
  35.2 3.3 %all-to-all-start.1 = ((bf16[4,32,576]{2,1,0:T(8,128)(2,1)}), bf16[4,32,576]{2,1,0:T(8,128)(2,1)S(1)}, u32[]{:S(2)}, u32[]{:S(2)}) async-start(bf16[4,32,576]{2,1,0:T(8,128)(2,1)} %bitcast.15), calls=%async_computation.1 | async-start | bytes 327680 | tf_op jit(solution)/shard_map/all_to_all | solution.py:798
  38.6 0.0 collective-permute-done.8.other_ref
  38.6 1.1 copy-done.1
  39.6 0.7 copy-done.2
  40.3 4.4 %join_pages.1 = (bf16[16,32,1152]{2,1,0:T(8,128)(2,1)S(1)}, bf16[8,32,1152]{2,1,0:T(8,128)(2,1)}) custom-call(s32[2]{0:T(128)S(1)} %copy-done.2, bf16[8,32,1152]{2,1,0:T(8,128)(2,1)S(1)} %copy-done.1, bf16[1,8,32,1152]{3,2,1,0:T(8,128)(2,1)S(1)} %bitcast.19, bf16[1,8,32,1152]{3,2,1,0:T(8,128)(2,1)S(1)} %collective-permute-done.8.other_ref), custom_call_target="tpu_custom_call" | custom-call | bytes 3000000 | tf_op jit(solution)/shard_map/join_pages/pallas_call | solution.py:231
  44.7 0.8 all-to-all-done.1
  45.6 0.0 collective-permute-done.9.refs_3_
  45.6 3.1 %collective-permute-start.10 = (bf16[16,32,1152]{2,1,0:T(8,128)(2,1)S(1)}, bf16[16,32,1152]{2,1,0:T(8,128)(2,1)S(1)}, u32[]{:S(2)}, u32[]{:S(2)}) collective-permute-start(bf16[16,32,1152]{2,1,0:T(8,128)(2,1)S(1)} %get-tuple-element.175.refs_7_), channel_id=1, source_target_pairs={{0,4},{5,1},{4,8},{9,5},{8,12},{13,9},{2,6},{7,3},{6,10},{11,7},{1... | collective-permute-start | bytes 3538952 | tf_op jit(solution)/shard_map/ppermute | solution.py:774
  48.7 0.1 collective-permute-start.11
  48.8 0.5 collective-permute-start.12
  49.3 3.3 %collective-permute-start.14 = (bf16[8,32,1152]{2,1,0:T(8,128)(2,1)}, bf16[8,32,1152]{2,1,0:T(8,128)(2,1)S(1)}, u32[]{:S(2)}, u32[]{:S(2)}) collective-permute-start(bf16[8,32,1152]{2,1,0:T(8,128)(2,1)} %collective-permute-done.9.refs_3_), channel_id=1, source_target_pairs={{0,4},{5,1},{4,8},{9,5},{8,12},{13,9},{2,6},{7,3},{6,10},{11,7},{1... | collective-permute-start | bytes 1769480 | tf_op jit(solution)/shard_map/ppermute | solution.py:774
  52.6 0.0 collective-permute-done.11.refs_2_
  52.6 0.0 collective-permute-done.12.refs_4_
  52.7 0.0 copy-done.16
  52.7 0.8 copy-done.17
  53.4 0.8 copy-done.18
  54.3 8.7 %score_part.9 = (f32[26,512,1024]{2,1,0:T(8,128)}, bf16[26,512,512]{2,1,0:T(8,128)(2,1)}, f32[26,1024]{1,0:T(8,128)}, f32[1,1024]{1,0:T(1,128)}, f32[1,1024]{1,0:T(1,128)}) custom-call(s32[1,224]{1,0:T(1,128)S(1)} %plan_blocks.1.limit_ref, bf16[640,1024]{1,0:T(8,128)(2,1)} %turn_queries.1.queries_ref, bf16[8,32,1152]{2,1,0:T(8,128)(2,1)} %get-tuple-element.168.refs_0_, ...), custom_call_target="tpu_custom_call" | custom-call | flops 1310720 | bytes 100000 | tf_op jit(solution)/shard_map/score_part/pallas_call | solution.py:553
  63.0 0.0 collective-permute-done.10.refs_8_
  63.0 0.1 collective-permute-start.16
  63.1 5.7 %collective-permute-start.13 = (bf16[16,32,1152]{2,1,0:T(8,128)(2,1)S(1)}, bf16[16,32,1152]{2,1,0:T(8,128)(2,1)}, u32[]{:S(2)}, u32[]{:S(2)}) collective-permute-start(bf16[16,32,1152]{2,1,0:T(8,128)(2,1)S(1)} %collective-permute-done.10.refs_8_), channel_id=1, source_target_pairs={{0,4},{5,1},{4,8},{9,5},{8,12},{13,9},{2,6},{7,3},{6,10},{11,7},{1... | collective-permute-start | bytes 3538952 | tf_op jit(solution)/shard_map/ppermute | solution.py:774
  68.8 0.0 collective-permute-done.14.refs_5_
  68.8 0.0 collective-permute-start.15
  68.8 1.6 %collective-permute-start.17 = (s32[1]{0:T(128)}, s32[1]{0:T(128)}, u32[]{:S(2)}, u32[]{:S(2)}) collective-permute-start(s32[1]{0:T(128)} %get-tuple-element.192), channel_id=1, source_target_pairs={{0,16},{16,0},{1,17},{17,1},{2,18},{18,2},{3,19},{19,3},{4,20},{20... | collective-permute-start | bytes 20 | tf_op jit(solution)/shard_map/ppermute | solution.py:304
  70.4 2.2 %collective-permute-done.17 = s32[1]{0:T(128)} collective-permute-done((s32[1]{0:T(128)}, s32[1]{0:T(128)}, u32[]{:S(2)}, u32[]{:S(2)}) %collective-permute-start.17) | collective-permute-done | bytes 36 | tf_op jit(solution)/shard_map/ppermute | solution.py:304
  73.8 0.0 collective-permute-done.15.refs_6_
  73.8 0.0 copy-start.20
  73.9 0.0 collective-permute-done.16.refs_9_
  73.9 0.8 copy-done.20
  74.7 0.4 copy-done.8
  75.1 11.8 %score_part.10 = (f32[26,512,1024]{2,1,0:T(8,128)}, bf16[26,512,512]{2,1,0:T(8,128)(2,1)}, f32[26,1024]{1,0:T(8,128)}, f32[1,1024]{1,0:T(1,128)}, f32[1,1024]{1,0:T(1,128)}) custom-call(s32[1,224]{1,0:T(1,128)S(1)} %plan_blocks.1.limit_ref, bf16[640,1024]{1,0:T(8,128)(2,1)} %turn_queries.1.queries_ref, ...), custom_call_target="tpu_custom_call", output_to_operand_aliasing={{0}: (5, {}), {1}: (6, {})} | custom-call | flops 2097152 | bytes 100000 | tf_op jit(solution)/shard_map/score_part/pallas_call | solution.py:553
  86.9 0.0 collective-permute-done.13.refs_7_
  86.9 0.1 collective-permute-start.19
  87.0 4.5 %collective-permute-start.20 = (bf16[16,32,1152]{2,1,0:T(8,128)(2,1)}, bf16[16,32,1152]{2,1,0:T(8,128)(2,1)S(1)}, u32[]{:S(2)}, u32[]{:S(2)}) collective-permute-start(bf16[16,32,1152]{2,1,0:T(8,128)(2,1)} %collective-permute-done.13.refs_7_), channel_id=1, source_target_pairs={{0,4},{5,1},{4,8},{9,5},{8,12},{13,9},{2,6},{7,3},{6,10},{11,7},{1... | collective-permute-start | bytes 3538952 | tf_op jit(solution)/shard_map/ppermute | solution.py:774
  91.4 0.1 collective-permute-start.18
  91.5 1.4 %collective-permute-done.18 = bf16[128,576]{1,0:T(8,128)(2,1)S(1)} collective-permute-done((bf16[128,576]{1,0:T(8,128)(2,1)S(1)}, bf16[128,576]{1,0:T(8,128)(2,1)S(1)}, u32[]{:S(2)}, u32[]{:S(2)}) %collective-permute-start.18) | collective-permute-done | bytes 147488 | tf_op jit(solution)/shard_map/ppermute | solution.py:771
  92.9 0.0 copy-done.6
  92.9 0.8 maximum_select_fusion.refs_6_
  93.7 0.0 collective-permute-done.19.refs_8_
  93.7 7.2 %score_part.11 = (f32[26,512,1024]{2,1,0:T(8,128)}, bf16[26,512,512]{2,1,0:T(8,128)(2,1)}, f32[26,1024]{1,0:T(8,128)}, f32[1,1024]{1,0:T(1,128)S(1)}, f32[1,1024...) custom-call(s32[1,224]{1,0:T(1,128)S(1)} %plan_blocks.1.limit_ref, ...), custom_call_target="tpu_custom_call", output_to_operand_aliasing={{0}: (5, {}), {1}: (6, {})} | custom-call | flops 1048576 | bytes 100000 | tf_op jit(solution)/shard_map/score_part/pallas_call | solution.py:553
  100.9 4.5 %collective-permute-done.20 = bf16[16,32,1152]{2,1,0:T(8,128)(2,1)S(1)} collective-permute-done((bf16[16,32,1152]{2,1,0:T(8,128)(2,1)}, bf16[16,32,1152]{2,1,0:T(8,128)(2,1)S(1)}, u32[]{:S(2)}, u32[]{:S(2)}) %collective-permute-start.20) | collective-permute-done | bytes 1179680 | tf_op jit(solution)/shard_map/ppermute | solution.py:774
  105.4 0.0 collective-permute-start.21
  105.4 1.8 %reshape.48 = bf16[1,2,36864]{2,1,0:T(2,128)(2,1)} reshape(bf16[128,576]{1,0:T(8,128)(2,1)} %bitcast.23) | data formatting | bytes 294912 | tf_op jit(solution)/shard_map/reshape | solution.py:896
  107.2 1.2 collective-permute-done.21
  108.4 16.2 %conditional.1 = (bf16[1,128,1024]{2,1,0:T(8,128)(2,1)}) conditional(s32[]{:T(128)} %convert_element_type.20, (s32[1,224]{1,0:T(1,128)S(1)}, bf16[640,1024]{1,0:T(8,128)(2,1)S(1)}, f32[26,1024]{1,0:T(8,128)}, f32[1,1024]{1,0:T(1,128)S(1)}, f32[1,1024]{1,0:T(1,128)S(1)}, /*index=5*/f32[256,1024]{1,0:T(8,128)}, bf16[512,256]{1,0:T(8,128)(2,1)}, ...), branch_computations={%region_2.3_spmd, %region_3.4_spmd} | conditional | flops 8055422976 | bytes 63854904 | solution.py:895
  108.4 15.9 %finish.2 = bf16[128,1024]{1,0:T(8,128)(2,1)} custom-call(s32[1,224]{1,0:T(1,128)S(1)} %get-tuple-element.62.limit_ref, bf16[640,1024]{1,0:T(8,128)(2,1)S(1)} %get-tuple-element.63.queries_ref, f32[26,1024]{1,0:T(8,128)} %get-tuple-element.64.marks, f32[1,1024]{1,0:T(1,128)S(1)} %get-tuple-element.65.sum_in, f32[1,1024]{1,0:T(1,128)S(1)} %get-tuple-element.66.high_in, ...), custom_call_target="tpu_custom_call" | custom-call | flops 6442450944 | bytes 30000000 | tf_op jit(solution)/shard_map/cond/branch_0_fun/finish/pallas_call | solution.py:692
  (21 shorter events, 0.1 us)
Async XLA Ops:
  5.6 20.3 %collective-permute-start.7 = (bf16[8,32,1152]{2,1,0:T(8,128)(2,1)}, bf16[8,32,1152]{2,1,0:T(8,128)(2,1)S(1)}, u32[]{:S(2)}, u32[]{:S(2)}) collective-permute-start(bf16[8,32,1152]{2,1,0:T(8,128)(2,1)} %get-tuple-element.168.refs_0_), channel_id=1, source_target_pairs={{0,4},{5,1},{4,8},{9,5},{8,12},{13,9},{2,6},{7,3},{6,10},{11,7},{1... | collective-permute-start | bytes 1769480 | tf_op jit(solution)/shard_map/ppermute | solution.py:774
  10.6 15.4 %all-to-all-start = ((f32[4,32,576]{2,1,0:T(8,128)}), f32[4,32,576]{2,1,0:T(8,128)S(1)}, u32[]{:S(2)}, u32[]{:S(2)}) async-start(f32[4,32,576]{2,1,0:T(8,128)} %bitcast.26), calls=%async_computation | async-start | bytes 655360 | tf_op jit(solution)/shard_map/all_to_all | solution.py:789
  14.4 14.6 %collective-permute-start.6 = (bf16[8,32,1152]{2,1,0:T(8,128)(2,1)}, bf16[8,32,1152]{2,1,0:T(8,128)(2,1)S(1)}, u32[]{:S(2)}, u32[]{:S(2)}) collective-permute-start(bf16[8,32,1152]{2,1,0:T(8,128)(2,1)} %bitcast.31), channel_id=1, source_target_pairs={{0,2},{2,0},{1,3},{3,1},{4,6},{6,4},{5,7},{7,5},{8,10},{10,8},{9,1... | collective-permute-start | bytes 1769480 | tf_op jit(solution)/shard_map/ppermute | solution.py:784
  26.0 26.7 %copy-start.16 = (bf16[8,32,1152]{2,1,0:T(8,128)(2,1)}, bf16[8,32,1152]{2,1,0:T(8,128)(2,1)S(1)}, u32[]{:S(2)}) copy-start(bf16[8,32,1152]{2,1,0:T(8,128)(2,1)S(1)} %collective-permute-done.7.refs_1_) | copy-start | bytes 1769476
  29.1 9.5 %collective-permute-start.8 = (bf16[1,8,32,1152]{3,2,1,0:T(8,128)(2,1)S(1)}, bf16[1,8,32,1152]{3,2,1,0:T(8,128)(2,1)S(1)}, u32[]{:S(2)}, u32[]{:S(2)}) collective-permute-start(bf16[1,8,32,1152]{3,2,1,0:T(8,128)(2,1)S(1)} %bitcast.18), channel_id=1, source_target_pairs={{0,1},{1,0},{2,3},{3,2},{4,5},{5,4},{6,7},{7,6},{8,9},{9,8},{10,11... | collective-permute-start | bytes 1769480 | tf_op jit(solution)/shard_map/ppermute | solution.py:771
  29.1 16.5 %collective-permute-start.9 = (bf16[8,32,1152]{2,1,0:T(8,128)(2,1)S(1)}, bf16[8,32,1152]{2,1,0:T(8,128)(2,1)}, u32[]{:S(2)}, u32[]{:S(2)}) collective-permute-start(bf16[8,32,1152]{2,1,0:T(8,128)(2,1)S(1)} %collective-permute-done.7.refs_1_), channel_id=1, source_target_pairs={{0,4},{5,1},{4,8},{9,5},{8,12},{13,9},{2,6},{7,3},{6,10},{11,7},{1... | collective-permute-start | bytes 1769480 | tf_op jit(solution)/shard_map/ppermute | solution.py:774
  35.2 10.3 %all-to-all-start.1 = ((bf16[4,32,576]{2,1,0:T(8,128)(2,1)}), bf16[4,32,576]{2,1,0:T(8,128)(2,1)S(1)}, u32[]{:S(2)}, u32[]{:S(2)}) async-start(bf16[4,32,576]{2,1,0:T(8,128)(2,1)} %bitcast.15), calls=%async_computation.1 | async-start | bytes 327680 | tf_op jit(solution)/shard_map/all_to_all | solution.py:798
  38.6 1.1 copy-start.1
  39.6 0.7 copy-start.2
  44.7 29.2 %copy-start = (bf16[16,32,1152]{2,1,0:T(8,128)(2,1)}, bf16[16,32,1152]{2,1,0:T(8,128)(2,1)S(1)}, u32[]{:S(2)}) copy-start(bf16[16,32,1152]{2,1,0:T(8,128)(2,1)S(1)} %get-tuple-element.175.refs_7_) | copy-start | bytes 3538948
  45.6 47.3 %copy-start.6 = (bf16[4,32,576]{2,1,0:T(8,128)(2,1)}, bf16[4,32,576]{2,1,0:T(8,128)(2,1)S(1)}, u32[]{:S(2)}) copy-start(bf16[4,32,576]{2,1,0:T(8,128)(2,1)S(1)} %all-to-all-done.1) | copy-start | bytes 442372
  45.6 17.4 %collective-permute-start.10 = (bf16[16,32,1152]{2,1,0:T(8,128)(2,1)S(1)}, bf16[16,32,1152]{2,1,0:T(8,128)(2,1)S(1)}, u32[]{:S(2)}, u32[]{:S(2)}) collective-permute-start(bf16[16,32,1152]{2,1,0:T(8,128)(2,1)S(1)} %get-tuple-element.175.refs_7_), channel_id=1, source_target_pairs={{0,4},{5,1},{4,8},{9,5},{8,12},{13,9},{2,6},{7,3},{6,10},{11,7},{1... | collective-permute-start | bytes 3538952 | tf_op jit(solution)/shard_map/ppermute | solution.py:774
  48.7 3.9 %collective-permute-start.11 = (bf16[8,32,1152]{2,1,0:T(8,128)(2,1)S(1)}, bf16[8,32,1152]{2,1,0:T(8,128)(2,1)S(1)}, u32[]{:S(2)}, u32[]{:S(2)}) collective-permute-start(bf16[8,32,1152]{2,1,0:T(8,128)(2,1)S(1)} %collective-permute-done.7.refs_1_), channel_id=1, source_target_pairs={{0,1},{1,0},{2,3},{3,2},{4,5},{5,4},{6,7},{7,6},{8,9},{9,8},{10,11... | collective-permute-start | bytes 1769480 | tf_op jit(solution)/shard_map/ppermute | solution.py:771
  48.8 3.8 %collective-permute-start.12 = (bf16[8,32,1152]{2,1,0:T(8,128)(2,1)}, bf16[8,32,1152]{2,1,0:T(8,128)(2,1)S(1)}, u32[]{:S(2)}, u32[]{:S(2)}) collective-permute-start(bf16[8,32,1152]{2,1,0:T(8,128)(2,1)} %collective-permute-done.9.refs_3_), channel_id=1, source_target_pairs={{0,1},{1,0},{2,3},{3,2},{4,5},{5,4},{6,7},{7,6},{8,9},{9,8},{10,11... | collective-permute-start | bytes 1769480 | tf_op jit(solution)/shard_map/ppermute | solution.py:771
  49.3 19.5 %collective-permute-start.14 = (bf16[8,32,1152]{2,1,0:T(8,128)(2,1)}, bf16[8,32,1152]{2,1,0:T(8,128)(2,1)S(1)}, u32[]{:S(2)}, u32[]{:S(2)}) collective-permute-start(bf16[8,32,1152]{2,1,0:T(8,128)(2,1)} %collective-permute-done.9.refs_3_), channel_id=1, source_target_pairs={{0,4},{5,1},{4,8},{9,5},{8,12},{13,9},{2,6},{7,3},{6,10},{11,7},{1... | collective-permute-start | bytes 1769480 | tf_op jit(solution)/shard_map/ppermute | solution.py:774
  52.6 0.8 copy-start.17
  53.4 0.8 copy-start.18
  63.0 10.9 %copy-start.7 = (bf16[16,32,1152]{2,1,0:T(8,128)(2,1)}, bf16[16,32,1152]{2,1,0:T(8,128)(2,1)S(1)}, u32[]{:S(2)}) copy-start(bf16[16,32,1152]{2,1,0:T(8,128)(2,1)S(1)} %collective-permute-done.10.refs_8_) | copy-start | bytes 3538948
  63.0 10.9 %collective-permute-start.16 = (bf16[16,32,1152]{2,1,0:T(8,128)(2,1)S(1)}, bf16[16,32,1152]{2,1,0:T(8,128)(2,1)S(1)}, u32[]{:S(2)}, u32[]{:S(2)}) collective-permute-start(bf16[16,32,1152]{2,1,0:T(8,128)(2,1)S(1)} %collective-permute-done.10.refs_8_), channel_id=1, source_target_pairs={{0,1},{1,0},{2,3},{3,2},{4,5},{5,4},{6,7},{7,6},{8,9},{9,8},{10,11... | collective-permute-start | bytes 3538952 | tf_op jit(solution)/shard_map/ppermute | solution.py:771
  63.1 23.8 %collective-permute-start.13 = (bf16[16,32,1152]{2,1,0:T(8,128)(2,1)S(1)}, bf16[16,32,1152]{2,1,0:T(8,128)(2,1)}, u32[]{:S(2)}, u32[]{:S(2)}) collective-permute-start(bf16[16,32,1152]{2,1,0:T(8,128)(2,1)S(1)} %collective-permute-done.10.refs_8_), channel_id=1, source_target_pairs={{0,4},{5,1},{4,8},{9,5},{8,12},{13,9},{2,6},{7,3},{6,10},{11,7},{1... | collective-permute-start | bytes 3538952 | tf_op jit(solution)/shard_map/ppermute | solution.py:774
  68.8 5.1 %copy-start.19 = (bf16[8,32,1152]{2,1,0:T(8,128)(2,1)}, bf16[8,32,1152]{2,1,0:T(8,128)(2,1)S(1)}, u32[]{:S(2)}) copy-start(bf16[8,32,1152]{2,1,0:T(8,128)(2,1)S(1)} %collective-permute-done.14.refs_5_) | copy-start | bytes 1769476
  68.8 5.1 %collective-permute-start.15 = (bf16[8,32,1152]{2,1,0:T(8,128)(2,1)S(1)}, bf16[8,32,1152]{2,1,0:T(8,128)(2,1)S(1)}, u32[]{:S(2)}, u32[]{:S(2)}) collective-permute-start(bf16[8,32,1152]{2,1,0:T(8,128)(2,1)S(1)} %collective-permute-done.14.refs_5_), channel_id=1, source_target_pairs={{0,1},{1,0},{2,3},{3,2},{4,5},{5,4},{6,7},{7,6},{8,9},{9,8},{10,11... | collective-permute-start | bytes 1769480 | tf_op jit(solution)/shard_map/ppermute | solution.py:771
  68.8 3.7 %collective-permute-start.17 = (s32[1]{0:T(128)}, s32[1]{0:T(128)}, u32[]{:S(2)}, u32[]{:S(2)}) collective-permute-start(s32[1]{0:T(128)} %get-tuple-element.192), channel_id=1, source_target_pairs={{0,16},{16,0},{1,17},{17,1},{2,18},{18,2},{3,19},{19,3},{4,20},{20... | collective-permute-start | bytes 20 | tf_op jit(solution)/shard_map/ppermute | solution.py:304
  73.8 0.8 copy-start.20
  73.9 1.2 copy-start.8
  75.1 18.6 %copy-start.3 = (bf16[640,1024]{1,0:T(8,128)(2,1)S(1)}, bf16[640,1024]{1,0:T(8,128)(2,1)}, u32[]{:S(2)}) copy-start(bf16[640,1024]{1,0:T(8,128)(2,1)} %turn_queries.1.queries_ref) | copy-start | bytes 3932164
  86.9 6.8 %collective-permute-start.19 = (bf16[16,32,1152]{2,1,0:T(8,128)(2,1)}, bf16[16,32,1152]{2,1,0:T(8,128)(2,1)}, u32[]{:S(2)}, u32[]{:S(2)}) collective-permute-start(bf16[16,32,1152]{2,1,0:T(8,128)(2,1)} %collective-permute-done.13.refs_7_), channel_id=1, source_target_pairs={{0,1},{1,0},{2,3},{3,2},{4,5},{5,4},{6,7},{7,6},{8,9},{9,8},{10,11... | collective-permute-start | bytes 3538952 | tf_op jit(solution)/shard_map/ppermute | solution.py:771
  87.0 18.4 %collective-permute-start.20 = (bf16[16,32,1152]{2,1,0:T(8,128)(2,1)}, bf16[16,32,1152]{2,1,0:T(8,128)(2,1)S(1)}, u32[]{:S(2)}, u32[]{:S(2)}) collective-permute-start(bf16[16,32,1152]{2,1,0:T(8,128)(2,1)} %collective-permute-done.13.refs_7_), channel_id=1, source_target_pairs={{0,4},{5,1},{4,8},{9,5},{8,12},{13,9},{2,6},{7,3},{6,10},{11,7},{1... | collective-permute-start | bytes 3538952 | tf_op jit(solution)/shard_map/ppermute | solution.py:774
  91.4 1.5 %collective-permute-start.18 = (bf16[128,576]{1,0:T(8,128)(2,1)S(1)}, bf16[128,576]{1,0:T(8,128)(2,1)S(1)}, u32[]{:S(2)}, u32[]{:S(2)}) collective-permute-start(bf16[128,576]{1,0:T(8,128)(2,1)S(1)} %bitcast.21), channel_id=1, source_target_pairs={{0,1},{1,0},{2,3},{3,2},{4,5},{5,4},{6,7},{7,6},{8,9},{9,8},{10,11... | collective-permute-start | bytes 442376 | tf_op jit(solution)/shard_map/ppermute | solution.py:771
  93.7 14.7 %copy-start.4 = (bf16[8,512,128]{2,1,0:T(8,128)(2,1)S(1)}, bf16[8,512,128]{2,1,0:T(8,128)(2,1)}, u32[]{:S(2)}) copy-start(bf16[8,512,128]{2,1,0:T(8,128)(2,1)} %param.18) | copy-start | bytes 3145732
  105.4 3.0 %collective-permute-start.21 = (bf16[16,32,1152]{2,1,0:T(8,128)(2,1)S(1)}, bf16[16,32,1152]{2,1,0:T(8,128)(2,1)}, u32[]{:S(2)}, u32[]{:S(2)}) collective-permute-start(bf16[16,32,1152]{2,1,0:T(8,128)(2,1)S(1)} %collective-permute-done.20), channel_id=1, source_target_pairs={{0,1},{1,0},{2,3},{3,2},{4,5},{5,4},{6,7},{7,6},{8,9},{9,8},{10,11... | collective-permute-start | bytes 3538952 | tf_op jit(solution)/shard_map/ppermute | solution.py:771

commit v4 on v3

--- a/solution.py
+++ b/solution.py
@@ -685,7 +685,7 @@
     _, latent_width, block_keys = values.shape
     _, pairs, pair_width = sources[0].shape
     heads, _, value_width = up_weight.shape
-    depth = 4
+    depth = 8
     n_last = sum(s.shape[0] for s in sources) // chunk
     row = pltpu.VMEM((1, rows), jnp.float32)
     work = (n_blocks // 2 + n_last) * block_keys * rows

time: 126 us -> 124 us (0.984)
  the two profiles are of different devices: /device:TPU:0 before, /device:TPU:6 now
where the time goes in v4:
time: 124 us; the launch traced here: 121 us
  Pallas kernels  56 us (45%)
  starting transfers between devices  33.6 us (27%)
  waiting for transfers between devices  17.5 us (14%)
  local copies, waits for them, and re-layouts  6.36 us (5%)
  other arithmetic  4.54 us (4%)
  between operations  3.01 us (2%)
    pallas_call x3, Pallas kernels, score_part(): pl.pallas_call(functools.partial(score_kernel, shape, base, len(sources),...  26.3 us
    ppermute x6, starting transfers between devices, stream(): return lax.ppermute(block, ('head', 'seq'), stream_route)  24.6 us
    pallas_call x1, Pallas kernels, finish(): pl.pallas_call(functools.partial(finish_kernel, shape, depth, n_blocks, l...  15.3 us
    pallas_call x1, Pallas kernels, pick_pages(): pl.pallas_call(functools.partial(pick_kernel, cap, 2 * pairs), out_shape=...  5 us
    unnamed x26, local copies, waits for them, and re-layouts  4.58 us
    ppermute x6, waiting for transfers between devices, stream(): return lax.ppermute(block, ('head', 'seq'), stream_route)  4.51 us
    pallas_call x1, Pallas kernels, join_pages(): pl.pallas_call(functools.partial(join_kernel, chunk, cap), out_shape=tupl...  4.37 us
    pallas_call x1, Pallas kernels, turn_queries(): pl.pallas_call(query_kernel, out_shape=jax.ShapeDtypeStruct((key_rows, ro...  3.99 us
  transfers between devices with their start and end apart: 18, of which 7 were waited for; matrix products, arithmetic and copies ran while one was open for 5% of the time, Pallas kernels for 29%

profile of v4, /device:TPU:6, one launch (start us, length us, event | category | flops | bytes accessed | tf_op | source)
XLA Modules:
  0.0 121.3 jit_solution(12676983884261255396)
XLA Ops:
  0.6 5.0 %pick_pages.1 = (s32[2]{0:T(128)}, s32[1]{0:T(128)}, s32[1]{0:T(128)}, s32[1]{0:T(128)}, bf16[8,32,1152]{2,1,0:T(8,128)(2,1)}, /*index=5*/bf16[8,32,1152]{2,1,0:...) custom-call(s32[2,64]{1,0:T(2,128)} %bitcast.29, s32[2,64]{1,0:T(2,128)} %slot_hbm.1, s32[2]{0:T(128)} %prefix_ref.1, ...), custom_call_target="tpu_custom_call" | custom-call | flops 1000000000 | bytes 6000000 | tf_op jit(solution)/shard_map/pick_pages/pallas_call | solution.py:163
  5.6 3.5 %collective-permute-start.7 = (bf16[8,32,1152]{2,1,0:T(8,128)(2,1)}, bf16[8,32,1152]{2,1,0:T(8,128)(2,1)S(1)}, u32[]{:S(2)}, u32[]{:S(2)}) collective-permute-start(bf16[8,32,1152]{2,1,0:T(8,128)(2,1)} %get-tuple-element.168.refs_0_), channel_id=1, source_target_pairs={{0,4},{5,1},{4,8},{9,5},{8,12},{13,9},{2,6},{7,3},{6,10},{11,7},{1... | collective-permute-start | bytes 1769480 | tf_op jit(solution)/shard_map/ppermute | solution.py:774
  9.2 3.8 %all-to-all-start = ((f32[4,32,576]{2,1,0:T(8,128)}), f32[4,32,576]{2,1,0:T(8,128)S(1)}, u32[]{:S(2)}, u32[]{:S(2)}) async-start(f32[4,32,576]{2,1,0:T(8,128)} %bitcast.26), calls=%async_computation | async-start | bytes 655360 | tf_op jit(solution)/shard_map/all_to_all | solution.py:789
  13.0 0.5 collective-permute-start.6
  14.1 0.8 multiply_sine_fusion.1
  14.9 1.1 plan_blocks.1.limit_ref
  16.0 4.0 %turn_queries.1.queries_ref = bf16[640,1024]{1,0:T(8,128)(2,1)} custom-call(bf16[128,1536]{1,0:T(8,128)(2,1)} %bitcast.25, bf16[8,128,512]{2,1,0:T(8,128)(2,1)} %up_hbm.1, f32[32,128]{1,0:T(8,128)} %get-tuple-element.215.cosine_ref, f32[32,128]{1,0:T(8,128)} %get-tuple-element.214.sine_ref), custom_call_target="tpu_custom_call" | custom-call | flops 134217728 | bytes 3000000 | tf_op jit(solution)/shard_map/turn_queries/pallas_call | solution.py:346
  20.0 0.5 add_convert_fusion
  20.5 0.6 fusion.8
  21.1 3.4 %all-to-all-done = f32[4,32,576]{2,1,0:T(8,128)S(1)} async-done(((f32[4,32,576]{2,1,0:T(8,128)}), f32[4,32,576]{2,1,0:T(8,128)S(1)}, u32[]{:S(2)}, u32[]{:S(2)}) %all-to-all-start) | async-done | bytes 294944 | tf_op jit(solution)/shard_map/all_to_all | solution.py:789
  24.5 0.0 collective-permute-done.7.refs_1_
  24.6 0.1 multiply_reduce_fusion
  24.7 3.0 %collective-permute-done.6 = bf16[8,32,1152]{2,1,0:T(8,128)(2,1)S(1)} collective-permute-done((bf16[8,32,1152]{2,1,0:T(8,128)(2,1)}, bf16[8,32,1152]{2,1,0:T(8,128)(2,1)S(1)}, u32[]{:S(2)}, u32[]{:S(2)}) %collective-permute-start.6) | collective-permute-done | bytes 589856 | tf_op jit(solution)/shard_map/ppermute | solution.py:784
  27.6 0.0 collective-permute-start.8
  27.6 4.5 %collective-permute-start.9 = (bf16[8,32,1152]{2,1,0:T(8,128)(2,1)S(1)}, bf16[8,32,1152]{2,1,0:T(8,128)(2,1)}, u32[]{:S(2)}, u32[]{:S(2)}) collective-permute-start(bf16[8,32,1152]{2,1,0:T(8,128)(2,1)S(1)} %collective-permute-done.7.refs_1_), channel_id=1, source_target_pairs={{0,4},{5,1},{4,8},{9,5},{8,12},{13,9},{2,6},{7,3},{6,10},{11,7},{1... | collective-permute-start | bytes 1769480 | tf_op jit(solution)/shard_map/ppermute | solution.py:774
  32.1 0.8 multiply_convert_fusion
  32.9 0.1 fusion.5
  33.0 0.1 maximum_select_fusion.1
  33.1 0.7 pad_maximum_fusion
  33.8 3.3 %all-to-all-start.1 = ((bf16[4,32,576]{2,1,0:T(8,128)(2,1)}), bf16[4,32,576]{2,1,0:T(8,128)(2,1)S(1)}, u32[]{:S(2)}, u32[]{:S(2)}) async-start(bf16[4,32,576]{2,1,0:T(8,128)(2,1)} %bitcast.15), calls=%async_computation.1 | async-start | bytes 327680 | tf_op jit(solution)/shard_map/all_to_all | solution.py:798
  37.1 0.0 collective-permute-done.8.other_ref
  37.1 0.0 copy-start.1
  37.1 1.1 copy-done.1
  38.2 0.7 copy-done.2
  38.9 4.4 %join_pages.1 = (bf16[16,32,1152]{2,1,0:T(8,128)(2,1)S(1)}, bf16[8,32,1152]{2,1,0:T(8,128)(2,1)}) custom-call(s32[2]{0:T(128)S(1)} %copy-done.2, bf16[8,32,1152]{2,1,0:T(8,128)(2,1)S(1)} %copy-done.1, bf16[1,8,32,1152]{3,2,1,0:T(8,128)(2,1)S(1)} %bitcast.19, bf16[1,8,32,1152]{3,2,1,0:T(8,128)(2,1)S(1)} %collective-permute-done.8.other_ref), custom_call_target="tpu_custom_call" | custom-call | bytes 3000000 | tf_op jit(solution)/shard_map/join_pages/pallas_call | solution.py:231
  43.3 0.0 copy-start
  43.3 0.8 all-to-all-done.1
  44.1 0.0 collective-permute-done.9.refs_3_
  44.1 3.1 %collective-permute-start.10 = (bf16[16,32,1152]{2,1,0:T(8,128)(2,1)S(1)}, bf16[16,32,1152]{2,1,0:T(8,128)(2,1)S(1)}, u32[]{:S(2)}, u32[]{:S(2)}) collective-permute-start(bf16[16,32,1152]{2,1,0:T(8,128)(2,1)S(1)} %get-tuple-element.175.refs_7_), channel_id=1, source_target_pairs={{0,4},{5,1},{4,8},{9,5},{8,12},{13,9},{2,6},{7,3},{6,10},{11,7},{1... | collective-permute-start | bytes 3538952 | tf_op jit(solution)/shard_map/ppermute | solution.py:774
  47.3 0.1 collective-permute-start.11
  47.3 0.5 collective-permute-start.12
  47.8 3.3 %collective-permute-start.14 = (bf16[8,32,1152]{2,1,0:T(8,128)(2,1)}, bf16[8,32,1152]{2,1,0:T(8,128)(2,1)S(1)}, u32[]{:S(2)}, u32[]{:S(2)}) collective-permute-start(bf16[8,32,1152]{2,1,0:T(8,128)(2,1)} %collective-permute-done.9.refs_3_), channel_id=1, source_target_pairs={{0,4},{5,1},{4,8},{9,5},{8,12},{13,9},{2,6},{7,3},{6,10},{11,7},{1... | collective-permute-start | bytes 1769480 | tf_op jit(solution)/shard_map/ppermute | solution.py:774
  51.2 0.0 collective-permute-done.11.refs_2_
  51.2 0.0 collective-permute-done.12.refs_4_
  51.2 0.8 copy-done.17
  52.0 0.8 copy-done.18
  52.8 8.7 %score_part.9 = (f32[26,512,1024]{2,1,0:T(8,128)}, bf16[26,512,512]{2,1,0:T(8,128)(2,1)}, f32[26,1024]{1,0:T(8,128)}, f32[1,1024]{1,0:T(1,128)}, f32[1,1024]{1,0:T(1,128)}) custom-call(s32[1,224]{1,0:T(1,128)S(1)} %plan_blocks.1.limit_ref, bf16[640,1024]{1,0:T(8,128)(2,1)} %turn_queries.1.queries_ref, bf16[8,32,1152]{2,1,0:T(8,128)(2,1)} %get-tuple-element.168.refs_0_, ...), custom_call_target="tpu_custom_call" | custom-call | flops 1310720 | bytes 100000 | tf_op jit(solution)/shard_map/score_part/pallas_call | solution.py:553
  61.5 0.0 collective-permute-done.10.refs_8_
  61.5 0.1 collective-permute-start.16
  61.6 5.7 %collective-permute-start.13 = (bf16[16,32,1152]{2,1,0:T(8,128)(2,1)S(1)}, bf16[16,32,1152]{2,1,0:T(8,128)(2,1)}, u32[]{:S(2)}, u32[]{:S(2)}) collective-permute-start(bf16[16,32,1152]{2,1,0:T(8,128)(2,1)S(1)} %collective-permute-done.10.refs_8_), channel_id=1, source_target_pairs={{0,4},{5,1},{4,8},{9,5},{8,12},{13,9},{2,6},{7,3},{6,10},{11,7},{1... | collective-permute-start | bytes 3538952 | tf_op jit(solution)/shard_map/ppermute | solution.py:774
  67.3 0.0 collective-permute-done.14.refs_5_
  67.3 0.0 collective-permute-start.15
  67.3 0.6 collective-permute-start.17
  67.9 3.2 %collective-permute-done.17 = s32[1]{0:T(128)} collective-permute-done((s32[1]{0:T(128)}, s32[1]{0:T(128)}, u32[]{:S(2)}, u32[]{:S(2)}) %collective-permute-start.17) | collective-permute-done | bytes 36 | tf_op jit(solution)/shard_map/ppermute | solution.py:304
  72.4 0.0 collective-permute-done.15.refs_6_
  72.4 0.0 collective-permute-done.16.refs_9_
  72.5 0.8 copy-done.20
  73.2 0.4 copy-done.8
  73.7 10.5 %score_part.10 = (f32[26,512,1024]{2,1,0:T(8,128)}, bf16[26,512,512]{2,1,0:T(8,128)(2,1)}, f32[26,1024]{1,0:T(8,128)}, f32[1,1024]{1,0:T(1,128)}, f32[1,1024]{1,0:T(1,128)}) custom-call(s32[1,224]{1,0:T(1,128)S(1)} %plan_blocks.1.limit_ref, bf16[640,1024]{1,0:T(8,128)(2,1)} %turn_queries.1.queries_ref, ...), custom_call_target="tpu_custom_call", output_to_operand_aliasing={{0}: (5, {}), {1}: (6, {})} | custom-call | flops 2097152 | bytes 100000 | tf_op jit(solution)/shard_map/score_part/pallas_call | solution.py:553
  84.2 0.0 collective-permute-done.13.refs_7_
  84.2 0.1 collective-permute-start.19
  84.2 4.5 %collective-permute-start.20 = (bf16[16,32,1152]{2,1,0:T(8,128)(2,1)}, bf16[16,32,1152]{2,1,0:T(8,128)(2,1)S(1)}, u32[]{:S(2)}, u32[]{:S(2)}) collective-permute-start(bf16[16,32,1152]{2,1,0:T(8,128)(2,1)} %collective-permute-done.13.refs_7_), channel_id=1, source_target_pairs={{0,4},{5,1},{4,8},{9,5},{8,12},{13,9},{2,6},{7,3},{6,10},{11,7},{1... | collective-permute-start | bytes 3538952 | tf_op jit(solution)/shard_map/ppermute | solution.py:774
  88.7 0.1 collective-permute-start.18
  88.8 1.4 %collective-permute-done.18 = bf16[128,576]{1,0:T(8,128)(2,1)S(1)} collective-permute-done((bf16[128,576]{1,0:T(8,128)(2,1)S(1)}, bf16[128,576]{1,0:T(8,128)(2,1)S(1)}, u32[]{:S(2)}, u32[]{:S(2)}) %collective-permute-start.18) | collective-permute-done | bytes 147488 | tf_op jit(solution)/shard_map/ppermute | solution.py:771
  90.2 0.0 copy-done.6
  90.2 0.8 maximum_select_fusion.refs_6_
  91.0 0.0 collective-permute-done.19.refs_8_
  91.0 7.2 %score_part.11 = (f32[26,512,1024]{2,1,0:T(8,128)}, bf16[26,512,512]{2,1,0:T(8,128)(2,1)}, f32[26,1024]{1,0:T(8,128)}, f32[1,1024]{1,0:T(1,128)S(1)}, f32[1,1024...) custom-call(s32[1,224]{1,0:T(1,128)S(1)} %plan_blocks.1.limit_ref, ...), custom_call_target="tpu_custom_call", output_to_operand_aliasing={{0}: (5, {}), {1}: (6, {})} | custom-call | flops 1048576 | bytes 100000 | tf_op jit(solution)/shard_map/score_part/pallas_call | solution.py:553
  98.2 4.5 %collective-permute-done.20 = bf16[16,32,1152]{2,1,0:T(8,128)(2,1)S(1)} collective-permute-done((bf16[16,32,1152]{2,1,0:T(8,128)(2,1)}, bf16[16,32,1152]{2,1,0:T(8,128)(2,1)S(1)}, u32[]{:S(2)}, u32[]{:S(2)}) %collective-permute-start.20) | collective-permute-done | bytes 1179680 | tf_op jit(solution)/shard_map/ppermute | solution.py:774
  102.6 0.0 collective-permute-start.21
  102.7 1.8 %reshape.48 = bf16[1,2,36864]{2,1,0:T(2,128)(2,1)} reshape(bf16[128,576]{1,0:T(8,128)(2,1)} %bitcast.23) | data formatting | bytes 294912 | tf_op jit(solution)/shard_map/reshape | solution.py:896
  104.4 1.2 collective-permute-done.21
  105.6 15.5 %conditional.1 = (bf16[1,128,1024]{2,1,0:T(8,128)(2,1)}) conditional(s32[]{:T(128)} %convert_element_type.20, (s32[1,224]{1,0:T(1,128)S(1)}, bf16[640,1024]{1,0:T(8,128)(2,1)S(1)}, f32[26,1024]{1,0:T(8,128)}, f32[1,1024]{1,0:T(1,128)S(1)}, f32[1,1024]{1,0:T(1,128)S(1)}, /*index=5*/f32[256,1024]{1,0:T(8,128)}, bf16[512,256]{1,0:T(8,128)(2,1)}, ...), branch_computations={%region_2.3_spmd, %region_3.4_spmd} | conditional | flops 8055422976 | bytes 63854904 | solution.py:895
  105.6 15.3 %finish.2 = bf16[128,1024]{1,0:T(8,128)(2,1)} custom-call(s32[1,224]{1,0:T(1,128)S(1)} %get-tuple-element.62.limit_ref, bf16[640,1024]{1,0:T(8,128)(2,1)S(1)} %get-tuple-element.63.queries_ref, f32[26,1024]{1,0:T(8,128)} %get-tuple-element.64.marks, f32[1,1024]{1,0:T(1,128)S(1)} %get-tuple-element.65.sum_in, f32[1,1024]{1,0:T(1,128)S(1)} %get-tuple-element.66.high_in, ...), custom_call_target="tpu_custom_call" | custom-call | flops 6442450944 | bytes 30000000 | tf_op jit(solution)/shard_map/cond/branch_0_fun/finish/pallas_call | solution.py:692
  (21 shorter events, 0.1 us)
Async XLA Ops:
  5.6 18.9 %collective-permute-start.7 = (bf16[8,32,1152]{2,1,0:T(8,128)(2,1)}, bf16[8,32,1152]{2,1,0:T(8,128)(2,1)S(1)}, u32[]{:S(2)}, u32[]{:S(2)}) collective-permute-start(bf16[8,32,1152]{2,1,0:T(8,128)(2,1)} %get-tuple-element.168.refs_0_), channel_id=1, source_target_pairs={{0,4},{5,1},{4,8},{9,5},{8,12},{13,9},{2,6},{7,3},{6,10},{11,7},{1... | collective-permute-start | bytes 1769480 | tf_op jit(solution)/shard_map/ppermute | solution.py:774
  9.2 15.4 %all-to-all-start = ((f32[4,32,576]{2,1,0:T(8,128)}), f32[4,32,576]{2,1,0:T(8,128)S(1)}, u32[]{:S(2)}, u32[]{:S(2)}) async-start(f32[4,32,576]{2,1,0:T(8,128)} %bitcast.26), calls=%async_computation | async-start | bytes 655360 | tf_op jit(solution)/shard_map/all_to_all | solution.py:789
  13.0 14.6 %collective-permute-start.6 = (bf16[8,32,1152]{2,1,0:T(8,128)(2,1)}, bf16[8,32,1152]{2,1,0:T(8,128)(2,1)S(1)}, u32[]{:S(2)}, u32[]{:S(2)}) collective-permute-start(bf16[8,32,1152]{2,1,0:T(8,128)(2,1)} %bitcast.31), channel_id=1, source_target_pairs={{0,2},{2,0},{1,3},{3,1},{4,6},{6,4},{5,7},{7,5},{8,10},{10,8},{9,1... | collective-permute-start | bytes 1769480 | tf_op jit(solution)/shard_map/ppermute | solution.py:784
  24.5 26.7 %copy-start.16 = (bf16[8,32,1152]{2,1,0:T(8,128)(2,1)}, bf16[8,32,1152]{2,1,0:T(8,128)(2,1)S(1)}, u32[]{:S(2)}) copy-start(bf16[8,32,1152]{2,1,0:T(8,128)(2,1)S(1)} %collective-permute-done.7.refs_1_) | copy-start | bytes 1769476
  27.6 9.5 %collective-permute-start.8 = (bf16[1,8,32,1152]{3,2,1,0:T(8,128)(2,1)S(1)}, bf16[1,8,32,1152]{3,2,1,0:T(8,128)(2,1)S(1)}, u32[]{:S(2)}, u32[]{:S(2)}) collective-permute-start(bf16[1,8,32,1152]{3,2,1,0:T(8,128)(2,1)S(1)} %bitcast.18), channel_id=1, source_target_pairs={{0,1},{1,0},{2,3},{3,2},{4,5},{5,4},{6,7},{7,6},{8,9},{9,8},{10,11... | collective-permute-start | bytes 1769480 | tf_op jit(solution)/shard_map/ppermute | solution.py:771
  27.6 16.5 %collective-permute-start.9 = (bf16[8,32,1152]{2,1,0:T(8,128)(2,1)S(1)}, bf16[8,32,1152]{2,1,0:T(8,128)(2,1)}, u32[]{:S(2)}, u32[]{:S(2)}) collective-permute-start(bf16[8,32,1152]{2,1,0:T(8,128)(2,1)S(1)} %collective-permute-done.7.refs_1_), channel_id=1, source_target_pairs={{0,4},{5,1},{4,8},{9,5},{8,12},{13,9},{2,6},{7,3},{6,10},{11,7},{1... | collective-permute-start | bytes 1769480 | tf_op jit(solution)/shard_map/ppermute | solution.py:774
  33.8 10.3 %all-to-all-start.1 = ((bf16[4,32,576]{2,1,0:T(8,128)(2,1)}), bf16[4,32,576]{2,1,0:T(8,128)(2,1)S(1)}, u32[]{:S(2)}, u32[]{:S(2)}) async-start(bf16[4,32,576]{2,1,0:T(8,128)(2,1)} %bitcast.15), calls=%async_computation.1 | async-start | bytes 327680 | tf_op jit(solution)/shard_map/all_to_all | solution.py:798
  37.1 1.1 copy-start.1
  38.2 0.7 copy-start.2
  43.3 29.2 %copy-start = (bf16[16,32,1152]{2,1,0:T(8,128)(2,1)}, bf16[16,32,1152]{2,1,0:T(8,128)(2,1)S(1)}, u32[]{:S(2)}) copy-start(bf16[16,32,1152]{2,1,0:T(8,128)(2,1)S(1)} %get-tuple-element.175.refs_7_) | copy-start | bytes 3538948
  44.1 46.0 %copy-start.6 = (bf16[4,32,576]{2,1,0:T(8,128)(2,1)}, bf16[4,32,576]{2,1,0:T(8,128)(2,1)S(1)}, u32[]{:S(2)}) copy-start(bf16[4,32,576]{2,1,0:T(8,128)(2,1)S(1)} %all-to-all-done.1) | copy-start | bytes 442372
  44.1 17.4 %collective-permute-start.10 = (bf16[16,32,1152]{2,1,0:T(8,128)(2,1)S(1)}, bf16[16,32,1152]{2,1,0:T(8,128)(2,1)S(1)}, u32[]{:S(2)}, u32[]{:S(2)}) collective-permute-start(bf16[16,32,1152]{2,1,0:T(8,128)(2,1)S(1)} %get-tuple-element.175.refs_7_), channel_id=1, source_target_pairs={{0,4},{5,1},{4,8},{9,5},{8,12},{13,9},{2,6},{7,3},{6,10},{11,7},{1... | collective-permute-start | bytes 3538952 | tf_op jit(solution)/shard_map/ppermute | solution.py:774
  47.3 3.9 %collective-permute-start.11 = (bf16[8,32,1152]{2,1,0:T(8,128)(2,1)S(1)}, bf16[8,32,1152]{2,1,0:T(8,128)(2,1)S(1)}, u32[]{:S(2)}, u32[]{:S(2)}) collective-permute-start(bf16[8,32,1152]{2,1,0:T(8,128)(2,1)S(1)} %collective-permute-done.7.refs_1_), channel_id=1, source_target_pairs={{0,1},{1,0},{2,3},{3,2},{4,5},{5,4},{6,7},{7,6},{8,9},{9,8},{10,11... | collective-permute-start | bytes 1769480 | tf_op jit(solution)/shard_map/ppermute | solution.py:771
  47.3 3.8 %collective-permute-start.12 = (bf16[8,32,1152]{2,1,0:T(8,128)(2,1)}, bf16[8,32,1152]{2,1,0:T(8,128)(2,1)S(1)}, u32[]{:S(2)}, u32[]{:S(2)}) collective-permute-start(bf16[8,32,1152]{2,1,0:T(8,128)(2,1)} %collective-permute-done.9.refs_3_), channel_id=1, source_target_pairs={{0,1},{1,0},{2,3},{3,2},{4,5},{5,4},{6,7},{7,6},{8,9},{9,8},{10,11... | collective-permute-start | bytes 1769480 | tf_op jit(solution)/shard_map/ppermute | solution.py:771
  47.8 19.5 %collective-permute-start.14 = (bf16[8,32,1152]{2,1,0:T(8,128)(2,1)}, bf16[8,32,1152]{2,1,0:T(8,128)(2,1)S(1)}, u32[]{:S(2)}, u32[]{:S(2)}) collective-permute-start(bf16[8,32,1152]{2,1,0:T(8,128)(2,1)} %collective-permute-done.9.refs_3_), channel_id=1, source_target_pairs={{0,4},{5,1},{4,8},{9,5},{8,12},{13,9},{2,6},{7,3},{6,10},{11,7},{1... | collective-permute-start | bytes 1769480 | tf_op jit(solution)/shard_map/ppermute | solution.py:774
  51.2 0.8 copy-start.17
  52.0 0.8 copy-start.18
  61.5 10.9 %copy-start.7 = (bf16[16,32,1152]{2,1,0:T(8,128)(2,1)}, bf16[16,32,1152]{2,1,0:T(8,128)(2,1)S(1)}, u32[]{:S(2)}) copy-start(bf16[16,32,1152]{2,1,0:T(8,128)(2,1)S(1)} %collective-permute-done.10.refs_8_) | copy-start | bytes 3538948
  61.5 10.9 %collective-permute-start.16 = (bf16[16,32,1152]{2,1,0:T(8,128)(2,1)S(1)}, bf16[16,32,1152]{2,1,0:T(8,128)(2,1)S(1)}, u32[]{:S(2)}, u32[]{:S(2)}) collective-permute-start(bf16[16,32,1152]{2,1,0:T(8,128)(2,1)S(1)} %collective-permute-done.10.refs_8_), channel_id=1, source_target_pairs={{0,1},{1,0},{2,3},{3,2},{4,5},{5,4},{6,7},{7,6},{8,9},{9,8},{10,11... | collective-permute-start | bytes 3538952 | tf_op jit(solution)/shard_map/ppermute | solution.py:771
  61.6 22.5 %collective-permute-start.13 = (bf16[16,32,1152]{2,1,0:T(8,128)(2,1)S(1)}, bf16[16,32,1152]{2,1,0:T(8,128)(2,1)}, u32[]{:S(2)}, u32[]{:S(2)}) collective-permute-start(bf16[16,32,1152]{2,1,0:T(8,128)(2,1)S(1)} %collective-permute-done.10.refs_8_), channel_id=1, source_target_pairs={{0,4},{5,1},{4,8},{9,5},{8,12},{13,9},{2,6},{7,3},{6,10},{11,7},{1... | collective-permute-start | bytes 3538952 | tf_op jit(solution)/shard_map/ppermute | solution.py:774
  67.3 5.1 %copy-start.19 = (bf16[8,32,1152]{2,1,0:T(8,128)(2,1)}, bf16[8,32,1152]{2,1,0:T(8,128)(2,1)S(1)}, u32[]{:S(2)}) copy-start(bf16[8,32,1152]{2,1,0:T(8,128)(2,1)S(1)} %collective-permute-done.14.refs_5_) | copy-start | bytes 1769476
  67.3 5.1 %collective-permute-start.15 = (bf16[8,32,1152]{2,1,0:T(8,128)(2,1)S(1)}, bf16[8,32,1152]{2,1,0:T(8,128)(2,1)S(1)}, u32[]{:S(2)}, u32[]{:S(2)}) collective-permute-start(bf16[8,32,1152]{2,1,0:T(8,128)(2,1)S(1)} %collective-permute-done.14.refs_5_), channel_id=1, source_target_pairs={{0,1},{1,0},{2,3},{3,2},{4,5},{5,4},{6,7},{7,6},{8,9},{9,8},{10,11... | collective-permute-start | bytes 1769480 | tf_op jit(solution)/shard_map/ppermute | solution.py:771
  67.3 3.8 %collective-permute-start.17 = (s32[1]{0:T(128)}, s32[1]{0:T(128)}, u32[]{:S(2)}, u32[]{:S(2)}) collective-permute-start(s32[1]{0:T(128)} %get-tuple-element.192), channel_id=1, source_target_pairs={{0,16},{16,0},{1,17},{17,1},{2,18},{18,2},{3,19},{19,3},{4,20},{20... | collective-permute-start | bytes 20 | tf_op jit(solution)/shard_map/ppermute | solution.py:304
  72.4 0.8 copy-start.20
  72.4 1.2 %copy-start.8 = (bf16[16,32,1152]{2,1,0:T(8,128)(2,1)}, bf16[16,32,1152]{2,1,0:T(8,128)(2,1)S(1)}, u32[]{:S(2)}) copy-start(bf16[16,32,1152]{2,1,0:T(8,128)(2,1)S(1)} %collective-permute-done.16.refs_9_) | copy-start | bytes 3538948
  73.7 17.3 %copy-start.3 = (bf16[640,1024]{1,0:T(8,128)(2,1)S(1)}, bf16[640,1024]{1,0:T(8,128)(2,1)}, u32[]{:S(2)}) copy-start(bf16[640,1024]{1,0:T(8,128)(2,1)} %turn_queries.1.queries_ref) | copy-start | bytes 3932164
  84.2 6.8 %collective-permute-start.19 = (bf16[16,32,1152]{2,1,0:T(8,128)(2,1)}, bf16[16,32,1152]{2,1,0:T(8,128)(2,1)}, u32[]{:S(2)}, u32[]{:S(2)}) collective-permute-start(bf16[16,32,1152]{2,1,0:T(8,128)(2,1)} %collective-permute-done.13.refs_7_), channel_id=1, source_target_pairs={{0,1},{1,0},{2,3},{3,2},{4,5},{5,4},{6,7},{7,6},{8,9},{9,8},{10,11... | collective-permute-start | bytes 3538952 | tf_op jit(solution)/shard_map/ppermute | solution.py:771
  84.2 18.4 %collective-permute-start.20 = (bf16[16,32,1152]{2,1,0:T(8,128)(2,1)}, bf16[16,32,1152]{2,1,0:T(8,128)(2,1)S(1)}, u32[]{:S(2)}, u32[]{:S(2)}) collective-permute-start(bf16[16,32,1152]{2,1,0:T(8,128)(2,1)} %collective-permute-done.13.refs_7_), channel_id=1, source_target_pairs={{0,4},{5,1},{4,8},{9,5},{8,12},{13,9},{2,6},{7,3},{6,10},{11,7},{1... | collective-permute-start | bytes 3538952 | tf_op jit(solution)/shard_map/ppermute | solution.py:774
  88.7 1.5 %collective-permute-start.18 = (bf16[128,576]{1,0:T(8,128)(2,1)S(1)}, bf16[128,576]{1,0:T(8,128)(2,1)S(1)}, u32[]{:S(2)}, u32[]{:S(2)}) collective-permute-start(bf16[128,576]{1,0:T(8,128)(2,1)S(1)} %bitcast.21), channel_id=1, source_target_pairs={{0,1},{1,0},{2,3},{3,2},{4,5},{5,4},{6,7},{7,6},{8,9},{9,8},{10,11... | collective-permute-start | bytes 442376 | tf_op jit(solution)/shard_map/ppermute | solution.py:771
  91.0 14.7 %copy-start.4 = (bf16[8,512,128]{2,1,0:T(8,128)(2,1)S(1)}, bf16[8,512,128]{2,1,0:T(8,128)(2,1)}, u32[]{:S(2)}) copy-start(bf16[8,512,128]{2,1,0:T(8,128)(2,1)} %param.18) | copy-start | bytes 3145732
  102.6 3.0 %collective-permute-start.21 = (bf16[16,32,1152]{2,1,0:T(8,128)(2,1)S(1)}, bf16[16,32,1152]{2,1,0:T(8,128)(2,1)}, u32[]{:S(2)}, u32[]{:S(2)}) collective-permute-start(bf16[16,32,1152]{2,1,0:T(8,128)(2,1)S(1)} %collective-permute-done.20), channel_id=1, source_target_pairs={{0,1},{1,0},{2,3},{3,2},{4,5},{5,4},{6,7},{7,6},{8,9},{9,8},{10,11... | collective-permute-start | bytes 3538952 | tf_op jit(solution)/shard_map/ppermute | solution.py:771
